TPU v7x, 128 devices: a whole 4x4x4 slice. The times are simulated.
128 devices in a mesh: fsdp: 8 (over z, core), dp: 16 (over x, y).
Axes of the slice: x: 4, y: 4, z: 4, core: 2. Of those that a mesh axis runs over, the one named last changes fastest.
Arguments:
- gradient: float32 [8192, 8192], P(('fsdp', 'dp')), may hold values from -6 to 6
- moment: float32 [8192, 8192], P(('fsdp', 'dp')), may hold values from -6 to 6
- second: float32 [8192, 8192], P(('fsdp', 'dp')), may hold values from 0.01 to 0.1
- statistics: float32 [128, 1024, 1024], P(('fsdp', 'dp')), as said below
- inv_roots: float32 [128, 1024, 1024], P(('fsdp', 'dp')), as said below
- owner_table: int32 [8, 8], P('fsdp'), may hold values from 0 to 7, each once within a row
Outputs:
- update: float32 [8192, 8192], P(('fsdp', 'dp'))
- new_moment: float32 [8192, 8192], P(('fsdp', 'dp'))
- new_second: float32 [8192, 8192], P(('fsdp', 'dp'))
- new_statistics: float32 [128, 1024, 1024], P(('fsdp', 'dp'))
Inputs may be any that keep to these rules, and one draw needn't show every extreme that they name: Each row of owner_table is a permutation of the 8 column blocks. `statistics`: every slot's matrix is symmetric. `inv_roots`: every slot's matrix is symmetric.
All inputs are finite; a program needn't handle non-finite values.
Results may differ from a plain program's by a relative error of at most 0.000075.
Values sent between devices are 32-bit elements; how exact they have to be, the bound alone decides.
No kernel may reach another device: no remote copies, remote signals or barrier semaphores. Data moves between devices by JAX's collectives and lax.ppermute only.
A program may use at most 128 MiB of HBM per device.

v0:
```python
import math

import jax
import jax.numpy as jnp
from jax import lax
from jax.sharding import PartitionSpec as P

BETA_STAT = 0.95
BETA_ONE = 0.9
BETA_TWO = 0.999
BIAS_ONE = 1.0 - 0.9**10
BIAS_TWO = 1.0 - 0.999**10
ADAM_EPS = 1e-08
CLIP_RMS = 0.25
PRECISE = lax.Precision.HIGHEST


def partner(block, axis, apart):
    count = lax.axis_size(axis)
    route = []
    for low in range(count):
        high = low | 1 << apart
        if high != low and high < count:
            route += [(low, high), (high, low)]
    return lax.ppermute(block, axis, route)


def matmul(left_mat, right_mat):
    return jnp.dot(left_mat, right_mat, precision=PRECISE, preferred_element_type=jnp.float32)


def contract(left_mat, right_mat, left_dim, right_dim):
    return lax.dot_general(
        left_mat,
        right_mat,
        (((left_dim,), (right_dim,)), ((), ())),
        precision=PRECISE,
        preferred_element_type=jnp.float32,
    )


def local(gradient, moment, second, statistics, inv_roots, owner_table):
    rows_dev = gradient.shape[0]
    width_cols = gradient.shape[1]
    slot_count = statistics.shape[0]
    block_order = statistics.shape[1]
    col_blocks = width_cols // block_order
    dp_count = lax.axis_size("dp")
    half_rows = rows_dev // 2
    side_bit = lax.axis_index("dp") % 2
    owner_row = owner_table[0]
    positions = jnp.arange(col_blocks, dtype=jnp.int32)
    column_of = jnp.sum(
        jnp.where(owner_row[None, :] == positions[:, None], positions[None, :], 0), axis=1
    )
    dest_pos = (jnp.arange(dp_count, dtype=jnp.int32) // 2)[:, None] * slot_count + jnp.arange(
        slot_count, dtype=jnp.int32
    )[None, :]
    send_cols = column_of[dest_pos.reshape(-1)]
    outgoing = jnp.take(
        gradient.reshape(rows_dev, col_blocks, block_order), send_cols, axis=1
    ).reshape(rows_dev, dp_count, slot_count, block_order)
    arrived = lax.all_to_all(outgoing, "dp", split_axis=1, concat_axis=0, tiled=True).reshape(
        block_order, slot_count, block_order
    )
    new_moment = BETA_ONE * moment + (1.0 - BETA_ONE) * gradient
    new_second = BETA_TWO * second + (1.0 - BETA_TWO) * gradient * gradient
    adam_step = new_moment / BIAS_ONE / (jnp.sqrt(new_second / BIAS_TWO) + ADAM_EPS)
    squares_part = jnp.sum(
        (adam_step * adam_step).reshape(rows_dev, col_blocks, block_order), axis=(0, 2)
    )
    block_squares = lax.psum(squares_part, "dp")
    total = lax.psum(jnp.sum(block_squares), "fsdp")
    slot_index = 0
    block_grad = arrived[:, slot_index, :]
    gram = lax.cond(
        side_bit == 0,
        lambda: contract(block_grad, block_grad, 1, 1),
        lambda: contract(block_grad, block_grad, 0, 0),
    )
    new_stats = [BETA_STAT * statistics[slot_index] + (1.0 - BETA_STAT) * gram]
    slot_index = 0
    block_grad = arrived[:, slot_index, :]
    own_root = inv_roots[slot_index]
    products = [
        lax.cond(
            side_bit == 0,
            lambda: matmul(own_root, block_grad),
            lambda: matmul(block_grad, own_root),
        )
    ]
    partner_parts = partner(jnp.stack(products), "dp", 0)
    slot_index = 0
    own_root = inv_roots[slot_index]
    other_part = partner_parts[slot_index]
    left_mat = jnp.where(side_bit == 0, own_root, other_part)
    right_mat = jnp.where(side_bit == 0, other_part, own_root)
    shaped = left_mat.reshape(dp_count, 2, half_rows, block_order)
    halves = [
        matmul(
            lax.dynamic_index_in_dim(shaped, side_bit, 1, keepdims=False).reshape(
                dp_count * half_rows, block_order
            ),
            right_mat,
        )
    ]
    half_blocks = jnp.stack(halves).reshape(slot_count, dp_count, half_rows, block_order)
    half_squares = jnp.sum(half_blocks * half_blocks, axis=(1, 2, 3))
    norm_rows = jnp.broadcast_to(half_squares[:, None], (slot_count, dp_count))
    returned, returned_norms = (
        lax.all_to_all(half_blocks, "dp", split_axis=1, concat_axis=0, tiled=True),
        lax.all_to_all(norm_rows, "dp", split_axis=1, concat_axis=0, tiled=True),
    )
    left_idx = 2 * (owner_row // slot_count) * slot_count + owner_row % slot_count
    right_idx = left_idx + slot_count
    pieces = jnp.concatenate([returned[left_idx, 0], returned[right_idx, 0]], axis=1)
    prec_sq = returned_norms[left_idx, 0] + returned_norms[right_idx, 0]
    ratio = jnp.sqrt(block_squares / (prec_sq + 1e-06))
    count_all = block_order * lax.axis_size("fsdp") * width_cols
    clip = jnp.minimum(1.0, CLIP_RMS * math.sqrt(count_all) / jnp.sqrt(total + 1e-06))
    update = (
        (pieces * (ratio * clip)[:, None, None]).transpose(1, 0, 2).reshape(rows_dev, width_cols)
    )
    return (update, new_moment, new_second, jnp.stack(new_stats))


def solution(mesh):
    placed = (
        P(("fsdp", "dp"), None),
        P(("fsdp", "dp"), None),
        P(("fsdp", "dp"), None),
        P(("fsdp", "dp"), None, None),
        P(("fsdp", "dp"), None, None),
        P("fsdp", None),
    )
    return jax.shard_map(
        local,
        mesh=mesh,
        in_specs=placed,
        out_specs=(
            P(("fsdp", "dp"), None),
            P(("fsdp", "dp"), None),
            P(("fsdp", "dp"), None),
            P(("fsdp", "dp"), None, None),
        ),
        check_vma=False,
    )
```

profile of v0, /device:TPU:6, one launch (start us, length us, event | category | flops | bytes accessed | tf_op | source)
XLA Modules:
  0.0 326.0 jit_solution(4659202218241745104)
XLA Ops:
  0.6 0.8 select_reduce_fusion
  2.1 1.7 copy.28
  3.9 2.8 gather_fusion.1
  6.7 5.1 %fusion = f32[64,16,1,1024]{3,0,2,1:T(8,128)} fusion(f32[16,64,1024]{2,1,0:T(8,128)} %gather_fusion.1, pred[16]{0:T(512)(128)(4,1)S(1)} %compare_and_fusion), kind=kLoop, calls=%fused_computation.7 | loop fusion | flops 1048576 | bytes 8388624 | tf_op jit(solution)/shard_map/jit(_take)/select_n | solution.py:60
  11.8 7.4 %all-to-all-start = ((f32[64,16,1,1024]{3,0,2,1:T(8,128)}), f32[64,16,1,1024]{3,0,2,1:T(8,128)}, u32[]{:S(2)}, u32[]{:S(2)}) async-start(f32[64,16,1,1024]{3,0,2,1:T(8,128)} %fusion), calls=%async_computation | async-start | bytes 8388608 | tf_op jit(solution)/shard_map/all_to_all | solution.py:63
  19.2 64.5 %all-to-all-done = f32[64,16,1,1024]{3,0,2,1:T(8,128)} async-done(((f32[64,16,1,1024]{3,0,2,1:T(8,128)}), f32[64,16,1,1024]{3,0,2,1:T(8,128)}, u32[]{:S(2)}, u32[]{:S(2)}) %all-to-all-start) | async-done | bytes 4194336 | tf_op jit(solution)/shard_map/all_to_all | solution.py:63
  83.8 17.5 %conditional.2 = (f32[1024,1024]{1,0:T(8,128)}) conditional(s32[]{:T(128)} %convert_element_type.4, (f32[1024,1024]{1,0:T(8,128)}, f32[1024,1024]{1,0:T(8,128)}) %tuple.31, (f32[1024,1024]{1,0:T(8,128)}, f32[1024,1024]{1,0:T(8,128)}) %tuple.32), branch_computations={%region_1.2_spmd, %region_2.3_spmd} | conditional | flops 12884901888 | bytes 12582920 | solution.py:86
  83.8 17.5 %fusion.18 = f32[1024,1024]{1,0:T(8,128)} fusion(f32[1024,1024]{1,0:T(8,128)} %get-tuple-element.18, f32[1024,1024]{1,0:T(8,128)} %get-tuple-element.19), kind=kOutput, calls=%fused_computation.51 | convolution fusion | flops 12884901888 | bytes 12582912 | tf_op jit(solution)/shard_map/cond/branch_1_fun/dot_general | solution.py:29
  101.3 89.8 %collective-permute-done = f32[1,1024,1024]{2,1,0:T(8,128)} collective-permute-done((f32[1,1024,1024]{2,1,0:T(8,128)}, f32[1,1024,1024]{2,1,0:T(8,128)}, u32[]{:S(2)}, u32[]{:S(2)}) %collective-permute-start) | collective-permute-done | bytes 4194336 | tf_op jit(solution)/shard_map/ppermute | solution.py:25
  191.1 3.1 broadcast_select_fusion
  194.4 2.0 copy-done
  196.4 10.4 %multiply_reduce_fusion = (f32[]{:T(128)}, f32[512,1024]{1,0:T(8,128)}) fusion(f32[512,1024]{1,0:T(8,128)S(1)} %bitcast.81, f32[1,1024,1024]{2,1,0:T(8,128)} %collective-permute-done, f32[1,1024,1024]{2,1,0:T(8,128)S(1)} %copy-done, pred[]{:T(512)S(6)} %eq.13), kind=kOutput, calls=%fused_computation.18 | convolution fusion | flops 6444548096 | bytes 12582917 | tf_op jit(solution)/shard_map/dot_general | solution.py:29
  206.8 0.8 broadcast_in_dim.40
  207.6 14.6 %all_to_all.40 = f32[1,16,1]{2,0,1:T(1,128)S(1)} all-to-all(f32[1,16,1]{2,0,1:T(1,128)S(1)} %broadcast_in_dim.40), channel_id=1, replica_groups=mesh['fsdp'=8,'dp'=16] {'dp'}, dimensions={1} | all-to-all | bytes 128 | tf_op jit(solution)/shard_map/all_to_all | solution.py:112
  222.2 6.3 %all-to-all-start.1 = ((f32[1,16,32,1024]{3,2,0,1:T(8,128)}), f32[1,16,32,1024]{3,2,0,1:T(8,128)}, u32[]{:S(2)}, u32[]{:S(2)}) async-start(f32[1,16,32,1024]{3,2,0,1:T(8,128)} %bitcast.80), calls=%async_computation.1 | async-start | bytes 4194304 | tf_op jit(solution)/shard_map/all_to_all | solution.py:111
  228.6 5.7 %multiply_reduce_fusion.1 = (f32[8192]{0:T(1024)S(1)}, f32[64,8192]{1,0:T(8,128)}, f32[64,8192]{1,0:T(8,128)}) fusion(f32[64,8192]{1,0:T(8,128)S(1)} %copy-done.1, f32[64,8192]{1,0:T(8,128)} %param.11, f32[64,8192]{1,0:T(8,128)} %param.12), kind=kLoop, calls=%fused_computation.19 | loop fusion | flops 6807552 | bytes 10518528 | tf_op jit(solution)/shard_map/reduce_sum | solution.py:69
  234.4 43.5 %psum.14 = f32[8]{0:T(128)S(1)} all-reduce(f32[8]{0:T(128)S(1)} %reduce_sum.46), channel_id=1, replica_groups=mesh['fsdp'=8,'dp'=16] {'dp'}, use_global_device_ids=true, to_apply=%region_5.6 | all-reduce | flops 8 | bytes 64 | tf_op jit(solution)/shard_map/psum | solution.py:72
  278.6 13.8 %psum.15 = f32[]{:T(128)} all-reduce(f32[]{:T(128)} %reduce_sum.48), channel_id=1, replica_groups=mesh['fsdp'=8,'dp'=16] {'fsdp'}, use_global_device_ids=true, to_apply=%region_8.9 | all-reduce | flops 1 | bytes 8 | tf_op jit(solution)/shard_map/psum | solution.py:73
  293.1 18.3 %conditional.3 = (f32[1024,1024]{1,0:T(8,128)}) conditional(s32[]{:T(128)} %convert_element_type.4, f32[1024,1024]{1,0:T(8,128)} %bitcast.9, f32[1024,1024]{1,0:T(8,128)} %bitcast.9), branch_computations={%region_9.10_spmd, %region_10.11_spmd} | conditional | flops 12884901888 | bytes 8388616 | solution.py:76
  293.3 18.1 %fusion.20 = f32[1024,1024]{1,0:T(8,128)} fusion(f32[1024,1024]{1,0:T(8,128)} %param.3), kind=kOutput, calls=%fused_computation.53 | convolution fusion | flops 12884901888 | bytes 8388608 | tf_op jit(solution)/shard_map/cond/branch_1_fun/dot_general | solution.py:33
  311.4 7.0 %fusion.1 = f32[1,1024,1024]{2,1,0:T(8,128)} fusion(f32[1024,1024]{1,0:T(8,128)} %get-tuple-element.32, f32[1,1024,1024]{2,1,0:T(8,128)} %param.13), kind=kLoop, calls=%fused_computation.9 | loop fusion | flops 3145728 | bytes 12582912 | tf_op jit(solution)/shard_map/stack | solution.py:124
  319.9 2.2 gather_fusion.3
  322.1 2.2 gather_fusion.2
  324.6 1.5 copy.26
  (23 shorter events, 3.4 us)
Async XLA Ops:
  11.8 72.0 %all-to-all-start = ((f32[64,16,1,1024]{3,0,2,1:T(8,128)}), f32[64,16,1,1024]{3,0,2,1:T(8,128)}, u32[]{:S(2)}, u32[]{:S(2)}) async-start(f32[64,16,1,1024]{3,0,2,1:T(8,128)} %fusion), calls=%async_computation | async-start | bytes 8388608 | tf_op jit(solution)/shard_map/all_to_all | solution.py:63
  101.3 89.8 %collective-permute-start = (f32[1,1024,1024]{2,1,0:T(8,128)}, f32[1,1024,1024]{2,1,0:T(8,128)}, u32[]{:S(2)}, u32[]{:S(2)}) collective-permute-start(f32[1,1024,1024]{2,1,0:T(8,128)} %bitcast.83), channel_id=1, source_target_pairs={{0,1},{1,0},{2,3},{3,2},{4,5},{5,4},{6,7},{7,6},{8,9},{9,8},{10,11... | collective-permute-start | bytes 12582920 | tf_op jit(solution)/shard_map/ppermute | solution.py:25
  194.2 2.2 copy-start
  206.8 21.8 %copy-start.1 = (f32[64,8192]{1,0:T(8,128)S(1)}, f32[64,8192]{1,0:T(8,128)}, u32[]{:S(2)}) copy-start(f32[64,8192]{1,0:T(8,128)} %param.10) | copy-start | bytes 6291460
  222.2 97.6 %all-to-all-start.1 = ((f32[1,16,32,1024]{3,2,0,1:T(8,128)}), f32[1,16,32,1024]{3,2,0,1:T(8,128)}, u32[]{:S(2)}, u32[]{:S(2)}) async-start(f32[1,16,32,1024]{3,2,0,1:T(8,128)} %bitcast.80), calls=%async_computation.1 | async-start | bytes 4194304 | tf_op jit(solution)/shard_map/all_to_all | solution.py:111
  228.6 64.5 %copy-start.2 = (s32[1,8]{1,0:T(1,128)S(1)}, s32[1,8]{1,0:T(1,128)}, u32[]{:S(2)}) copy-start(s32[1,8]{1,0:T(1,128)} %param.15) | copy-start | bytes 100
where the time goes:
time: 331 us; the launch traced here: 326 us
  waiting for transfers between devices  154 us (47%)
  blocking collectives  72 us (22%)
  matrix products  46 us (14%)
  other arithmetic  23 us (7%)
  local copies, waits for them, and re-layouts  15.4 us (5%)
  starting transfers between devices  13.7 us (4%)
    ppermute x1, waiting for transfers between devices, partner(): return lax.ppermute(block, axis, route)  89.8 us
    all_to_all x1, waiting for transfers between devices, local(): lax.all_to_all(outgoing, 'dp', split_axis=1, concat_axis=0, tiled=True)  64.5 us
    psum x1, blocking collectives, local(): block_squares = lax.psum(squares_part, 'dp')  43.5 us
    dot_general x2, matrix products, matmul(): jnp.dot(left_mat, right_mat, precision=PRECISE, preferred_element_type=jn...  27.9 us
    dot_general x1, matrix products, contract(): lax.dot_general(left_mat, right_mat, (((left_dim,), (right_dim,)), ((), (...  18.1 us
    all_to_all x1, blocking collectives, local(): lax.all_to_all(norm_rows, 'dp', split_axis=1, concat_axis=0, tiled=True)  14.6 us
    psum x1, blocking collectives, local(): total = lax.psum(jnp.sum(block_squares), 'fsdp')  13.8 us
    all_to_all x1, starting transfers between devices, local(): lax.all_to_all(outgoing, 'dp', split_axis=1, concat_axis=0, tiled=True)  7.43 us
  transfers between devices with their start and end apart: 3, of which 2 were waited for; matrix products, arithmetic and copies ran while one was open for 10% of the time, Pallas kernels for 0%

commit v1 on v0

v1 whole, which is shorter than its diff:
```python
import math

import jax
import jax.numpy as jnp
from jax import lax
from jax.experimental import pallas as pl
from jax.experimental.pallas import tpu as pltpu
from jax.sharding import PartitionSpec as P

BETA_STAT = 0.95
BETA_ONE = 0.9
BETA_TWO = 0.999
BIAS_ONE = 1.0 - 0.9**10
BIAS_TWO = 1.0 - 0.999**10
ADAM_EPS = 1e-08
CLIP_RMS = 0.25
SPLIT = lax.Precision.HIGH
SIDE = 4


def route(move):
    pairs = []
    for src in range(SIDE * SIDE):
        x, y = move(src // SIDE, src % SIDE)
        pairs.append((src, (x % SIDE) * SIDE + y % SIDE))
    return pairs


NEAR = route(lambda x, y: (x, y ^ 1))
FAR = route(lambda x, y: (x, 3 - y))
GROUPS = [
    [SIDE * x + y for x in range(SIDE) for y in (0, 3)],
    [SIDE * x + y for x in range(SIDE) for y in (1, 2)],
]


def near(v):
    return lax.ppermute(v, "dp", NEAR)


def far(v):
    return lax.ppermute(v, "dp", FAR)


def along_x(v, shift):
    return lax.ppermute(v, "dp", route(lambda x, y: (x + shift, y)))


def swap(v, axis, bit):
    count = lax.axis_size(axis)
    return lax.ppermute(v, axis, [(i, i ^ bit) for i in range(count)])


def dot(a, b, a_dim=1, b_dim=0):
    return lax.dot_general(
        a, b, (((a_dim,), (b_dim,)), ((), ())), precision=SPLIT, preferred_element_type=jnp.float32
    )


def take_columns(gradient, cols, order):
    rows, count = gradient.shape[0], cols.shape[0]

    def body(cols_ref, g_ref, out_ref):
        out_ref[0] = g_ref[...]

    return pl.pallas_call(
        body,
        grid_spec=pltpu.PrefetchScalarGridSpec(
            num_scalar_prefetch=1,
            grid=(count,),
            in_specs=[pl.BlockSpec((rows, order), lambda k, cols_ref: (0, cols_ref[k]))],
            out_specs=pl.BlockSpec((1, rows, order), lambda k, cols_ref: (k, 0, 0)),
        ),
        out_shape=jax.ShapeDtypeStruct((count, rows, order), jnp.float32),
        cost_estimate=pl.CostEstimate(
            flops=0, bytes_accessed=8 * count * rows * order, transcendentals=0
        ),
    )(cols, gradient)


def place_columns(pieces, source, scale):
    count, rows, order = pieces.shape

    def body(source_ref, scale_ref, p_ref, out_ref):
        out_ref[...] = p_ref[0] * scale_ref[pl.program_id(0)]

    return pl.pallas_call(
        body,
        grid_spec=pltpu.PrefetchScalarGridSpec(
            num_scalar_prefetch=2,
            grid=(count,),
            in_specs=[
                pl.BlockSpec((1, rows, order), lambda k, source_ref, scale_ref: (source_ref[k], 0, 0))
            ],
            out_specs=pl.BlockSpec((rows, order), lambda k, source_ref, scale_ref: (0, k)),
        ),
        out_shape=jax.ShapeDtypeStruct((rows, count * order), jnp.float32),
        cost_estimate=pl.CostEstimate(
            flops=count * rows * order, bytes_accessed=8 * count * rows * order, transcendentals=0
        ),
    )(source, scale, pieces)


def pack_symmetric(mat):
    half = mat.shape[0] // 2
    row = lax.broadcasted_iota(jnp.int32, (half, half), 0)
    col = lax.broadcasted_iota(jnp.int32, (half, half), 1)
    both = jnp.where(row <= col, mat[:half, :half], mat[half:, half:])
    diag = jnp.sum(jnp.where(row == col, mat[half:, half:], 0.0), axis=0)
    last = jnp.zeros((8, 2 * half), jnp.float32).at[0, :half].set(diag)
    return jnp.concatenate([jnp.concatenate([mat[:half, half:], both], axis=1), last], axis=0)


def unpack_symmetric(packed):
    half = packed.shape[1] // 2
    row = lax.broadcasted_iota(jnp.int32, (half, half), 0)
    col = lax.broadcasted_iota(jnp.int32, (half, half), 1)
    cross, both, diag = packed[:half, :half], packed[:half, half:], packed[half, :half]
    top = jnp.where(row <= col, both, both.T)
    low = jnp.where(row > col, both, jnp.where(row == col, diag[:, None], both.T))
    return jnp.concatenate(
        [jnp.concatenate([top, cross], axis=1), jnp.concatenate([cross.T, low], axis=1)], axis=0
    )


def local(gradient, moment, second, statistics, inv_roots, owner_table):
    rows_dev, width = gradient.shape
    order = statistics.shape[1]
    col_blocks = width // order
    half = order // 2
    place = lax.axis_index("dp")
    x, y = place // SIDE, place % SIDE
    is_left = y % 2 == 0
    high = y // 2
    outer = (y == 0) | (y == 3)

    owner_row = owner_table[0]
    positions = jnp.arange(col_blocks, dtype=jnp.int32)
    column_of = jnp.sum(
        jnp.where(owner_row[None, :] == positions[:, None], positions[None, :], 0), axis=1
    )

    root = inv_roots[0]
    root_rows = root.reshape(SIDE, SIDE, rows_dev, order)
    rows_outer = jnp.concatenate([root_rows[:, 0:1], root_rows[:, 3:4]], axis=1).reshape(half, order)
    rows_inner = root_rows[:, 1:3].reshape(half, order)
    sent_rows = jnp.pad(jnp.where(outer, rows_inner, rows_outer), ((0, 8), (0, 0)))
    got = near(jnp.where(is_left, sent_rows, pack_symmetric(root)))

    shift = jnp.arange(SIDE, dtype=jnp.int32)[:, None]
    other = jnp.arange(2, dtype=jnp.int32)[None, :]
    send_pos = 2 * ((x + shift) % SIDE) + (high ^ other)
    outgoing = take_columns(gradient, column_of[send_pos.reshape(-1)], order)
    outgoing = outgoing.reshape(SIDE, 2, rows_dev, order)
    arrived = [outgoing[0]] + [along_x(outgoing[d], d) for d in range(1, SIDE)]
    own_y = [v[0] for v in arrived]
    far_y = [far(v[1]) for v in arrived]
    near_own = [near(v) for v in own_y]
    near_far = [near(v) for v in far_y]
    block = jnp.zeros((SIDE, SIDE, rows_dev, order), jnp.float32)
    for pieces, from_y in ((own_y, y), (far_y, 3 - y), (near_own, y ^ 1), (near_far, 3 - (y ^ 1))):
        for d in range(SIDE):
            block = lax.dynamic_update_slice(
                block, pieces[d][None, None], ((x - d) % SIDE, from_y, 0, 0)
            )
    block = block.reshape(order, order)

    new_moment = BETA_ONE * moment + (1.0 - BETA_ONE) * gradient
    new_second = BETA_TWO * second + (1.0 - BETA_TWO) * gradient * gradient
    adam_step = new_moment / BIAS_ONE / (jnp.sqrt(new_second / BIAS_TWO) + ADAM_EPS)
    squares = jnp.sum((adam_step * adam_step).reshape(rows_dev, col_blocks, order), axis=(0, 2))
    for bit in (4, 8, 3, 1):
        squares = squares + swap(squares, "dp", bit)
    total = jnp.broadcast_to(jnp.sum(squares), squares.shape)
    for bit in (1, 2, 4):
        total = total + swap(total, "fsdp", bit)

    own_rows = jnp.where(outer, rows_outer, rows_inner)
    left_rows = jnp.where(is_left, own_rows, got[:half])
    right_mat = lax.cond(is_left, lambda: unpack_symmetric(got), lambda: root)
    shaped = dot(dot(left_rows, block), right_mat)
    sum_sq = jnp.sum(shaped * shaped)
    sums = lax.all_to_all(
        jnp.broadcast_to(sum_sq, (SIDE * SIDE, 8, 128)), "dp", 0, 0, tiled=True
    )[:, 0, 0]
    pieces = lax.all_to_all(
        shaped.reshape(2 * SIDE, rows_dev, order),
        "dp",
        0,
        0,
        axis_index_groups=GROUPS,
        tiled=True,
    )

    stat = statistics[0]
    new_stat = lax.cond(
        is_left,
        lambda: BETA_STAT * stat + (1.0 - BETA_STAT) * dot(block, block, 1, 1),
        lambda: BETA_STAT * stat + (1.0 - BETA_STAT) * dot(block, block, 0, 0),
    )

    prec_sq = jnp.sum(sums.reshape(col_blocks, 2), axis=1)[owner_row]
    ratio = jnp.sqrt(squares / (prec_sq + 1e-06))
    count_all = order * lax.axis_size("fsdp") * width
    clip = jnp.minimum(1.0, CLIP_RMS * math.sqrt(count_all) / jnp.sqrt(total + 1e-06))
    update = place_columns(pieces, owner_row, ratio * clip)
    return (update, new_moment, new_second, new_stat[None])


def solution(mesh):
    placed = (
        P(("fsdp", "dp"), None),
        P(("fsdp", "dp"), None),
        P(("fsdp", "dp"), None),
        P(("fsdp", "dp"), None, None),
        P(("fsdp", "dp"), None, None),
        P("fsdp", None),
    )
    return jax.shard_map(
        local,
        mesh=mesh,
        in_specs=placed,
        out_specs=(
            P(("fsdp", "dp"), None),
            P(("fsdp", "dp"), None),
            P(("fsdp", "dp"), None),
            P(("fsdp", "dp"), None, None),
        ),
        check_vma=False,
    )
```

time: 331 us -> 238 us (0.72); the launches traced: 326 us -> 237 us
  waiting for transfers between devices: 154 us -> 86.5 us
  blocking collectives: 72 us -> 11.2 us
  local copies, waits for them, and re-layouts: 15.4 us -> 37.5 us
  starting transfers between devices: 13.7 us -> 34.9 us
  matrix products: 46 us -> 28.3 us
  Pallas kernels: 0 us -> 12.7 us
    all_to_all x2 -> x1, waiting for transfers between devices: 64.5 us -> 0.01 us  [local(): lax.all_to_all(shaped.reshape(2 * SIDE, rows_dev, order), 'dp', 0, 0, axi...]
    psum x2 -> x0, blocking collectives: 57.3 us -> none  [the longest x1 43.5 us: local(): block_squares = lax.psum(squares_part, 'dp')]
    ppermute x1 -> x23, starting transfers between devices: 0.01 us -> 28.5 us  [the longest x9 10.9 us: near(): return lax.ppermute(v, 'dp', NEAR)]
    dot_general x3, matrix products: 46 us -> 28.3 us  [dot(): lax.dot_general(a, b, (((a_dim,), (b_dim,)), ((), ())), precision=SPLIT,...]
    dynamic_update_slice x0 -> x16, local copies, waits for them, and re-layouts: none -> 16.4 us  [local(): lax.dynamic_update_slice(block, pieces[d][None, None], ((x - d) % SIDE, f...]
    pallas_call x0 -> x2, Pallas kernels: none -> 12.7 us  [the longest x1 6.34 us: place_columns(): pl.pallas_call(body, grid_spec=pltpu.PrefetchScalarGridSpec(num_scalar_pr...]
    gather x6 -> x2, local copies, waits for them, and re-layouts: 9.19 us -> 1.8 us  [the longest x1 1.15 us: local(): outgoing = take_columns(gradient, column_of[send_pos.reshape(-1)], order)]
    all_to_all x2 -> x1, starting transfers between devices: 13.7 us -> 6.39 us  [local(): lax.all_to_all(shaped.reshape(2 * SIDE, rows_dev, order), 'dp', 0, 0, axi...]
  transfers between devices with their start and end apart: 3 -> 24, of which waited for: 2 -> 14; matrix products, arithmetic and copies ran while one was open for 10% -> 24% of each run, Pallas kernels for 0% -> 0%
where the time goes in v1:
time: 238 us; the launch traced here: 237 us
  waiting for transfers between devices  86.5 us (36%)
  local copies, waits for them, and re-layouts  37.5 us (16%)
  starting transfers between devices  34.9 us (15%)
  matrix products  28.3 us (12%)
  other arithmetic  24.7 us (10%)
  Pallas kernels  12.7 us (5%)
  blocking collectives  11.2 us (5%)
    ppermute x9, waiting for transfers between devices, near(): return lax.ppermute(v, 'dp', NEAR)  49.1 us
    ppermute x7, waiting for transfers between devices, swap(): return lax.ppermute(v, axis, [(i, i ^ bit) for i in range(count)])  32.3 us
    dot_general x3, matrix products, dot(): lax.dot_general(a, b, (((a_dim,), (b_dim,)), ((), ())), precision=SPLIT,...  28.3 us
    dynamic_update_slice x16, local copies, waits for them, and re-layouts, local(): lax.dynamic_update_slice(block, pieces[d][None, None], ((x - d) % SIDE, f...  16.4 us
    all_to_all x1, blocking collectives, local(): lax.all_to_all(jnp.broadcast_to(sum_sq, (SIDE * SIDE, 8, 128)), 'dp', 0,...  11.2 us
    ppermute x9, starting transfers between devices, near(): return lax.ppermute(v, 'dp', NEAR)  10.9 us
    ppermute x4, starting transfers between devices, far(): return lax.ppermute(v, 'dp', FAR)  7.46 us
    ppermute x7, starting transfers between devices, swap(): return lax.ppermute(v, axis, [(i, i ^ bit) for i in range(count)])  7.29 us
  transfers between devices with their start and end apart: 24, of which 14 were waited for; matrix products, arithmetic and copies ran while one was open for 24% of the time, Pallas kernels for 0%

profile of v1, /device:TPU:6, one launch (start us, length us, event | category | flops | bytes accessed | tf_op | source)
XLA Modules:
  0.0 236.6 jit_solution(6889439400206714056)
XLA Ops:
  2.8 6.3 %shard_map.93 = f32[8,64,1024]{2,1,0:T(8,128)} custom-call(s32[8]{0:T(128)} %gather_fusion, f32[64,8192]{1,0:T(8,128)} %g_ref.1), custom_call_target="tpu_custom_call" | custom-call | bytes 4194304 | tf_op jit(solution)/shard_map/pallas_call | solution.py:66
  16.6 3.0 %collective-permute-start.8 = (f32[64,1024]{1,0:T(8,128)}, f32[64,1024]{1,0:T(8,128)S(1)}, u32[]{:S(2)}, u32[]{:S(2)}) collective-permute-start(f32[64,1024]{1,0:T(8,128)} %get-tuple-element.57), channel_id=1, source_target_pairs={{0,3},{1,2},{2,1},{3,0},{4,7},{5,6},{6,5},{7,4},{8,11},{9,10},{10,... | collective-permute-start | bytes 786440 | tf_op jit(solution)/shard_map/ppermute | solution.py:42
  22.4 3.9 %slice_select_fusion.2 = (f32[4,2,64,1024]{3,2,1,0:T(8,128)S(1)}, f32[4,2,64,1024]{3,2,1,0:T(8,128)}) fusion(f32[4,4,64,1024]{3,2,1,0:T(8,128)} %bitcast.91, f32[4,1,64,1024]{3,2,1,0:T(8,128)} %get-tuple-element.55, f32[4,1,64,1024]{3,2,1,0:T(8,128)S(1)} %get-tuple-element.54, pred[]{:T(512)S(6)} %or.3), kind=kLoop, calls=%fused_computation.25 | loop fusion | flops 1572864 | bytes 8388609 | tf_op jit(solution)/shard_map/jit(_where)/select_n | solution.py:147
  31.7 2.9 %fusion.3 = f32[520,1024]{1,0:T(8,128)} fusion(f32[1,512]{1,0:T(1,128)S(1)} %bitcast.97, f32[512,512]{1,0:T(8,128)} %get-tuple-element.53, f32[512,512]{1,0:T(8,128)S(1)} %get-tuple-element.51, f32[512,1024]{1,0:T(8,128)S(1)} %bitcast.95, pred[]{:T(512)S(6)} %eq.49), kind=kLoop, calls=%fused_computation.16 | loop fusion | flops 2662400 | bytes 6326273 | tf_op jit(solution)/shard_map/jit(_where)/select_n | solution.py:148
  53.0 4.8 %collective-permute-done.11 = f32[64,1024]{1,0:T(8,128)S(1)} collective-permute-done((f32[64,1024]{1,0:T(8,128)S(1)}, f32[64,1024]{1,0:T(8,128)S(1)}, u32[]{:S(2)}, u32[]{:S(2)}) %collective-permute-start.11) | collective-permute-done | bytes 262176 | tf_op jit(solution)/shard_map/ppermute | solution.py:42
  62.2 33.2 %collective-permute-done.13 = f32[64,1024]{1,0:T(8,128)S(1)} collective-permute-done((f32[64,1024]{1,0:T(8,128)S(1)}, f32[64,1024]{1,0:T(8,128)S(1)}, u32[]{:S(2)}, u32[]{:S(2)}) %collective-permute-start.13) | collective-permute-done | bytes 262176 | tf_op jit(solution)/shard_map/ppermute | solution.py:38
  98.0 3.0 %collective-permute-done.14 = f32[64,1024]{1,0:T(8,128)S(1)} collective-permute-done((f32[64,1024]{1,0:T(8,128)S(1)}, f32[64,1024]{1,0:T(8,128)S(1)}, u32[]{:S(2)}, u32[]{:S(2)}) %collective-permute-start.14) | collective-permute-done | bytes 262176 | tf_op jit(solution)/shard_map/ppermute | solution.py:38
  103.6 3.0 %collective-permute-done.15 = f32[64,1024]{1,0:T(8,128)S(1)} collective-permute-done((f32[64,1024]{1,0:T(8,128)S(1)}, f32[64,1024]{1,0:T(8,128)S(1)}, u32[]{:S(2)}, u32[]{:S(2)}) %collective-permute-start.15) | collective-permute-done | bytes 262176 | tf_op jit(solution)/shard_map/ppermute | solution.py:38
  112.9 4.9 %collective-permute-done.18 = f32[64,1024]{1,0:T(8,128)S(1)} collective-permute-done((f32[64,1024]{1,0:T(8,128)S(1)}, f32[64,1024]{1,0:T(8,128)S(1)}, u32[]{:S(2)}, u32[]{:S(2)}) %collective-permute-start.18) | collective-permute-done | bytes 262176 | tf_op jit(solution)/shard_map/ppermute | solution.py:38
  122.0 7.0 %fusion.5 = f32[512,1024]{1,0:T(8,128)} fusion(f32[1024,1024]{1,0:T(8,128)} %bitcast.38, f32[512,1024]{1,0:T(8,128)S(1)} %bitcast.96, f32[520,1024]{1,0:T(8,128)S(1)} %collective-permute-done.4, pred[]{:T(512)S(6)} %eq.49), kind=kOutput, calls=%fused_computation.20 | convolution fusion | flops 3221749760 | bytes 10485761 | tf_op jit(solution)/shard_map/dot_general | solution.py:55
  129.0 11.9 %conditional.2 = (f32[1024,1024]{0,1:T(8,128)}) conditional(s32[]{:T(128)} %convert_element_type.6, (f32[1024,1024]{1,0:T(8,128)}) %tuple.49, f32[520,1024]{1,0:T(8,128)S(1)} %collective-permute-done.4), branch_computations={%region_4.5_spmd, %region_5.6_spmd} | conditional | flops 4718592 | bytes 22026248 | solution.py:180
  136.5 4.4 %maximum_maximum_fusion = f32[1024,1024]{0,1:T(8,128)} fusion(f32[512,512]{0,1:T(8,128)} %get-tuple-element.45, f32[512,512]{0,1:T(8,128)} %get-tuple-element.47, f32[512,512]{0,1:T(8,128)S(1)} %copy.36, f32[512,512]{0,1:T(8,128)} %get-tuple-element.44), kind=kLoop, calls=%fused_computation.2 | loop fusion | flops 3145728 | bytes 8388608 | tf_op jit(solution)/shard_map/cond/branch_1_fun/concatenate | solution.py:121
  140.9 8.3 %multiply_reduce_fusion = (f32[]{:T(128)}, f32[512,1024]{1,0:T(8,128)}) fusion(f32[512,1024]{1,0:T(8,128)} %fusion.5, f32[1024,1024]{0,1:T(8,128)} %get-tuple-element.69), kind=kOutput, calls=%fused_computation.22 | convolution fusion | flops 3222274048 | bytes 8388612 | tf_op jit(solution)/shard_map/dot_general | solution.py:55
  150.0 11.2 %all_to_all.10 = f32[16,8,128]{2,1,0:T(8,128)S(1)} all-to-all(f32[16,8,128]{2,1,0:T(8,128)S(1)} %broadcast_in_dim.101), channel_id=1, replica_groups=mesh['fsdp'=8,'dp'=16] {'dp'}, dimensions={0} | all-to-all | bytes 131072 | tf_op jit(solution)/shard_map/all_to_all | solution.py:183
  161.2 6.4 %all-to-all-start.1 = ((f32[8,64,1024]{2,1,0:T(8,128)}), f32[8,64,1024]{2,1,0:T(8,128)}, u32[]{:S(2)}, u32[]{:S(2)}) async-start(f32[8,64,1024]{2,1,0:T(8,128)} %bitcast.94), calls=%async_computation.1 | async-start | bytes 4194304 | tf_op jit(solution)/shard_map/all_to_all | solution.py:186
  167.6 5.7 %multiply_reduce_fusion.1 = (f32[8192]{0:T(1024)S(1)}, f32[64,8192]{1,0:T(8,128)}, f32[64,8192]{1,0:T(8,128)}) fusion(f32[64,8192]{1,0:T(8,128)S(1)} %copy-done.1, f32[64,8192]{1,0:T(8,128)} %param.13, f32[64,8192]{1,0:T(8,128)} %param.14), kind=kLoop, calls=%fused_computation.23 | loop fusion | flops 6807552 | bytes 10518528 | tf_op jit(solution)/shard_map/reduce_sum | solution.py:171
  174.4 16.6 %collective-permute-done = f32[8]{0:T(128)S(1)} collective-permute-done((f32[8]{0:T(128)S(1)}, f32[8]{0:T(128)S(1)}, u32[]{:S(2)}, u32[]{:S(2)}) %collective-permute-start) | collective-permute-done | bytes 64 | tf_op jit(solution)/shard_map/ppermute | solution.py:51
  191.0 5.0 %collective-permute-done.1 = f32[8]{0:T(128)S(1)} collective-permute-done((f32[8]{0:T(128)S(1)}, f32[8]{0:T(128)S(1)}, u32[]{:S(2)}, u32[]{:S(2)}) %collective-permute-start.1) | collective-permute-done | bytes 64 | tf_op jit(solution)/shard_map/ppermute | solution.py:51
  196.4 4.4 %collective-permute-done.2 = f32[8]{0:T(128)S(1)} collective-permute-done((f32[8]{0:T(128)S(1)}, f32[8]{0:T(128)S(1)}, u32[]{:S(2)}, u32[]{:S(2)}) %collective-permute-start.2) | collective-permute-done | bytes 64 | tf_op jit(solution)/shard_map/ppermute | solution.py:51
  200.8 3.5 %collective-permute-done.3 = f32[8]{0:T(128)S(1)} collective-permute-done((f32[8]{0:T(128)S(1)}, f32[8]{0:T(128)S(1)}, u32[]{:S(2)}, u32[]{:S(2)}) %collective-permute-start.3) | collective-permute-done | bytes 64 | tf_op jit(solution)/shard_map/ppermute | solution.py:51
  211.7 4.0 %collective-permute-start.22 = (f32[8]{0:T(128)S(1)}, f32[8]{0:T(128)S(1)}, u32[]{:S(2)}, u32[]{:S(2)}) collective-permute-start(f32[8]{0:T(128)S(1)} %fusion.23), channel_id=1, source_target_pairs={{0,64},{16,80},{32,96},{48,112},{64,0},{80,16},{96,32},{112,48},{1... | collective-permute-start | bytes 104 | tf_op jit(solution)/shard_map/ppermute | solution.py:51
  215.7 13.0 %conditional.3 = (f32[1,1024,1024]{2,1,0:T(8,128)}) conditional(s32[]{:T(128)} %convert_element_type.6, (f32[1,1024,1024]{2,1,0:T(8,128)}, f32[1024,1024]{1,0:T(8,128)}) %tuple.26, (f32[1,1024,1024]{2,1,0:T(8,128)}, f32[1024,1024]{1,0:T(8,128)}) %tuple.26), branch_computations={%region_9.10_spmd, %region_10.11_spmd} | conditional | flops 6445596672 | bytes 12582920 | solution.py:196
  215.7 13.0 %fusion.2 = f32[1,1024,1024]{2,1,0:T(8,128)} fusion(f32[1,1024,1024]{2,1,0:T(8,128)} %get-tuple-element.33, f32[1024,1024]{1,0:T(8,128)} %get-tuple-element.34), kind=kOutput, calls=%fused_computation.13 | convolution fusion | flops 6445596672 | bytes 12582912 | tf_op jit(solution)/shard_map/cond/branch_1_fun/dot_general | solution.py:55
  230.3 6.3 %shard_map.94 = f32[64,8192]{1,0:T(8,128)} custom-call(s32[8]{0:T(128)} %bitcast.100, f32[8]{0:T(128)} %minimum_multiply_fusion.scale_ref, f32[8,64,1024]{2,1,0:T(8,128)} %all-to-all-done.1.p_ref), custom_call_target="tpu_custom_call" | custom-call | flops 524288 | bytes 4194304 | tf_op jit(solution)/shard_map/pallas_call | solution.py:87
  (98 shorter events, 74.8 us)
Async XLA Ops:
  11.7 24.8 %collective-permute-start.5 = (f32[2,64,1024]{2,1,0:T(8,128)}, f32[2,64,1024]{2,1,0:T(8,128)}, u32[]{:S(2)}, u32[]{:S(2)}) collective-permute-start(f32[2,64,1024]{2,1,0:T(8,128)} %get-tuple-element.60), channel_id=1, source_target_pairs={{0,4},{1,5},{2,6},{3,7},{4,8},{5,9},{6,10},{7,11},{8,12},{9,13},{1... | collective-permute-start | bytes 1572872 | tf_op jit(solution)/shard_map/ppermute | solution.py:46
  12.1 25.6 %collective-permute-start.6 = (f32[2,64,1024]{2,1,0:T(8,128)}, f32[2,64,1024]{2,1,0:T(8,128)}, u32[]{:S(2)}, u32[]{:S(2)}) collective-permute-start(f32[2,64,1024]{2,1,0:T(8,128)} %get-tuple-element.59), channel_id=1, source_target_pairs={{0,8},{1,9},{2,10},{3,11},{4,12},{5,13},{6,14},{7,15},{8,0},{9,1},... | collective-permute-start | bytes 1572872 | tf_op jit(solution)/shard_map/ppermute | solution.py:46
  14.6 25.3 %collective-permute-start.7 = (f32[2,64,1024]{2,1,0:T(8,128)}, f32[2,64,1024]{2,1,0:T(8,128)}, u32[]{:S(2)}, u32[]{:S(2)}) collective-permute-start(f32[2,64,1024]{2,1,0:T(8,128)} %get-tuple-element.58), channel_id=1, source_target_pairs={{0,12},{1,13},{2,14},{3,15},{4,0},{5,1},{6,2},{7,3},{8,4},{9,5},{1... | collective-permute-start | bytes 1572872 | tf_op jit(solution)/shard_map/ppermute | solution.py:46
  16.6 18.1 %collective-permute-start.8 = (f32[64,1024]{1,0:T(8,128)}, f32[64,1024]{1,0:T(8,128)S(1)}, u32[]{:S(2)}, u32[]{:S(2)}) collective-permute-start(f32[64,1024]{1,0:T(8,128)} %get-tuple-element.57), channel_id=1, source_target_pairs={{0,3},{1,2},{2,1},{3,0},{4,7},{5,6},{6,5},{7,4},{8,11},{9,10},{10,... | collective-permute-start | bytes 786440 | tf_op jit(solution)/shard_map/ppermute | solution.py:42
  19.6 38.9 %collective-permute-start.12 = (f32[64,1024]{1,0:T(8,128)}, f32[64,1024]{1,0:T(8,128)}, u32[]{:S(2)}, u32[]{:S(2)}) collective-permute-start(f32[64,1024]{1,0:T(8,128)} %get-tuple-element.56), channel_id=1, source_target_pairs={{0,1},{1,0},{2,3},{3,2},{4,5},{5,4},{6,7},{7,6},{8,9},{9,8},{10,11... | collective-permute-start | bytes 786440 | tf_op jit(solution)/shard_map/ppermute | solution.py:38
  34.6 87.4 %collective-permute-start.4 = (f32[520,1024]{1,0:T(8,128)}, f32[520,1024]{1,0:T(8,128)S(1)}, u32[]{:S(2)}, u32[]{:S(2)}) collective-permute-start(f32[520,1024]{1,0:T(8,128)} %fusion.3), channel_id=1, source_target_pairs={{0,1},{1,0},{2,3},{3,2},{4,5},{5,4},{6,7},{7,6},{8,9},{9,8},{10,11... | collective-permute-start | bytes 6389768 | tf_op jit(solution)/shard_map/ppermute | solution.py:38
  36.5 72.7 %collective-permute-start.16 = (f32[64,1024]{1,0:T(8,128)S(1)}, f32[64,1024]{1,0:T(8,128)S(1)}, u32[]{:S(2)}, u32[]{:S(2)}) collective-permute-start(f32[64,1024]{1,0:T(8,128)S(1)} %collective-permute-done.8), channel_id=1, source_target_pairs={{0,1},{1,0},{2,3},{3,2},{4,5},{5,4},{6,7},{7,6},{8,9},{9,8},{10,11... | collective-permute-start | bytes 786440 | tf_op jit(solution)/shard_map/ppermute | solution.py:38
  37.8 11.4 %collective-permute-start.9 = (f32[64,1024]{1,0:T(8,128)S(1)}, f32[64,1024]{1,0:T(8,128)S(1)}, u32[]{:S(2)}, u32[]{:S(2)}) collective-permute-start(f32[64,1024]{1,0:T(8,128)S(1)} %get-tuple-element.66), channel_id=1, source_target_pairs={{0,3},{1,2},{2,1},{3,0},{4,7},{5,6},{6,5},{7,4},{8,11},{9,10},{10,... | collective-permute-start | bytes 786440 | tf_op jit(solution)/shard_map/ppermute | solution.py:42
  40.0 11.3 %collective-permute-start.10 = (f32[64,1024]{1,0:T(8,128)S(1)}, f32[64,1024]{1,0:T(8,128)S(1)}, u32[]{:S(2)}, u32[]{:S(2)}) collective-permute-start(f32[64,1024]{1,0:T(8,128)S(1)} %get-tuple-element.64), channel_id=1, source_target_pairs={{0,3},{1,2},{2,1},{3,0},{4,7},{5,6},{6,5},{7,4},{8,11},{9,10},{10,... | collective-permute-start | bytes 786440 | tf_op jit(solution)/shard_map/ppermute | solution.py:42
  49.2 8.6 %collective-permute-start.11 = (f32[64,1024]{1,0:T(8,128)S(1)}, f32[64,1024]{1,0:T(8,128)S(1)}, u32[]{:S(2)}, u32[]{:S(2)}) collective-permute-start(f32[64,1024]{1,0:T(8,128)S(1)} %get-tuple-element.62), channel_id=1, source_target_pairs={{0,3},{1,2},{2,1},{3,0},{4,7},{5,6},{6,5},{7,4},{8,11},{9,10},{10,... | collective-permute-start | bytes 786440 | tf_op jit(solution)/shard_map/ppermute | solution.py:42
  51.3 44.1 %collective-permute-start.13 = (f32[64,1024]{1,0:T(8,128)S(1)}, f32[64,1024]{1,0:T(8,128)S(1)}, u32[]{:S(2)}, u32[]{:S(2)}) collective-permute-start(f32[64,1024]{1,0:T(8,128)S(1)} %get-tuple-element.65), channel_id=1, source_target_pairs={{0,1},{1,0},{2,3},{3,2},{4,5},{5,4},{6,7},{7,6},{8,9},{9,8},{10,11... | collective-permute-start | bytes 786440 | tf_op jit(solution)/shard_map/ppermute | solution.py:38
  57.8 43.2 %collective-permute-start.14 = (f32[64,1024]{1,0:T(8,128)S(1)}, f32[64,1024]{1,0:T(8,128)S(1)}, u32[]{:S(2)}, u32[]{:S(2)}) collective-permute-start(f32[64,1024]{1,0:T(8,128)S(1)} %get-tuple-element.63), channel_id=1, source_target_pairs={{0,1},{1,0},{2,3},{3,2},{4,5},{5,4},{6,7},{7,6},{8,9},{9,8},{10,11... | collective-permute-start | bytes 786440 | tf_op jit(solution)/shard_map/ppermute | solution.py:38
  58.5 48.1 %collective-permute-start.15 = (f32[64,1024]{1,0:T(8,128)S(1)}, f32[64,1024]{1,0:T(8,128)S(1)}, u32[]{:S(2)}, u32[]{:S(2)}) collective-permute-start(f32[64,1024]{1,0:T(8,128)S(1)} %get-tuple-element.61), channel_id=1, source_target_pairs={{0,1},{1,0},{2,3},{3,2},{4,5},{5,4},{6,7},{7,6},{8,9},{9,8},{10,11... | collective-permute-start | bytes 786440 | tf_op jit(solution)/shard_map/ppermute | solution.py:38
  95.4 16.9 %collective-permute-start.17 = (f32[64,1024]{1,0:T(8,128)S(1)}, f32[64,1024]{1,0:T(8,128)S(1)}, u32[]{:S(2)}, u32[]{:S(2)}) collective-permute-start(f32[64,1024]{1,0:T(8,128)S(1)} %collective-permute-done.9), channel_id=1, source_target_pairs={{0,1},{1,0},{2,3},{3,2},{4,5},{5,4},{6,7},{7,6},{8,9},{9,8},{10,11... | collective-permute-start | bytes 786440 | tf_op jit(solution)/shard_map/ppermute | solution.py:38
  101.0 16.9 %collective-permute-start.18 = (f32[64,1024]{1,0:T(8,128)S(1)}, f32[64,1024]{1,0:T(8,128)S(1)}, u32[]{:S(2)}, u32[]{:S(2)}) collective-permute-start(f32[64,1024]{1,0:T(8,128)S(1)} %collective-permute-done.10), channel_id=1, source_target_pairs={{0,1},{1,0},{2,3},{3,2},{4,5},{5,4},{6,7},{7,6},{8,9},{9,8},{10,11... | collective-permute-start | bytes 786440 | tf_op jit(solution)/shard_map/ppermute | solution.py:38
  106.6 14.7 %collective-permute-start.19 = (f32[64,1024]{1,0:T(8,128)S(1)}, f32[64,1024]{1,0:T(8,128)S(1)}, u32[]{:S(2)}, u32[]{:S(2)}) collective-permute-start(f32[64,1024]{1,0:T(8,128)S(1)} %collective-permute-done.11), channel_id=1, source_target_pairs={{0,1},{1,0},{2,3},{3,2},{4,5},{5,4},{6,7},{7,6},{8,9},{9,8},{10,11... | collective-permute-start | bytes 786440 | tf_op jit(solution)/shard_map/ppermute | solution.py:38
  161.2 69.1 %all-to-all-start.1 = ((f32[8,64,1024]{2,1,0:T(8,128)}), f32[8,64,1024]{2,1,0:T(8,128)}, u32[]{:S(2)}, u32[]{:S(2)}) async-start(f32[8,64,1024]{2,1,0:T(8,128)} %bitcast.94), calls=%async_computation.1 | async-start | bytes 4194304 | tf_op jit(solution)/shard_map/all_to_all | solution.py:186
  173.5 17.5 %collective-permute-start = (f32[8]{0:T(128)S(1)}, f32[8]{0:T(128)S(1)}, u32[]{:S(2)}, u32[]{:S(2)}) collective-permute-start(f32[8]{0:T(128)S(1)} %reduce_sum.63), channel_id=1, source_target_pairs={{0,4},{1,5},{2,6},{3,7},{4,0},{5,1},{6,2},{7,3},{8,12},{9,13},{10,... | collective-permute-start | bytes 104 | tf_op jit(solution)/shard_map/ppermute | solution.py:51
  191.0 5.0 %collective-permute-start.1 = (f32[8]{0:T(128)S(1)}, f32[8]{0:T(128)S(1)}, u32[]{:S(2)}, u32[]{:S(2)}) collective-permute-start(f32[8]{0:T(128)S(1)} %add.207), channel_id=1, source_target_pairs={{0,8},{1,9},{2,10},{3,11},{4,12},{5,13},{6,14},{7,15},{8,0},{9,1},... | collective-permute-start | bytes 104 | tf_op jit(solution)/shard_map/ppermute | solution.py:51
  196.0 4.8 %collective-permute-start.2 = (f32[8]{0:T(128)S(1)}, f32[8]{0:T(128)S(1)}, u32[]{:S(2)}, u32[]{:S(2)}) collective-permute-start(f32[8]{0:T(128)S(1)} %add.208), channel_id=1, source_target_pairs={{0,3},{1,2},{2,1},{3,0},{4,7},{5,6},{6,5},{7,4},{8,11},{9,10},{10,... | collective-permute-start | bytes 104 | tf_op jit(solution)/shard_map/ppermute | solution.py:51
  200.8 3.5 %collective-permute-start.3 = (f32[8]{0:T(128)S(1)}, f32[8]{0:T(128)S(1)}, u32[]{:S(2)}, u32[]{:S(2)}) collective-permute-start(f32[8]{0:T(128)S(1)} %add.209), channel_id=1, source_target_pairs={{0,1},{1,0},{2,3},{3,2},{4,5},{5,4},{6,7},{7,6},{8,9},{9,8},{10,11... | collective-permute-start | bytes 104 | tf_op jit(solution)/shard_map/ppermute | solution.py:51
  205.6 1.2 collective-permute-start.20
  207.4 3.6 %collective-permute-start.21 = (f32[8]{0:T(128)S(1)}, f32[8]{0:T(128)S(1)}, u32[]{:S(2)}, u32[]{:S(2)}) collective-permute-start(f32[8]{0:T(128)S(1)} %broadcast_add_fusion.1), channel_id=1, source_target_pairs={{0,32},{16,48},{32,0},{48,16},{64,96},{80,112},{96,64},{112,80},{1... | collective-permute-start | bytes 104 | tf_op jit(solution)/shard_map/ppermute | solution.py:51
  211.7 18.0 %collective-permute-start.22 = (f32[8]{0:T(128)S(1)}, f32[8]{0:T(128)S(1)}, u32[]{:S(2)}, u32[]{:S(2)}) collective-permute-start(f32[8]{0:T(128)S(1)} %fusion.23), channel_id=1, source_target_pairs={{0,64},{16,80},{32,96},{48,112},{64,0},{80,16},{96,32},{112,48},{1... | collective-permute-start | bytes 104 | tf_op jit(solution)/shard_map/ppermute | solution.py:51
  (4 other events, 107.8 us)

commit v2 on v1

v2 whole, which is shorter than its diff:
```python
import math

import jax
import jax.numpy as jnp
from jax import lax
from jax.experimental import pallas as pl
from jax.experimental.pallas import tpu as pltpu
from jax.sharding import PartitionSpec as P

BETA_STAT = 0.95
BETA_ONE = 0.9
BETA_TWO = 0.999
BIAS_ONE = 1.0 - 0.9**10
BIAS_TWO = 1.0 - 0.999**10
ADAM_EPS = 1e-08
CLIP_RMS = 0.25
SIDE = 4


def route(move):
    pairs = []
    for src in range(SIDE * SIDE):
        x, y = move(src // SIDE, src % SIDE)
        pairs.append((src, (x % SIDE) * SIDE + y % SIDE))
    return pairs


NEAR = route(lambda x, y: (x, y ^ 1))
FAR = route(lambda x, y: (x, 3 - y))
VMEM_BYTES = 56 * 2**20
GROUPS = [
    [SIDE * x + y for x in range(SIDE) for y in (0, 3)],
    [SIDE * x + y for x in range(SIDE) for y in (1, 2)],
]


def near(v):
    return lax.ppermute(v, "dp", NEAR)


def far(v):
    return lax.ppermute(v, "dp", FAR)


def along_x(v, shift):
    return lax.ppermute(v, "dp", route(lambda x, y: (x + shift, y)))


def swap(v, axis, bit):
    count = lax.axis_size(axis)
    return lax.ppermute(v, axis, [(i, i ^ bit) for i in range(count)])

ANY = pl.BlockSpec(memory_space=pl.ANY)
VMEM = pl.BlockSpec(memory_space=pltpu.VMEM)
SMEM = pl.BlockSpec(memory_space=pltpu.SMEM)


def call(body, out, in_specs, out_specs, scratch, flops, moved):
    return pl.pallas_call(
        body,
        out_shape=out,
        in_specs=in_specs,
        out_specs=out_specs,
        scratch_shapes=scratch,
        compiler_params=pltpu.CompilerParams(vmem_limit_bytes=VMEM_BYTES),
        cost_estimate=pl.CostEstimate(flops=flops, bytes_accessed=moved, transcendentals=0),
    )


def f32(*shape):
    return jax.ShapeDtypeStruct(shape, jnp.float32)


def spot():
    place = lax.axis_index("dp")
    x, y = lax.shift_right_logical(place, 2), lax.bitwise_and(place, 3)
    is_left = lax.bitwise_and(y, 1) == 0
    outer = jnp.logical_or(y == 0, y == 3)
    return x, y, is_left, outer


def side_y(outer, g):
    return jnp.where(outer, 3 * g, 1 + g)


def run(copies):
    for copy in copies:
        copy.start()
    return copies


def finish(copies):
    for copy in copies:
        copy.wait()


def split(v):
    high = v.astype(jnp.bfloat16)
    return high, (v - high.astype(jnp.float32)).astype(jnp.bfloat16)


def mul(a, b):
    return jnp.dot(a, b, preferred_element_type=jnp.float32)


def mul_split(a_high, a_low, b_high, b_low):
    return mul(a_high, b_high) + (mul(a_high, b_low) + mul(a_low, b_high))


def cut(gradient, root, owner_table):
    rows, width = gradient.shape
    order = root.shape[0]
    half = order // 2
    count = width // order
    part = rows // 2

    def body(owner_ref, g_ref, root_ref, own_ref, oth_ref, x1_ref, x2_ref, x3_ref, c_ref, sems):
        x, y, is_left, outer = spot()
        outs = [(own_ref, oth_ref)] + [(r.at[0], r.at[1]) for r in (x1_ref, x2_ref, x3_ref)]
        copies = []
        for d in range(SIDE):
            for j in range(2):
                pos = 2 * lax.bitwise_and(x + d, 3) + lax.bitwise_xor(lax.shift_right_logical(y, 1), j)
                col = jnp.int32(0)
                for c in range(count):
                    col = col + jnp.where(owner_ref[0, c] == pos, c, 0)
                copies.append(
                    pltpu.make_async_copy(
                        g_ref.at[:, pl.ds(pl.multiple_of(col * order, order), order)],
                        outs[d][j],
                        sems.at[2 * d + j],
                    )
                )
        run(copies)

        @pl.when(is_left)
        def _():
            sent = []
            for k in range(2 * SIDE):
                row = ((k // 2) * SIDE + side_y(jnp.logical_not(outer), k % 2)) * rows
                sent.append(
                    pltpu.make_async_copy(
                        root_ref.at[pl.ds(pl.multiple_of(row, rows), part), :],
                        c_ref.at[pl.ds(k * part, part), :],
                        sems.at[2 * SIDE + k],
                    )
                )
            finish(run(sent))

        @pl.when(jnp.logical_not(is_left))
        def _():
            finish(
                run(
                    [
                        pltpu.make_async_copy(
                            root_ref.at[pl.ds(h * half // 2, half // 2), pl.ds(half, half)],
                            c_ref.at[:, pl.ds(h * half, half)],
                            sems.at[2 * SIDE + h],
                        )
                        for h in range(2)
                    ]
                )
            )

        finish(copies)

    return call(
        body,
        [f32(rows, order)] * 2 + [f32(2, rows, order)] * 3 + [f32(half // 2, order)],
        [SMEM, ANY, ANY],
        [ANY] * 6,
        [pltpu.SemaphoreType.DMA((4 * SIDE,))],
        0,
        24 * rows * width,
    )(owner_table, gradient, root)


def pack(root, rows, which, *after):
    order = root.shape[0]
    half, quarter = order // 2, order // 4
    part = rows // 4

    def body(root_ref, *refs):
        out_ref, buf, sems = refs[len(after) :]
        x, y, is_left, outer = spot()
        body_rows = 2 * SIDE * part
        out_ref[body_rows:, :] = jnp.zeros((8, order), jnp.float32)

        @pl.when(is_left)
        def _():
            sent = []
            for k in range(2 * SIDE):
                row = ((k // 2) * SIDE + side_y(jnp.logical_not(outer), k % 2)) * rows
                row = row + rows // 2 + which * part
                sent.append(
                    pltpu.make_async_copy(
                        root_ref.at[pl.ds(pl.multiple_of(row, part), part), :],
                        out_ref.at[pl.ds(k * part, part), :],
                        sems.at[k],
                    )
                )
            finish(run(sent))

        @pl.when(jnp.logical_not(is_left))
        def _():
            at = pl.ds(which * half, half)
            finish(run([pltpu.make_async_copy(root_ref.at[at, at], buf, sems.at[0])]))
            row = lax.broadcasted_iota(jnp.int32, (quarter, quarter), 0)
            col = lax.broadcasted_iota(jnp.int32, (quarter, quarter), 1)
            low = buf[quarter:, quarter:]
            both = jnp.where(row <= col, buf[:quarter, :quarter], low)
            mid = quarter // 2
            for h in range(2):
                out_ref[:body_rows, h * half : h * half + quarter] = buf[h * mid : (h + 1) * mid, quarter:]
                out_ref[:body_rows, h * half + quarter : (h + 1) * half] = both[h * mid : (h + 1) * mid]
            out_ref[body_rows : body_rows + 1, :quarter] = jnp.sum(
                jnp.where(row == col, low, 0.0), axis=0, keepdims=True
            )

    return call(
        body,
        f32(2 * SIDE * part + 8, order),
        [ANY] * (1 + len(after)),
        VMEM,
        [pltpu.VMEM((half, half), jnp.float32), pltpu.SemaphoreType.DMA((2 * SIDE,))],
        0,
        4 * half * order,
    )(root, *after)


def first_product(pieces, root):
    rows, order = pieces[0].shape
    half, tile = order // 2, order // 4
    count = len(pieces)

    def body(*refs):
        piece_refs, root_ref = refs[:count], refs[count]
        g_out, high_ref, low_ref, g_buf, r_buf, g_high, g_low, r_high, r_low, sems = refs[count + 1 :]
        x, y, is_left, outer = spot()
        from_y = (y, 3 - y, lax.bitwise_xor(y, 1), 3 - lax.bitwise_xor(y, 1))
        copies = []
        for k in range(count):
            row = (lax.bitwise_and(x - k % SIDE, 3) * SIDE + from_y[k // SIDE]) * rows
            copies.append(
                pltpu.make_async_copy(
                    piece_refs[k], g_buf.at[pl.ds(pl.multiple_of(row, rows), rows), :], sems.at[k]
                )
            )
        run(copies)

        def cut_two(src, high, low, first, last):
            def step(i, carry):
                at = pl.ds(pl.multiple_of(i * 64, 64), 64)
                a, b = split(src[at, :])
                high[at, :] = a
                low[at, :] = b
                return carry

            lax.fori_loop(first, last, step, 0)

        @pl.when(is_left)
        def _():
            sent = []
            for k in range(2 * SIDE):
                row = ((k // 2) * SIDE + side_y(outer, k % 2)) * rows
                sent.append(
                    pltpu.make_async_copy(
                        root_ref.at[pl.ds(pl.multiple_of(row, rows), rows), :],
                        r_buf.at[pl.ds(k * rows, rows), :],
                        sems.at[count + k],
                    )
                )
            finish(run(sent))
            cut_two(r_buf, r_high, r_low, 0, half // 64)

        @pl.when(jnp.logical_not(is_left))
        def _():
            finish(run([pltpu.make_async_copy(root_ref, r_buf, sems.at[count])]))
            cut_two(r_buf, r_high, r_low, 0, order // 64)

        finish(copies)
        out = pltpu.make_async_copy(g_buf, g_out, sems.at[0])
        out.start()
        cut_two(g_buf, g_high, g_low, 0, order // 64)

        def product(a_high, a_low, b_high, b_low, tiles):
            def step(i, carry):
                at = pl.ds(pl.multiple_of(i * tile, tile), tile)
                for n in range(2):
                    cols = slice(n * half, (n + 1) * half)
                    acc = mul_split(a_high[at, :], a_low[at, :], b_high[:, cols], b_low[:, cols])
                    high_ref[at, cols], low_ref[at, cols] = split(acc)
                return carry

            lax.fori_loop(0, tiles, step, 0)

        @pl.when(is_left)
        def _():
            product(r_high, r_low, g_high, g_low, 2)

        @pl.when(jnp.logical_not(is_left))
        def _():
            product(g_high, g_low, r_high, r_low, 4)

        out.wait()

    part = jax.ShapeDtypeStruct((order, order), jnp.bfloat16)
    whole = pltpu.VMEM((order, order), jnp.float32)
    short = pltpu.VMEM((order, order), jnp.bfloat16)
    return call(
        body,
        [f32(order, order), part, part],
        [ANY] * (count + 1),
        [ANY, VMEM, VMEM],
        [whole, whole, short, short, short, short, pltpu.SemaphoreType.DMA((count + 2 * SIDE,))],
        6 * order**3,
        16 * order * order,
    )(*pieces, root)


def unfold(c_ref, b_high, b_low, base):
    half = c_ref.shape[1] // 2
    quarter = half // 2
    mid = quarter // 2
    row = lax.broadcasted_iota(jnp.int32, (quarter, quarter), 0)
    col = lax.broadcasted_iota(jnp.int32, (quarter, quarter), 1)
    cross = jnp.concatenate([c_ref[:mid, :quarter], c_ref[:mid, half : half + quarter]], axis=0)
    both = jnp.concatenate([c_ref[:mid, quarter:half], c_ref[:mid, half + quarter :]], axis=0)
    diag = c_ref[mid : mid + 1, :quarter]
    turned = both.T
    top = jnp.where(row <= col, both, turned)
    low = jnp.where(row > col, both, jnp.where(row == col, diag, turned))
    for r, left_mat, right_mat in ((0, top, cross), (1, cross.T, low)):
        at = slice(base + r * quarter, base + (r + 1) * quarter)
        b_high[at, :quarter], b_low[at, :quarter] = split(left_mat)
        b_high[at, quarter:], b_low[at, quarter:] = split(right_mat)


def second_product(which, t_high, t_low, chunks, squares):
    order = t_high.shape[0]
    half, quarter = order // 2, order // 4
    dests = 2 * SIDE
    part = quarter // dests
    count = len(chunks)

    def body(high_ref, low_ref, *refs):
        chunk_refs, sq_ref = refs[:count], refs[count]
        out_ref, sq_out, b_high, b_low = refs[count + 1 :]
        x, y, is_left, outer = spot()

        @pl.when(is_left)
        def _():
            c_ref = chunk_refs[0]
            if which == 0:
                unfold(chunk_refs[1], b_high, b_low, 0)
                for h in range(2):
                    cols = slice(h * quarter, (h + 1) * quarter)
                    turned = c_ref[:, h * half : (h + 1) * half].T
                    b_high[half:, cols], b_low[half:, cols] = split(turned)
            else:
                for h in range(2):
                    at = slice(h * quarter, (h + 1) * quarter)
                    b_high[at, :], b_low[at, :] = split(c_ref[:, h * half : (h + 1) * half])
                unfold(chunk_refs[2], b_high, b_low, half)
            total = jnp.float32(0.0)
            for m in range(2):
                at = slice(m * quarter, (m + 1) * quarter)
                acc = mul_split(high_ref[at, :], low_ref[at, :], b_high[...], b_low[...])
                total = total + jnp.sum(acc * acc)
                for k in range(SIDE):
                    for h in range(2):
                        first = (2 * k + h) * part
                        out_ref[m * SIDE + k, :, h * half : (h + 1) * half] = acc[first : first + part]
            sq_out[...] = sq_ref[...] + total

        @pl.when(jnp.logical_not(is_left))
        def _():
            if which == 0:
                a = chunk_refs[0][...]
            else:
                a = jnp.concatenate([chunk_refs[1][: quarter // 2], chunk_refs[2][: quarter // 2]], axis=0)
            a_high, a_low = split(a)
            total = jnp.float32(0.0)
            for n in range(2):
                cols = slice(n * half, (n + 1) * half)
                acc = mul_split(a_high, a_low, high_ref[:, cols], low_ref[:, cols])
                total = total + jnp.sum(acc * acc)
                for k in range(dests):
                    if which == 0:
                        out_ref[k, :, cols] = acc[k * part : (k + 1) * part]
                    else:
                        few = part // 2
                        out_ref[k, :few, cols] = acc[k * few : (k + 1) * few]
                        out_ref[k, few:, cols] = acc[quarter // 2 + k * few : quarter // 2 + (k + 1) * few]
            sq_out[...] = sq_ref[...] + total

    short = pltpu.VMEM((order, half), jnp.bfloat16)
    return call(
        body,
        [f32(dests, part, order), f32(8, 128)],
        [VMEM] * (3 + count),
        [VMEM, VMEM],
        [short, short],
        3 * order**3 // 2,
        10 * order * order,
    )(t_high, t_low, *chunks, squares)


def update_statistics(block, stat, after):
    order = block.shape[0]
    tile = order // 4
    tiles = order // tile

    def body(g_ref, s_ref, after_ref, out_ref, high, low):
        x, y, is_left, outer = spot()

        @pl.when(is_left)
        def _():
            for i in range(tiles):
                at = slice(i * tile, (i + 1) * tile)
                high[at, :], low[at, :] = split(g_ref[at, :])

        @pl.when(jnp.logical_not(is_left))
        def _():
            for i in range(tiles):
                for j in range(tiles):
                    at, cols = slice(i * tile, (i + 1) * tile), slice(j * tile, (j + 1) * tile)
                    high[at, cols], low[at, cols] = split(g_ref[cols, at].T)

        def outer_mul(a, b):
            return lax.dot_general(a, b, (((1,), (1,)), ((), ())), preferred_element_type=jnp.float32)

        for i in range(tiles):
            at = slice(i * tile, (i + 1) * tile)
            for j in range(i, tiles):
                to = slice(j * tile, (j + 1) * tile)
                acc = outer_mul(high[at, :], high[to, :]) + (
                    outer_mul(high[at, :], low[to, :]) + outer_mul(low[at, :], high[to, :])
                )
                acc = (1.0 - BETA_STAT) * acc
                out_ref[at, to] = BETA_STAT * s_ref[at, to] + acc
                if i != j:
                    out_ref[to, at] = BETA_STAT * s_ref[to, at] + acc.T

    short = pltpu.VMEM((order, order), jnp.bfloat16)
    return call(
        body,
        f32(order, order),
        [VMEM, VMEM, ANY],
        VMEM,
        [short, short],
        4 * order**3,
        12 * order * order,
    )(block, stat, after)


def place_columns(first, second, owner_table, scale):
    count, part, order = first.shape
    half = order // 2

    def body(owner_ref, scale_ref, first_ref, second_ref, out_ref):
        x, y, is_left, outer = spot()
        for c in range(count):
            p = owner_ref[0, c]
            s = scale_ref[c]
            from_left = (lax.bitwise_and(p, 1) == 0) == outer
            a, b = first_ref[p, :, :half], first_ref[p, :, half:]
            d, e = second_ref[p, :, :half], second_ref[p, :, half:]
            out_ref[:part, c * order : c * order + half] = a * s
            out_ref[:part, c * order + half : (c + 1) * order] = jnp.where(from_left, d, b) * s
            out_ref[part:, c * order : c * order + half] = jnp.where(from_left, b, d) * s
            out_ref[part:, c * order + half : (c + 1) * order] = e * s

    return call(
        body,
        f32(2 * part, count * order),
        [SMEM, SMEM, VMEM, VMEM],
        VMEM,
        [],
        count * part * order,
        16 * count * part * order,
    )(owner_table, scale, first, second)


def sent_back(v):
    return lax.all_to_all(v, "dp", 0, 0, axis_index_groups=GROUPS, tiled=True)


def local(gradient, moment, second, statistics, inv_roots, owner_table):
    rows_dev, width = gradient.shape
    order = statistics.shape[1]
    col_blocks = width // order
    root = inv_roots[0]

    own, oth, x1, x2, x3, chunk = cut(gradient, root, owner_table)
    near_own = [near(own)]
    chunk_a = near(chunk)
    far_y = [far(oth)]
    own_y = [own]
    for d, v in ((1, x1), (3, x3), (2, x2)):
        arrived = along_x(v, d)
        own_y.append(arrived[0])
        far_y.append(far(arrived[1]))
    near_far = [near(far_y[0])]
    for d in range(1, SIDE):
        near_own.append(near(own_y[d]))
        near_far.append(near(far_y[d]))

    new_moment = BETA_ONE * moment + (1.0 - BETA_ONE) * gradient
    new_second = BETA_TWO * second + (1.0 - BETA_TWO) * gradient * gradient
    adam_step = new_moment / BIAS_ONE / (jnp.sqrt(new_second / BIAS_TWO) + ADAM_EPS)
    sums = jnp.sum((adam_step * adam_step).reshape(rows_dev, col_blocks, order), axis=(0, 2))
    for bit in (4, 8, 3):
        sums = sums + swap(sums, "dp", bit)
    total = jnp.broadcast_to(jnp.sum(sums), sums.shape)
    bit = 1
    while bit < lax.axis_size("fsdp"):
        total = total + swap(total, "fsdp", bit)
        bit *= 2
    sums = jnp.stack([sums, total])

    chunk_b = near(pack(root, rows_dev, 0, near_far[1], sums))
    chunk_c = near(pack(root, rows_dev, 1, near_far[2]))
    sums = sums + swap(sums, "dp", 1)

    order_d = (0, 1, 3, 2)
    pieces = []
    for group in (own_y, far_y, near_own, near_far):
        by_shift = dict(zip(order_d, group))
        pieces += [by_shift[d] for d in range(SIDE)]
    block, t_high, t_low = first_product(pieces, root)
    half_a, squares = second_product(
        0, t_high, t_low, [chunk_a, chunk_b], jnp.zeros((8, 128), jnp.float32)
    )
    back_a = sent_back(half_a)
    half_b, squares = second_product(1, t_high, t_low, [chunk_a, chunk_b, chunk_c], squares)
    back_b = sent_back(half_b)
    squares = squares + near(squares)
    prec_sq = sent_back(jnp.broadcast_to(squares, (2 * SIDE, 8, 128)))[:, 0, 0]

    new_stat = update_statistics(block, statistics[0], half_b)

    ratio = jnp.sqrt(sums[0] / (prec_sq[owner_table[0]] + 1e-06))
    count_all = order * lax.axis_size("fsdp") * width
    clip = jnp.minimum(1.0, CLIP_RMS * math.sqrt(count_all) / jnp.sqrt(sums[1] + 1e-06))
    update = place_columns(back_a, back_b, owner_table, ratio * clip)
    return (update, new_moment, new_second, new_stat[None])


def solution(mesh):
    placed = (
        P(("fsdp", "dp"), None),
        P(("fsdp", "dp"), None),
        P(("fsdp", "dp"), None),
        P(("fsdp", "dp"), None, None),
        P(("fsdp", "dp"), None, None),
        P("fsdp", None),
    )
    return jax.shard_map(
        local,
        mesh=mesh,
        in_specs=placed,
        out_specs=(
            P(("fsdp", "dp"), None),
            P(("fsdp", "dp"), None),
            P(("fsdp", "dp"), None),
            P(("fsdp", "dp"), None, None),
        ),
        check_vma=False,
    )
```

time: 238 us -> 297 us (1.25)
  Pallas kernels: 12.7 us -> 137 us
  local copies, waits for them, and re-layouts: 37.5 us -> 5.1 us
  matrix products: 28.3 us -> 0 us
  other arithmetic: 24.7 us -> 7.54 us
  starting transfers between devices: 34.9 us -> 49.3 us
    pallas_call x2 -> x8, Pallas kernels: 12.7 us -> 137 us  [the longest x1 97.4 us: cut(): call(body, [f32(rows, order)] * 2 + [f32(2, rows, order)] * 3 + [f32(half...]
    dot_general x3 -> x0, matrix products: 28.3 us -> none  [dot(): lax.dot_general(a, b, (((a_dim,), (b_dim,)), ((), ())), precision=SPLIT,...]
    dynamic_update_slice x16 -> x0, local copies, waits for them, and re-layouts: 16.4 us -> none  [local(): lax.dynamic_update_slice(block, pieces[d][None, None], ((x - d) % SIDE, f...]
    ppermute x7, waiting for transfers between devices: 32.3 us -> 20.3 us  [swap(): return lax.ppermute(v, axis, [(i, i ^ bit) for i in range(count)])]
    all_to_all x1 -> x2, waiting for transfers between devices: 0.01 us -> 10.8 us  [sent_back(): return lax.all_to_all(v, 'dp', 0, 0, axis_index_groups=GROUPS, tiled=True)]
    select_n x5 -> x1, other arithmetic: 9.72 us -> 0.01 us  [local(): ratio = jnp.sqrt(sums[0] / (prec_sq[owner_table[0]] + 1e-06))]
    slice x5 -> x1, local copies, waits for them, and re-layouts: 7.29 us -> 0.14 us  [local(): prec_sq = sent_back(jnp.broadcast_to(squares, (2 * SIDE, 8, 128)))[:, 0, 0]]
    squeeze x4 -> x3, local copies, waits for them, and re-layouts: 5.11 us -> 0.12 us  [local(): far_y.append(far(arrived[1]))]
  transfers between devices with their start and end apart: 24 -> 28, of which waited for: 14 -> 17; matrix products, arithmetic and copies ran while one was open for 24% -> 3% of each run, Pallas kernels for 0% -> 10%
where the time goes in v2:
time: 297 us; the launch traced here: 296 us
  Pallas kernels  137 us (46%)
  waiting for transfers between devices  84.2 us (28%)
  starting transfers between devices  49.3 us (17%)
  blocking collectives  12.5 us (4%)
  other arithmetic  7.54 us (3%)
  local copies, waits for them, and re-layouts  5.1 us (2%)
    pallas_call x1, Pallas kernels, cut(): call(body, [f32(rows, order)] * 2 + [f32(2, rows, order)] * 3 + [f32(half...  97.4 us
    ppermute x12, waiting for transfers between devices, near(): return lax.ppermute(v, 'dp', NEAR)  48.5 us
    ppermute x7, waiting for transfers between devices, swap(): return lax.ppermute(v, axis, [(i, i ^ bit) for i in range(count)])  20.3 us
    ppermute x12, starting transfers between devices, near(): return lax.ppermute(v, 'dp', NEAR)  14.5 us
    all_to_all x1, blocking collectives, sent_back(): return lax.all_to_all(v, 'dp', 0, 0, axis_index_groups=GROUPS, tiled=True)  12.5 us
    ppermute x7, starting transfers between devices, swap(): return lax.ppermute(v, axis, [(i, i ^ bit) for i in range(count)])  11.8 us
    pallas_call x2, Pallas kernels, second_product(): call(body, [f32(dests, part, order), f32(8, 128)], [VMEM] * (3 + count),...  11.7 us
    pallas_call x1, Pallas kernels, update_statistics(): call(body, f32(order, order), [VMEM, VMEM, ANY], VMEM, [short, short], 4...  10.8 us
  transfers between devices with their start and end apart: 28, of which 17 were waited for; matrix products, arithmetic and copies ran while one was open for 3% of the time, Pallas kernels for 10%

profile of v2, /device:TPU:6, one launch (start us, length us, event | category | flops | bytes accessed | tf_op | source)
XLA Modules:
  0.0 296.3 jit_solution(13491934876024377455)
XLA Ops:
  0.7 97.4 %shard_map.93 = (f32[64,1024]{1,0:T(8,128)}, f32[64,1024]{1,0:T(8,128)}, f32[2,64,1024]{2,1,0:T(8,128)}, f32[2,64,1024]{2,1,0:T(8,128)}, f32[2,64,1024]{2,1,0:T(8,128)}, /*index=5*/f32[256,1024]{1,0:T(8,128)}) custom-call(s32[1,8]{1,0:T(1,128)} %owner_ref.3, f32[64,8192]{1,0:T(8,128)} %g_ref.1, f32[1024,1024]{1,0:T(8,128)} %bitcast.29), custom_call_target="tpu_custom_call" | custom-call | bytes 12582912 | tf_op jit(solution)/shard_map/pallas_call | solution.py:167
  101.5 3.0 %collective-permute-start.10 = (f32[64,1024]{1,0:T(8,128)}, f32[64,1024]{1,0:T(8,128)}, u32[]{:S(2)}, u32[]{:S(2)}) collective-permute-start(f32[64,1024]{1,0:T(8,128)} %get-tuple-element.21), channel_id=1, source_target_pairs={{0,3},{1,2},{2,1},{3,0},{4,7},{5,6},{6,5},{7,4},{8,11},{9,10},{10,... | collective-permute-start | bytes 786440 | tf_op jit(solution)/shard_map/ppermute | solution.py:42
  104.6 3.5 %multiply_reduce_fusion = (f32[8192]{0:T(1024)S(1)}, f32[64,8192]{1,0:T(8,128)}, f32[64,8192]{1,0:T(8,128)}) fusion(f32[64,8192]{1,0:T(8,128)S(1)} %copy-done, f32[64,8192]{1,0:T(8,128)S(1)} %copy-done.3, f32[64,8192]{1,0:T(8,128)S(1)} %copy-done.4), kind=kLoop, calls=%fused_computation.3 | loop fusion | flops 6807552 | bytes 10518528 | tf_op jit(solution)/shard_map/reduce_sum | solution.py:512
  109.4 13.8 %collective-permute-done = f32[8]{0:T(128)S(1)} collective-permute-done((f32[8]{0:T(128)S(1)}, f32[8]{0:T(128)S(1)}, u32[]{:S(2)}, u32[]{:S(2)}) %collective-permute-start) | collective-permute-done | bytes 64 | tf_op jit(solution)/shard_map/ppermute | solution.py:51
  124.6 3.6 %collective-permute-done.1 = f32[8]{0:T(128)S(1)} collective-permute-done((f32[8]{0:T(128)S(1)}, f32[8]{0:T(128)S(1)}, u32[]{:S(2)}, u32[]{:S(2)}) %collective-permute-start.1) | collective-permute-done | bytes 64 | tf_op jit(solution)/shard_map/ppermute | solution.py:51
  128.2 3.0 %collective-permute-start.2 = (f32[8]{0:T(128)S(1)}, f32[8]{0:T(128)S(1)}, u32[]{:S(2)}, u32[]{:S(2)}) collective-permute-start(f32[8]{0:T(128)S(1)} %add.58), channel_id=1, source_target_pairs={{0,3},{1,2},{2,1},{3,0},{4,7},{5,6},{6,5},{7,4},{8,11},{9,10},{10,... | collective-permute-start | bytes 104 | tf_op jit(solution)/shard_map/ppermute | solution.py:51
  138.7 2.7 collective-permute-start.11
  143.6 4.0 %collective-permute-start.5 = (f32[8]{0:T(128)S(1)}, f32[8]{0:T(128)S(1)}, u32[]{:S(2)}, u32[]{:S(2)}) collective-permute-start(f32[8]{0:T(128)S(1)} %fusion.4), channel_id=1, source_target_pairs={{0,64},{16,80},{32,96},{48,112},{64,0},{80,16},{96,32},{112,48},{1... | collective-permute-start | bytes 104 | tf_op jit(solution)/shard_map/ppermute | solution.py:51
  150.9 3.9 %collective-permute-done.13.refs_7_ = f32[64,1024]{1,0:T(8,128)S(1)} collective-permute-done((f32[64,1024]{1,0:T(8,128)S(1)}, f32[64,1024]{1,0:T(8,128)S(1)}, u32[]{:S(2)}, u32[]{:S(2)}) %collective-permute-start.13) | collective-permute-done | bytes 262176 | tf_op jit(solution)/shard_map/ppermute | solution.py:42
  164.0 4.2 %collective-permute-done.21.refs_15_.refs_0_ = f32[64,1024]{1,0:T(8,128)S(1)} collective-permute-done((f32[64,1024]{1,0:T(8,128)S(1)}, f32[64,1024]{1,0:T(8,128)S(1)}, u32[]{:S(2)}, u32[]{:S(2)}) %collective-permute-start.21) | collective-permute-done | bytes 262176 | tf_op jit(solution)/shard_map/ppermute | solution.py:38
  174.2 22.1 %collective-permute-done.15.refs_9_ = f32[64,1024]{1,0:T(8,128)S(1)} collective-permute-done((f32[64,1024]{1,0:T(8,128)S(1)}, f32[64,1024]{1,0:T(8,128)S(1)}, u32[]{:S(2)}, u32[]{:S(2)}) %collective-permute-start.15) | collective-permute-done | bytes 262176 | tf_op jit(solution)/shard_map/ppermute | solution.py:38
  197.8 4.2 %collective-permute-done.16.refs_10_ = f32[64,1024]{1,0:T(8,128)S(1)} collective-permute-done((f32[64,1024]{1,0:T(8,128)S(1)}, f32[64,1024]{1,0:T(8,128)S(1)}, u32[]{:S(2)}, u32[]{:S(2)}) %collective-permute-start.16) | collective-permute-done | bytes 262176 | tf_op jit(solution)/shard_map/ppermute | solution.py:38
  203.4 4.2 %collective-permute-done.17.refs_11_ = f32[64,1024]{1,0:T(8,128)S(1)} collective-permute-done((f32[64,1024]{1,0:T(8,128)S(1)}, f32[64,1024]{1,0:T(8,128)S(1)}, u32[]{:S(2)}, u32[]{:S(2)}) %collective-permute-start.17) | collective-permute-done | bytes 262176 | tf_op jit(solution)/shard_map/ppermute | solution.py:38
  207.6 5.6 %collective-permute-done.20.refs_14_ = f32[64,1024]{1,0:T(8,128)S(1)} collective-permute-done((f32[64,1024]{1,0:T(8,128)S(1)}, f32[64,1024]{1,0:T(8,128)S(1)}, u32[]{:S(2)}, u32[]{:S(2)}) %collective-permute-start.20) | collective-permute-done | bytes 262176 | tf_op jit(solution)/shard_map/ppermute | solution.py:38
  214.0 9.8 %shard_map.94 = (f32[1024,1024]{1,0:T(8,128)}, bf16[1024,1024]{1,0:T(8,128)(2,1)}, bf16[1024,1024]{1,0:T(8,128)(2,1)}) custom-call(f32[64,1024]{1,0:T(8,128)} %get-tuple-element.17.refs_0_, f32[64,1024]{1,0:T(8,128)} %copy-done.11, f32[64,1024]{1,0:T(8,128)} %copy-done.13, f32[64,1024]{1,0:T(8,128)} %copy-done.12, ...), custom_call_target="tpu_custom_call" | custom-call | flops 6442450944 | bytes 16777216 | tf_op jit(solution)/shard_map/pallas_call | solution.py:310
  226.0 5.9 %shard_map.97 = (f32[8,32,1024]{2,1,0:T(8,128)}, f32[8,128]{1,0:T(8,128)}) custom-call(bf16[1024,1024]{1,0:T(8,128)(2,1)} %get-tuple-element.22.high_ref, bf16[1024,1024]{1,0:T(8,128)(2,1)} %get-tuple-element.23.low_ref, f32[256,1024]{1,0:T(8,128)} %copy-done.5, f32[136,1024]{1,0:T(8,128)} %copy-done.7, f32[8,128]{1,0:T(8,128)} %broadcast_in_dim.14.refs_2_), custom_call_target="tpu_custom_call" | custom-call | flops 1610612736 | bytes 10485760 | tf_op jit(solution)/shard_map/pallas_call | solution.py:398
  231.9 2.6 collective-permute-done.24.refs_2_
  235.4 5.8 %shard_map.98 = (f32[8,32,1024]{2,1,0:T(8,128)}, f32[8,128]{1,0:T(8,128)}) custom-call(bf16[1024,1024]{1,0:T(8,128)(2,1)} %get-tuple-element.22.high_ref, bf16[1024,1024]{1,0:T(8,128)(2,1)} %get-tuple-element.23.low_ref, f32[256,1024]{1,0:T(8,128)} %copy-done.5, f32[136,1024]{1,0:T(8,128)} %copy-done.7, f32[136,1024]{1,0:T(8,128)} %copy-done.8, ...), custom_call_target="tpu_custom_call" | custom-call | flops 1610612736 | bytes 10485760 | tf_op jit(solution)/shard_map/pallas_call | solution.py:398
  245.9 12.5 %all_to_all.15 = f32[8,8,128]{2,1,0:T(8,128)S(1)} all-to-all(f32[8,8,128]{2,1,0:T(8,128)S(1)} %broadcast_in_dim.15), channel_id=1, replica_groups={{0,3,4,7,8,11,12,15},{1,2,5,6,9,10,13,14},{16,19,20,23,24,27,28,31},{17..., dimensions={0} | all-to-all | bytes 65536 | tf_op jit(solution)/shard_map/all_to_all | solution.py:486
  258.4 5.6 %all-to-all-start.2 = ((f32[8,32,1024]{2,1,0:T(8,128)}), f32[8,32,1024]{2,1,0:T(8,128)S(1)}, u32[]{:S(2)}, u32[]{:S(2)}) async-start(f32[8,32,1024]{2,1,0:T(8,128)} %get-tuple-element.28.after_ref), calls=%async_computation.2 | async-start | bytes 2097152 | tf_op jit(solution)/shard_map/all_to_all | solution.py:486
  264.1 10.8 %all-to-all-done.2.second_ref = f32[8,32,1024]{2,1,0:T(8,128)S(1)} async-done(((f32[8,32,1024]{2,1,0:T(8,128)}), f32[8,32,1024]{2,1,0:T(8,128)S(1)}, u32[]{:S(2)}, u32[]{:S(2)}) %all-to-all-start.2) | async-done | bytes 1048608 | tf_op jit(solution)/shard_map/all_to_all | solution.py:486
  274.9 5.2 %all-to-all-start.1 = ((f32[8,32,1024]{2,1,0:T(8,128)}), f32[8,32,1024]{2,1,0:T(8,128)S(1)}, u32[]{:S(2)}, u32[]{:S(2)}) async-start(f32[8,32,1024]{2,1,0:T(8,128)} %get-tuple-element.27), calls=%async_computation.1 | async-start | bytes 2097152 | tf_op jit(solution)/shard_map/all_to_all | solution.py:486
  280.1 10.8 %shard_map.100 = f32[1024,1024]{1,0:T(8,128)} custom-call(f32[1024,1024]{1,0:T(8,128)} %get-tuple-element.29.g_ref, f32[1024,1024]{1,0:T(8,128)} %bitcast.33, f32[8,32,1024]{2,1,0:T(8,128)} %get-tuple-element.28.after_ref), custom_call_target="tpu_custom_call" | custom-call | flops 4294967296 | bytes 12582912 | tf_op jit(solution)/shard_map/pallas_call | solution.py:446
  293.3 3.0 %shard_map.99 = f32[64,8192]{1,0:T(8,128)} custom-call(s32[1,8]{1,0:T(1,128)} %owner_ref.3, f32[8]{0:T(128)} %bitcast_multiply_fusion.scale_ref, f32[8,32,1024]{2,1,0:T(8,128)} %copy-done.2, f32[8,32,1024]{2,1,0:T(8,128)} %copy-done.1), custom_call_target="tpu_custom_call" | custom-call | flops 262144 | bytes 4194304 | tf_op jit(solution)/shard_map/pallas_call | solution.py:474
  (118 shorter events, 48.1 us)
Async XLA Ops:
  98.0 38.6 %collective-permute-start.7 = (f32[2,64,1024]{2,1,0:T(8,128)}, f32[2,64,1024]{2,1,0:T(8,128)S(1)}, u32[]{:S(2)}, u32[]{:S(2)}) collective-permute-start(f32[2,64,1024]{2,1,0:T(8,128)} %get-tuple-element.18), channel_id=1, source_target_pairs={{0,4},{1,5},{2,6},{3,7},{4,8},{5,9},{6,10},{7,11},{8,12},{9,13},{1... | collective-permute-start | bytes 1572872 | tf_op jit(solution)/shard_map/ppermute | solution.py:46
  98.5 40.2 %collective-permute-start.9 = (f32[2,64,1024]{2,1,0:T(8,128)}, f32[2,64,1024]{2,1,0:T(8,128)S(1)}, u32[]{:S(2)}, u32[]{:S(2)}) collective-permute-start(f32[2,64,1024]{2,1,0:T(8,128)} %get-tuple-element.20), channel_id=1, source_target_pairs={{0,12},{1,13},{2,14},{3,15},{4,0},{5,1},{6,2},{7,3},{8,4},{9,5},{1... | collective-permute-start | bytes 1572872 | tf_op jit(solution)/shard_map/ppermute | solution.py:46
  100.1 47.4 %collective-permute-start.8 = (f32[2,64,1024]{2,1,0:T(8,128)}, f32[2,64,1024]{2,1,0:T(8,128)S(1)}, u32[]{:S(2)}, u32[]{:S(2)}) collective-permute-start(f32[2,64,1024]{2,1,0:T(8,128)} %get-tuple-element.19), channel_id=1, source_target_pairs={{0,8},{1,9},{2,10},{3,11},{4,12},{5,13},{6,14},{7,15},{8,0},{9,1},... | collective-permute-start | bytes 1572872 | tf_op jit(solution)/shard_map/ppermute | solution.py:46
  101.5 42.0 %collective-permute-start.10 = (f32[64,1024]{1,0:T(8,128)}, f32[64,1024]{1,0:T(8,128)}, u32[]{:S(2)}, u32[]{:S(2)}) collective-permute-start(f32[64,1024]{1,0:T(8,128)} %get-tuple-element.21), channel_id=1, source_target_pairs={{0,3},{1,2},{2,1},{3,0},{4,7},{5,6},{6,5},{7,4},{8,11},{9,10},{10,... | collective-permute-start | bytes 786440 | tf_op jit(solution)/shard_map/ppermute | solution.py:42
  108.2 15.0 %collective-permute-start = (f32[8]{0:T(128)S(1)}, f32[8]{0:T(128)S(1)}, u32[]{:S(2)}, u32[]{:S(2)}) collective-permute-start(f32[8]{0:T(128)S(1)} %reduce_sum.27), channel_id=1, source_target_pairs={{0,4},{1,5},{2,6},{3,7},{4,0},{5,1},{6,2},{7,3},{8,12},{9,13},{10,... | collective-permute-start | bytes 104 | tf_op jit(solution)/shard_map/ppermute | solution.py:51
  123.2 5.0 %collective-permute-start.1 = (f32[8]{0:T(128)S(1)}, f32[8]{0:T(128)S(1)}, u32[]{:S(2)}, u32[]{:S(2)}) collective-permute-start(f32[8]{0:T(128)S(1)} %add.57), channel_id=1, source_target_pairs={{0,8},{1,9},{2,10},{3,11},{4,12},{5,13},{6,14},{7,15},{8,0},{9,1},... | collective-permute-start | bytes 104 | tf_op jit(solution)/shard_map/ppermute | solution.py:51
  135.6 20.1 %collective-permute-start.14 = (f32[64,1024]{1,0:T(8,128)S(1)}, f32[64,1024]{1,0:T(8,128)S(1)}, u32[]{:S(2)}, u32[]{:S(2)}) collective-permute-start(f32[64,1024]{1,0:T(8,128)S(1)} %copy-done.17), channel_id=1, source_target_pairs={{0,1},{1,0},{2,3},{3,2},{4,5},{5,4},{6,7},{7,6},{8,9},{9,8},{10,11... | collective-permute-start | bytes 786440 | tf_op jit(solution)/shard_map/ppermute | solution.py:38
  138.7 12.0 %collective-permute-start.11 = (f32[64,1024]{1,0:T(8,128)S(1)}, f32[64,1024]{1,0:T(8,128)S(1)}, u32[]{:S(2)}, u32[]{:S(2)}) collective-permute-start(f32[64,1024]{1,0:T(8,128)S(1)} %get-tuple-element.37), channel_id=1, source_target_pairs={{0,3},{1,2},{2,1},{3,0},{4,7},{5,6},{6,5},{7,4},{8,11},{9,10},{10,... | collective-permute-start | bytes 786440 | tf_op jit(solution)/shard_map/ppermute | solution.py:42
  141.5 13.3 %collective-permute-start.13 = (f32[64,1024]{1,0:T(8,128)S(1)}, f32[64,1024]{1,0:T(8,128)S(1)}, u32[]{:S(2)}, u32[]{:S(2)}) collective-permute-start(f32[64,1024]{1,0:T(8,128)S(1)} %get-tuple-element.33), channel_id=1, source_target_pairs={{0,3},{1,2},{2,1},{3,0},{4,7},{5,6},{6,5},{7,4},{8,11},{9,10},{10,... | collective-permute-start | bytes 786440 | tf_op jit(solution)/shard_map/ppermute | solution.py:42
  143.6 5.5 %collective-permute-start.5 = (f32[8]{0:T(128)S(1)}, f32[8]{0:T(128)S(1)}, u32[]{:S(2)}, u32[]{:S(2)}) collective-permute-start(f32[8]{0:T(128)S(1)} %fusion.4), channel_id=1, source_target_pairs={{0,64},{16,80},{32,96},{48,112},{64,0},{80,16},{96,32},{112,48},{1... | collective-permute-start | bytes 104 | tf_op jit(solution)/shard_map/ppermute | solution.py:51
  147.6 9.5 %collective-permute-start.18 = (f32[64,1024]{1,0:T(8,128)}, f32[64,1024]{1,0:T(8,128)S(1)}, u32[]{:S(2)}, u32[]{:S(2)}) collective-permute-start(f32[64,1024]{1,0:T(8,128)} %collective-permute-done.10.refs_4_), channel_id=1, source_target_pairs={{0,1},{1,0},{2,3},{3,2},{4,5},{5,4},{6,7},{7,6},{8,9},{9,8},{10,11... | collective-permute-start | bytes 786440 | tf_op jit(solution)/shard_map/ppermute | solution.py:38
  149.1 10.0 %collective-permute-start.12 = (f32[64,1024]{1,0:T(8,128)S(1)}, f32[64,1024]{1,0:T(8,128)S(1)}, u32[]{:S(2)}, u32[]{:S(2)}) collective-permute-start(f32[64,1024]{1,0:T(8,128)S(1)} %get-tuple-element.35), channel_id=1, source_target_pairs={{0,3},{1,2},{2,1},{3,0},{4,7},{5,6},{6,5},{7,4},{8,11},{9,10},{10,... | collective-permute-start | bytes 786440 | tf_op jit(solution)/shard_map/ppermute | solution.py:42
  150.7 11.9 %collective-permute-start.19 = (f32[64,1024]{1,0:T(8,128)S(1)}, f32[64,1024]{1,0:T(8,128)S(1)}, u32[]{:S(2)}, u32[]{:S(2)}) collective-permute-start(f32[64,1024]{1,0:T(8,128)S(1)} %collective-permute-done.11.refs_5_), channel_id=1, source_target_pairs={{0,1},{1,0},{2,3},{3,2},{4,5},{5,4},{6,7},{7,6},{8,9},{9,8},{10,11... | collective-permute-start | bytes 786440 | tf_op jit(solution)/shard_map/ppermute | solution.py:38
  154.8 13.4 %collective-permute-start.21 = (f32[64,1024]{1,0:T(8,128)S(1)}, f32[64,1024]{1,0:T(8,128)S(1)}, u32[]{:S(2)}, u32[]{:S(2)}) collective-permute-start(f32[64,1024]{1,0:T(8,128)S(1)} %collective-permute-done.13.refs_7_), channel_id=1, source_target_pairs={{0,1},{1,0},{2,3},{3,2},{4,5},{5,4},{6,7},{7,6},{8,9},{9,8},{10,11... | collective-permute-start | bytes 786440 | tf_op jit(solution)/shard_map/ppermute | solution.py:38
  155.6 68.2 %collective-permute-start.22 = (f32[256,1024]{1,0:T(8,128)S(1)}, f32[256,1024]{1,0:T(8,128)S(1)}, u32[]{:S(2)}, u32[]{:S(2)}) collective-permute-start(f32[256,1024]{1,0:T(8,128)S(1)} %copy-done.16), channel_id=1, source_target_pairs={{0,1},{1,0},{2,3},{3,2},{4,5},{5,4},{6,7},{7,6},{8,9},{9,8},{10,11... | collective-permute-start | bytes 3145736 | tf_op jit(solution)/shard_map/ppermute | solution.py:38
  157.0 39.3 %collective-permute-start.15 = (f32[64,1024]{1,0:T(8,128)S(1)}, f32[64,1024]{1,0:T(8,128)S(1)}, u32[]{:S(2)}, u32[]{:S(2)}) collective-permute-start(f32[64,1024]{1,0:T(8,128)S(1)} %get-tuple-element.38.refs_1_), channel_id=1, source_target_pairs={{0,1},{1,0},{2,3},{3,2},{4,5},{5,4},{6,7},{7,6},{8,9},{9,8},{10,11... | collective-permute-start | bytes 786440 | tf_op jit(solution)/shard_map/ppermute | solution.py:38
  159.1 42.9 %collective-permute-start.16 = (f32[64,1024]{1,0:T(8,128)S(1)}, f32[64,1024]{1,0:T(8,128)S(1)}, u32[]{:S(2)}, u32[]{:S(2)}) collective-permute-start(f32[64,1024]{1,0:T(8,128)S(1)} %get-tuple-element.36.refs_2_), channel_id=1, source_target_pairs={{0,1},{1,0},{2,3},{3,2},{4,5},{5,4},{6,7},{7,6},{8,9},{9,8},{10,11... | collective-permute-start | bytes 786440 | tf_op jit(solution)/shard_map/ppermute | solution.py:38
  162.6 44.9 %collective-permute-start.17 = (f32[64,1024]{1,0:T(8,128)S(1)}, f32[64,1024]{1,0:T(8,128)S(1)}, u32[]{:S(2)}, u32[]{:S(2)}) collective-permute-start(f32[64,1024]{1,0:T(8,128)S(1)} %get-tuple-element.34.refs_3_), channel_id=1, source_target_pairs={{0,1},{1,0},{2,3},{3,2},{4,5},{5,4},{6,7},{7,6},{8,9},{9,8},{10,11... | collective-permute-start | bytes 786440 | tf_op jit(solution)/shard_map/ppermute | solution.py:38
  168.2 44.9 %collective-permute-start.20 = (f32[64,1024]{1,0:T(8,128)S(1)}, f32[64,1024]{1,0:T(8,128)S(1)}, u32[]{:S(2)}, u32[]{:S(2)}) collective-permute-start(f32[64,1024]{1,0:T(8,128)S(1)} %collective-permute-done.12.refs_6_), channel_id=1, source_target_pairs={{0,1},{1,0},{2,3},{3,2},{4,5},{5,4},{6,7},{7,6},{8,9},{9,8},{10,11... | collective-permute-start | bytes 786440 | tf_op jit(solution)/shard_map/ppermute | solution.py:38
  196.3 28.8 %collective-permute-start.23 = (f32[136,1024]{1,0:T(8,128)}, f32[136,1024]{1,0:T(8,128)S(1)}, u32[]{:S(2)}, u32[]{:S(2)}) collective-permute-start(f32[136,1024]{1,0:T(8,128)} %shard_map.95), channel_id=1, source_target_pairs={{0,1},{1,0},{2,3},{3,2},{4,5},{5,4},{6,7},{7,6},{8,9},{9,8},{10,11... | collective-permute-start | bytes 1671176 | tf_op jit(solution)/shard_map/ppermute | solution.py:38
  202.0 32.6 %collective-permute-start.24 = (f32[136,1024]{1,0:T(8,128)S(1)}, f32[136,1024]{1,0:T(8,128)S(1)}, u32[]{:S(2)}, u32[]{:S(2)}) collective-permute-start(f32[136,1024]{1,0:T(8,128)S(1)} %copy-done.6), channel_id=1, source_target_pairs={{0,1},{1,0},{2,3},{3,2},{4,5},{5,4},{6,7},{7,6},{8,9},{9,8},{10,11... | collective-permute-start | bytes 1671176 | tf_op jit(solution)/shard_map/ppermute | solution.py:38
  258.4 16.4 %all-to-all-start.2 = ((f32[8,32,1024]{2,1,0:T(8,128)}), f32[8,32,1024]{2,1,0:T(8,128)S(1)}, u32[]{:S(2)}, u32[]{:S(2)}) async-start(f32[8,32,1024]{2,1,0:T(8,128)} %get-tuple-element.28.after_ref), calls=%async_computation.2 | async-start | bytes 2097152 | tf_op jit(solution)/shard_map/all_to_all | solution.py:486
  264.0 16.1 %collective-permute-start.6 = (f32[2,8]{1,0:T(2,128)S(1)}, f32[2,8]{1,0:T(2,128)S(1)}, u32[]{:S(2)}, u32[]{:S(2)}) collective-permute-start(f32[2,8]{1,0:T(2,128)S(1)} %copy-done.14), channel_id=1, source_target_pairs={{0,1},{1,0},{2,3},{3,2},{4,5},{5,4},{6,7},{7,6},{8,9},{9,8},{10,11... | collective-permute-start | bytes 200 | tf_op jit(solution)/shard_map/ppermute | solution.py:51
  274.9 17.4 %all-to-all-start.1 = ((f32[8,32,1024]{2,1,0:T(8,128)}), f32[8,32,1024]{2,1,0:T(8,128)S(1)}, u32[]{:S(2)}, u32[]{:S(2)}) async-start(f32[8,32,1024]{2,1,0:T(8,128)} %get-tuple-element.27), calls=%async_computation.1 | async-start | bytes 2097152 | tf_op jit(solution)/shard_map/all_to_all | solution.py:486
  (31 other events, 967.5 us)

commit v3 on v2

v3 whole, which is shorter than its diff:
```python
import math

import jax
import jax.numpy as jnp
from jax import lax
from jax.experimental import pallas as pl
from jax.experimental.pallas import tpu as pltpu
from jax.sharding import PartitionSpec as P

BETA_STAT = 0.95
BETA_ONE = 0.9
BETA_TWO = 0.999
BIAS_ONE = 1.0 - 0.9**10
BIAS_TWO = 1.0 - 0.999**10
ADAM_EPS = 1e-08
CLIP_RMS = 0.25
SIDE = 4


def route(move):
    pairs = []
    for src in range(SIDE * SIDE):
        x, y = move(src // SIDE, src % SIDE)
        pairs.append((src, (x % SIDE) * SIDE + y % SIDE))
    return pairs


NEAR = route(lambda x, y: (x, y ^ 1))
FAR = route(lambda x, y: (x, 3 - y))
GROUPS = [
    [SIDE * x + y for x in range(SIDE) for y in (0, 3)],
    [SIDE * x + y for x in range(SIDE) for y in (1, 2)],
]


def near(v):
    return lax.ppermute(v, "dp", NEAR)


def far(v):
    return lax.ppermute(v, "dp", FAR)


def along_x(v, shift):
    return lax.ppermute(v, "dp", route(lambda x, y: (x + shift, y)))


def tie(v, *after):
    return lax.optimization_barrier((v, *after))[0]


def swap(v, axis, bit):
    count = lax.axis_size(axis)
    return lax.ppermute(v, axis, [(i, i ^ bit) for i in range(count)])

HBM = pl.BlockSpec(memory_space=pltpu.HBM)
VMEM = pl.BlockSpec(memory_space=pltpu.VMEM)
SMEM = pl.BlockSpec(memory_space=pltpu.SMEM)


def call(body, out, in_specs, out_specs, scratch, flops, moved, vmem=16):
    return pl.pallas_call(
        body,
        out_shape=out,
        in_specs=in_specs,
        out_specs=out_specs,
        scratch_shapes=scratch,
        compiler_params=pltpu.CompilerParams(vmem_limit_bytes=vmem * 2**20),
        cost_estimate=pl.CostEstimate(flops=flops, bytes_accessed=moved, transcendentals=0),
    )


def f32(*shape):
    return jax.ShapeDtypeStruct(shape, jnp.float32)


def spot():
    place = lax.axis_index("dp")
    x, y = lax.shift_right_logical(place, 2), lax.bitwise_and(place, 3)
    is_left = lax.bitwise_and(y, 1) == 0
    outer = jnp.logical_or(y == 0, y == 3)
    return x, y, is_left, outer


def rows_of(k, x, y, rows):
    return (lax.bitwise_and(x + k // 2, 3) * SIDE + (3 - y if k % 2 else y)) * rows


def run(copies):
    for copy in copies:
        copy.start()
    return copies


def finish(copies):
    for copy in copies:
        copy.wait()


def split(v):
    high = v.astype(jnp.bfloat16)
    return high, (v - high.astype(jnp.float32)).astype(jnp.bfloat16)


def mul(a, b):
    return jnp.dot(a, b, preferred_element_type=jnp.float32)


def mul_split(a_high, a_low, b_high, b_low):
    return mul(a_high, b_high) + (mul(a_high, b_low) + mul(a_low, b_high))


def unit_copies(root_ref, unit, rows, x, y, is_left, to_ref, sems, base):
    few = rows // 4
    copies = []
    for k in range(2 * SIDE):
        row = rows_of(k, x, lax.bitwise_xor(y, 1), rows) + unit * few
        copies.append(
            pltpu.make_async_copy(
                root_ref.at[pl.ds(pl.multiple_of(row, few), few), :],
                to_ref.at[pl.ds(k * few, few), :],
                sems.at[base + k],
            )
        )
    return copies


def cross_copies(root_ref, unit, to_ref, sems, base):
    order = root_ref.shape[0]
    half, part = order // 2, order // 8
    return [
        pltpu.make_async_copy(
            root_ref.at[pl.ds((2 * unit + h) * part, part), pl.ds(half, half)],
            to_ref.at[:, pl.ds(h * half, half)],
            sems.at[base + h],
        )
        for h in range(2)
    ]


def column_of(owner_ref, pos, count):
    col = jnp.int32(0)
    for c in range(count):
        col = col + jnp.where(owner_ref[0, c] == pos, c, 0)
    return col


def position(x, y, d, j):
    return 2 * lax.bitwise_and(x + d, 3) + lax.bitwise_xor(lax.shift_right_logical(y, 1), j)


def cut(gradient, root, owner_table):
    rows, width = gradient.shape
    order = root.shape[0]
    count = width // order
    part = order // 8

    def body(owner_ref, g_ref, root_ref, lead_ref, oth_ref, x1_ref, x2_ref, x3_ref, sems):
        x, y, is_left, outer = spot()
        outs = [(lead_ref.at[pl.ds(part, rows), :], oth_ref)]
        outs += [(r.at[pl.ds(0, rows), :], r.at[pl.ds(rows, rows), :]) for r in (x1_ref, x2_ref, x3_ref)]
        copies = []
        for d in range(SIDE):
            for j in range(2):
                col = column_of(owner_ref, position(x, y, d, j), count)
                at = pl.ds(pl.multiple_of(col * order, order), order)
                copies.append(pltpu.make_async_copy(g_ref.at[:, at], outs[d][j], sems.at[2 * d + j]))
        run(copies)
        chunk_ref = lead_ref.at[pl.ds(0, part), :]

        @pl.when(is_left)
        def _():
            finish(run(unit_copies(root_ref, 0, rows, x, y, is_left, chunk_ref, sems, 2 * SIDE)))

        @pl.when(jnp.logical_not(is_left))
        def _():
            finish(run(cross_copies(root_ref, 0, chunk_ref, sems, 2 * SIDE)))

        finish(copies)

    return call(
        body,
        [f32(part + rows, order), f32(rows, order)] + [f32(2 * rows, order)] * 3,
        [SMEM, HBM, HBM],
        [VMEM] * 5,
        [pltpu.SemaphoreType.DMA((4 * SIDE,))],
        0,
        8 * rows * width,
        60,
    )(owner_table, gradient, root)


def adam(gradient, moment, second, order):
    rows, width = gradient.shape
    count = width // order

    def body(g_ref, m_ref, s_ref, m_out, s_out, sums_ref):
        for c in range(count):
            cols = slice(c * order, (c + 1) * order)

            def step(i, total):
                at = pl.ds(pl.multiple_of(i * 8, 8), 8)
                g = g_ref[at, cols]
                new_m = BETA_ONE * m_ref[at, cols] + (1.0 - BETA_ONE) * g
                new_s = BETA_TWO * s_ref[at, cols] + (1.0 - BETA_TWO) * g * g
                m_out[at, cols] = new_m
                s_out[at, cols] = new_s
                a = new_m / BIAS_ONE / (jnp.sqrt(new_s / BIAS_TWO) + ADAM_EPS)
                return total + a * a

            total = lax.fori_loop(0, rows // 8, step, jnp.zeros((8, order), jnp.float32))
            sums_ref[c : c + 1, :] = jnp.sum(total, axis=0, keepdims=True)

    return call(
        body,
        [f32(rows, width)] * 2 + [f32(8, order)],
        [VMEM] * 3,
        [VMEM] * 3,
        [],
        0,
        24 * rows * width,
    )(gradient, moment, second)


def pack(root, rows, units):
    order = root.shape[0]
    half, quarter, part = order // 2, order // 4, order // 8
    fold = units[-1]
    last = (len(units) - 1) * part

    def body(root_ref, out_ref, buf, sems):
        x, y, is_left, outer = spot()
        out_ref[last + part :, :] = jnp.zeros((8, order), jnp.float32)

        @pl.when(is_left)
        def _():
            copies = []
            for i, unit in enumerate(units):
                to_ref = out_ref.at[pl.ds(i * part, part), :]
                copies += unit_copies(root_ref, unit, rows, x, y, is_left, to_ref, sems, 2 * SIDE * i)
            finish(run(copies))

        @pl.when(jnp.logical_not(is_left))
        def _():
            at = pl.ds((fold - 2) * half, half)
            copies = [pltpu.make_async_copy(root_ref.at[at, at], buf, sems.at[0])]
            for i, unit in enumerate(units[:-1]):
                to_ref = out_ref.at[pl.ds(i * part, part), :]
                copies += cross_copies(root_ref, unit, to_ref, sems, 2 * i + 1)
            finish(run(copies))
            row = lax.broadcasted_iota(jnp.int32, (quarter, quarter), 0)
            col = lax.broadcasted_iota(jnp.int32, (quarter, quarter), 1)
            low = buf[quarter:, quarter:]
            both = jnp.where(row <= col, buf[:quarter, :quarter], low)
            at = slice(last, last + part)
            for h in range(2):
                out_ref[at, h * half : h * half + quarter] = buf[h * part : (h + 1) * part, quarter:]
                out_ref[at, h * half + quarter : (h + 1) * half] = both[h * part : (h + 1) * part]
            out_ref[last + part : last + part + 1, :quarter] = jnp.sum(
                jnp.where(row == col, low, 0.0), axis=0, keepdims=True
            )

    return call(
        body,
        f32(last + part + 8, order),
        [HBM],
        VMEM,
        [pltpu.VMEM((half, half), jnp.float32), pltpu.SemaphoreType.DMA((2 * SIDE * len(units),))],
        0,
        8 * len(units) * part * order,
    )(root)


def in_vmem(*shape):
    return pltpu.VMEM(shape, jnp.bfloat16)


def cut_two(src, high, low, tiles):
    def step(i, carry):
        at = pl.ds(pl.multiple_of(i * 64, 64), 64)
        high[at, :], low[at, :] = split(src[at, :])
        return carry

    lax.fori_loop(0, tiles, step, 0)


def split_root(root, rows):
    order = root.shape[0]

    def body(root_ref, high_ref, low_ref, buf, sems):
        x, y, is_left, outer = spot()

        @pl.when(is_left)
        def _():
            copies = []
            for k in range(2 * SIDE):
                row = rows_of(k, x, y, rows)
                copies.append(
                    pltpu.make_async_copy(
                        root_ref.at[pl.ds(pl.multiple_of(row, rows), rows), :],
                        buf.at[pl.ds(k * rows, rows), :],
                        sems.at[k],
                    )
                )
            finish(run(copies))
            cut_two(buf, high_ref, low_ref, order // 128)

        @pl.when(jnp.logical_not(is_left))
        def _():
            finish(run([pltpu.make_async_copy(root_ref, buf, sems.at[0])]))
            cut_two(buf, high_ref, low_ref, order // 64)

    return call(
        body,
        [in_vmem(order, order)] * 2,
        [HBM],
        [VMEM, VMEM],
        [pltpu.VMEM((order, order), jnp.float32), pltpu.SemaphoreType.DMA((2 * SIDE,))],
        0,
        8 * order * order,
    )(root)


def first_product(pieces, rows, r_high, r_low):
    order = r_high.shape[0]
    half, tile = order // 2, order // 4
    count = len(pieces)

    def body(*refs):
        piece_refs, (rh_ref, rl_ref) = refs[:count], refs[count : count + 2]
        gh_ref, gl_ref, high_ref, low_ref, buf, sems = refs[count + 2 :]
        x, y, is_left, outer = spot()
        from_y = (y, 3 - y, lax.bitwise_xor(y, 1), 3 - lax.bitwise_xor(y, 1))
        copies = []
        for k in range(count):
            row = (lax.bitwise_and(x - k % SIDE, 3) * SIDE + from_y[k // SIDE]) * rows
            copies.append(
                pltpu.make_async_copy(
                    piece_refs[k].at[pl.ds(pieces[k][1], rows), :],
                    buf.at[pl.ds(pl.multiple_of(row, rows), rows), :],
                    sems.at[k],
                )
            )
        finish(run(copies))
        cut_two(buf, gh_ref, gl_ref, order // 64)

        def product(a_high, a_low, b_high, b_low, tiles):
            def step(i, carry):
                at = pl.ds(pl.multiple_of(i * tile, tile), tile)
                for n in range(2):
                    cols = slice(n * half, (n + 1) * half)
                    acc = mul_split(a_high[at, :], a_low[at, :], b_high[:, cols], b_low[:, cols])
                    high_ref[at, cols], low_ref[at, cols] = split(acc)
                return carry

            lax.fori_loop(0, tiles, step, 0)

        @pl.when(is_left)
        def _():
            product(rh_ref, rl_ref, gh_ref, gl_ref, 2)

        @pl.when(jnp.logical_not(is_left))
        def _():
            product(gh_ref, gl_ref, rh_ref, rl_ref, 4)

    return call(
        body,
        [in_vmem(order, order)] * 4,
        [HBM] * count + [VMEM] * 2,
        [VMEM] * 4,
        [pltpu.VMEM((order, order), jnp.float32), pltpu.SemaphoreType.DMA((count,))],
        0,
        order * order,
    )(*(piece for piece, _ in pieces), r_high, r_low)


def unfold(c_ref, first, b_high, b_low, base):
    half = c_ref.shape[1] // 2
    quarter = half // 2
    mid = quarter // 2
    row = lax.broadcasted_iota(jnp.int32, (quarter, quarter), 0)
    col = lax.broadcasted_iota(jnp.int32, (quarter, quarter), 1)
    at = slice(first, first + mid)
    cross = jnp.concatenate([c_ref[at, :quarter], c_ref[at, half : half + quarter]], axis=0)
    both = jnp.concatenate([c_ref[at, quarter:half], c_ref[at, half + quarter :]], axis=0)
    diag = c_ref[first + mid : first + mid + 1, :quarter]
    turned = both.T
    top = jnp.where(row <= col, both, turned)
    low = jnp.where(row > col, both, jnp.where(row == col, diag, turned))
    for r, left_mat, right_mat in ((0, top, cross), (1, cross.T, low)):
        at = slice(base + r * quarter, base + (r + 1) * quarter)
        b_high[at, :quarter], b_low[at, :quarter] = split(left_mat)
        b_high[at, quarter:], b_low[at, quarter:] = split(right_mat)


def second_product(which, t_high, t_low, chunks, squares):
    order = t_high.shape[0]
    half, quarter, eighth = order // 2, order // 4, order // 8
    dests = 2 * SIDE
    part = quarter // dests
    few = part // 2
    count = len(chunks)

    def body(high_ref, low_ref, *refs):
        chunk_refs, sq_ref = refs[:count], refs[count]
        whole, sq_out, b_high, b_low = refs[count + 1 :]
        x, y, is_left, outer = spot()
        outs = []
        for k in range(dests):
            to_y = 3 - y if k % 2 else y
            outs.append(whole.at[2 * lax.bitwise_and(x + k // 2, 3) + lax.shift_right_logical(to_y, 1)])
        units = [(chunk_refs[0], 0), (chunk_refs[1], 0), (chunk_refs[1], eighth), (chunk_refs[-1], 0)]

        @pl.when(is_left)
        def _():
            for q in range(4):
                c_ref, first = units[q // 2]
                at = slice(q * eighth, (q + 1) * eighth)
                mat = c_ref[first : first + eighth, (q % 2) * half : (q % 2 + 1) * half]
                if which == 0:
                    b_high[half:, at], b_low[half:, at] = split(mat.T)
                else:
                    b_high[at, :], b_low[at, :] = split(mat)
            unfold(*units[2 + which], b_high, b_low, half * which)
            total = jnp.float32(0.0)
            for m in range(2):
                at = slice(m * quarter, (m + 1) * quarter)
                acc = mul_split(high_ref[at, :], low_ref[at, :], b_high[...], b_low[...])
                total = total + jnp.sum(acc * acc)
                for k in range(SIDE):
                    for h in range(2):
                        first = (2 * k + h) * part
                        for q in range(SIDE):
                            at = slice((h * SIDE + q) * part, (h * SIDE + q + 1) * part)
                            lanes = slice(q * 128, (q + 1) * 128)
                            outs[m * SIDE + k][at, :] = acc[first : first + part, lanes]
            sq_out[...] = sq_ref[...] + total

        @pl.when(jnp.logical_not(is_left))
        def _():
            mats = []
            for c_ref, first in units[2 * which : 2 * which + 2]:
                mats.append(c_ref[first : first + eighth, :])
            a_high, a_low = split(jnp.concatenate(mats, axis=0))
            total = jnp.float32(0.0)
            for n in range(2):
                cols = slice(n * half, (n + 1) * half)
                acc = mul_split(a_high, a_low, high_ref[:, cols], low_ref[:, cols])
                total = total + jnp.sum(acc * acc)
                for k in range(dests):
                    for q in range(SIDE):
                        first = (n * SIDE + q) * part
                        lanes = slice(q * 128, (q + 1) * 128)
                        outs[k][first : first + few, :] = acc[k * few : (k + 1) * few, lanes]
                        outs[k][first + few : first + part, :] = acc[
                            eighth + k * few : eighth + (k + 1) * few, lanes
                        ]
            sq_out[...] = sq_ref[...] + total

        if which == 1:
            for k in range(dests):
                whole[k, 8 * part :, :] = sq_out[...]

    short = pltpu.VMEM((order, half), jnp.bfloat16)
    return call(
        body,
        [f32(dests, 8 * part + 8 * which, 128), f32(8, 128)],
        [VMEM] * (3 + count),
        [VMEM] * 2,
        [short, short],
        0,
        140 * order * order * which,
    )(t_high, t_low, *chunks, squares)


def update_statistics(g_high, g_low, stat):
    order = g_high.shape[0]
    tile = order // 4
    tiles = order // tile

    def body(gh_ref, gl_ref, s_ref, out_ref, zero_ref, high, low):
        x, y, is_left, outer = spot()
        zero_ref[...] = jnp.zeros((8, 128), jnp.float32)

        @pl.when(is_left)
        def _():
            high[...] = gh_ref[...]
            low[...] = gl_ref[...]

        @pl.when(jnp.logical_not(is_left))
        def _():
            for i in range(tiles):
                for j in range(tiles):
                    at, cols = slice(i * tile, (i + 1) * tile), slice(j * tile, (j + 1) * tile)
                    high[at, cols] = gh_ref[cols, at].T
                    low[at, cols] = gl_ref[cols, at].T

        def outer_mul(a, b):
            return lax.dot_general(a, b, (((1,), (1,)), ((), ())), preferred_element_type=jnp.float32)

        for i in range(tiles):
            at = slice(i * tile, (i + 1) * tile)
            for j in range(i, tiles):
                to = slice(j * tile, (j + 1) * tile)
                acc = outer_mul(high[at, :], high[to, :]) + (
                    outer_mul(high[at, :], low[to, :]) + outer_mul(low[at, :], high[to, :])
                )
                acc = (1.0 - BETA_STAT) * acc
                out_ref[at, to] = BETA_STAT * s_ref[at, to] + acc
                if i != j:
                    out_ref[to, at] = BETA_STAT * s_ref[to, at] + acc.T

    short = pltpu.VMEM((order, order), jnp.bfloat16)
    return call(
        body,
        [f32(order, order), f32(8, 128)],
        [VMEM, VMEM, VMEM],
        [VMEM, VMEM],
        [short, short],
        0,
        order * order,
        24,
    )(g_high, g_low, stat)


def place_columns(first, second, ends, sums, totals, owner_table, largest):
    count = first.shape[0]
    part = first.shape[1] // 8
    order = 8 * first.shape[2]
    end = 8 * part

    def body(owner_ref, first_ref, second_ref, ends_ref, sums_ref, totals_ref, out_ref, scratch):
        x, y, is_left, outer = spot()
        total = jnp.sum(jnp.sum(totals_ref[...], axis=0, keepdims=True), axis=1, keepdims=True)
        clip = jnp.minimum(1.0, largest / jnp.sqrt(total + 1e-06))
        scratch[...] = jnp.broadcast_to(jnp.sum(sums_ref[...], axis=1, keepdims=True), (count, 128))
        for k in range(count):
            from_y = 3 - y if k % 2 else y
            p = 2 * lax.bitwise_and(x - k // 2, 3) + lax.shift_right_logical(from_y, 1)
            from_left = lax.bitwise_and(from_y, 1) == 0
            col = column_of(owner_ref, p, count)
            squares = second_ref[p, end : end + 1, :] + ends_ref[p, :1, :]
            scale = jnp.sqrt(scratch[pl.ds(col, 1), :] / (squares + 1e-06)) * clip
            for j in range(8):
                cols = pl.ds(pl.multiple_of(col * order + j * 128, 128), 128)
                at = slice(j * part, (j + 1) * part)
                back = (j + 4) % 8
                across = slice(back * part, (back + 1) * part)
                if j < 4:
                    out_ref[:part, cols] = first_ref[p, at, :] * scale
                    other = jnp.where(from_left, first_ref[p, across, :], second_ref[p, at, :])
                    out_ref[part:, cols] = other * scale
                else:
                    other = jnp.where(from_left, second_ref[p, across, :], first_ref[p, at, :])
                    out_ref[:part, cols] = other * scale
                    out_ref[part:, cols] = second_ref[p, at, :] * scale

    return call(
        body,
        f32(2 * part, count * order),
        [SMEM] + [VMEM] * 5,
        VMEM,
        [pltpu.VMEM((count, 128), jnp.float32)],
        0,
        16 * count * part * order,
    )(owner_table, first, second, ends, sums, totals)


def sent_back(parts):
    return lax.all_to_all(parts, "dp", 0, 0, axis_index_groups=GROUPS, tiled=True)


def local(gradient, moment, second, statistics, inv_roots, owner_table):
    rows_dev, width = gradient.shape
    order = statistics.shape[1]
    root = inv_roots[0]

    lead, oth, x1, x2, x3 = cut(gradient, root, owner_table)
    lead_got = near(lead)
    far_y = {0: far(oth)}
    new_moment, new_second, own_sums = adam(gradient, moment, second, order)
    got_x = {1: along_x(x1, 1), 3: along_x(x3, 3)}
    got_x[2] = along_x(tie(x2, far_y[0], own_sums), 2)
    own_y = {d: got_x[d][:rows_dev] for d in (1, 2, 3)}
    oth_y = {d: got_x[d][rows_dev:] for d in (1, 2, 3)}
    own_sums = tie(own_sums, got_x[2])
    sums = own_sums
    for d in (1, 2, 3):
        sums = sums + along_x(own_sums, d)
    far_y[1] = far(tie(oth_y[1], got_x[3]))
    far_y[3] = far(tie(oth_y[3], got_x[1]))
    far_y[2] = far(jnp.concatenate([oth_y[2], sums], axis=0))
    sums = sums + far_y[2][rows_dev:]

    near_own, near_far = {}, {}
    near_far[0] = near(tie(far_y[0], lead_got))
    near_own[3] = near(tie(own_y[3], near_far[0]))
    near_far[3] = near(tie(far_y[3], near_own[3], got_x[2]))
    near_own[1] = near(tie(own_y[1], lead_got))
    near_far[1] = near(tie(far_y[1], near_own[1]))
    near_own[2] = near(tie(own_y[2], near_far[1], far_y[2]))
    near_far[2] = near(tie(jnp.concatenate([far_y[2][:rows_dev], sums], axis=0), near_far[3]))
    sums = sums + near_far[2][rows_dev:]

    chunk_b = pack(root, rows_dev, (1, 2))
    chunk_c = pack(root, rows_dev, (3,))
    r_high, r_low = split_root(root, rows_dev)
    chunk_b = near(tie(chunk_b, near_own[2], near_far[2]))
    chunk_c = near(tie(chunk_c, near_far[2]))

    lead_rows = lead.shape[0] - rows_dev
    pieces = [(lead, lead_rows)] + [(got_x[d], 0) for d in (1, 2, 3)]
    pieces += [(far_y[d], 0) for d in range(SIDE)]
    pieces += [(lead_got, lead_rows)] + [(near_own[d], 0) for d in (1, 2, 3)]
    pieces += [(near_far[d], 0) for d in range(SIDE)]
    g_high, g_low, t_high, t_low = first_product(pieces, rows_dev, r_high, r_low)
    new_stat, squares = update_statistics(g_high, g_low, statistics[0])
    half_a, squares = second_product(0, t_high, t_low, [lead_got, chunk_b], squares)
    back_a = sent_back(half_a)
    half_b, _ = second_product(1, t_high, t_low, [lead_got, chunk_b, chunk_c], squares)
    back_b = sent_back(tie(half_b, back_a))
    ends = near(back_b[:, half_a.shape[1] :])

    totals = tie(sums, back_a)
    bit = 1
    while bit < lax.axis_size("fsdp"):
        totals = totals + swap(totals, "fsdp", bit)
        bit *= 2

    count_all = order * lax.axis_size("fsdp") * width
    update = place_columns(
        back_a, back_b, ends, sums, totals, owner_table, CLIP_RMS * math.sqrt(count_all)
    )
    return (update, new_moment, new_second, new_stat[None])


def solution(mesh):
    placed = (
        P(("fsdp", "dp"), None),
        P(("fsdp", "dp"), None),
        P(("fsdp", "dp"), None),
        P(("fsdp", "dp"), None, None),
        P(("fsdp", "dp"), None, None),
        P("fsdp", None),
    )
    return jax.shard_map(
        local,
        mesh=mesh,
        in_specs=placed,
        out_specs=(
            P(("fsdp", "dp"), None),
            P(("fsdp", "dp"), None),
            P(("fsdp", "dp"), None),
            P(("fsdp", "dp"), None, None),
        ),
        check_vma=False,
    )
```

time: 297 us -> 154 us (0.52)
  Pallas kernels: 137 us -> 31 us
  waiting for transfers between devices: 84.2 us -> 70.3 us
  blocking collectives: 12.5 us -> 0 us
  other arithmetic: 7.54 us -> 0.08 us
  starting transfers between devices: 49.3 us -> 42.7 us
    pallas_call x8 -> x10, Pallas kernels: 137 us -> 31 us  [the longest x1 7.02 us: update_statistics(): call(body, [f32(order, order), f32(8, 128)], [VMEM, VMEM, VMEM], [VMEM, V...]
    ppermute x3 -> x6, waiting for transfers between devices: 0.01 us -> 18.6 us  [along_x(): return lax.ppermute(v, 'dp', route(lambda x, y: (x + shift, y)))]
    ppermute x7 -> x3, waiting for transfers between devices: 20.3 us -> 3.98 us  [swap(): return lax.ppermute(v, axis, [(i, i ^ bit) for i in range(count)])]
    all_to_all x1 -> x0, blocking collectives: 12.5 us -> none  [sent_back(): return lax.all_to_all(v, 'dp', 0, 0, axis_index_groups=GROUPS, tiled=True)]
    all_to_all x2, waiting for transfers between devices: 10.8 us -> 1.13 us  [sent_back(): lax.all_to_all(parts, 'dp', 0, 0, axis_index_groups=GROUPS, tiled=True)]
    ppermute x12 -> x11, waiting for transfers between devices: 48.5 us -> 40.4 us  [near(): return lax.ppermute(v, 'dp', NEAR)]
    ppermute x7 -> x3, starting transfers between devices: 11.8 us -> 5.84 us  [swap(): return lax.ppermute(v, axis, [(i, i ^ bit) for i in range(count)])]
    ppermute x12 -> x11, starting transfers between devices: 14.5 us -> 9.05 us  [near(): return lax.ppermute(v, 'dp', NEAR)]
  transfers between devices with their start and end apart: 28 -> 26, of which waited for: 17 -> 13; matrix products, arithmetic and copies ran while one was open for 3% -> 0% of each run, Pallas kernels for 10% -> 14%
where the time goes in v3:
time: 154 us; the launch traced here: 152 us
  waiting for transfers between devices  70.3 us (46%)
  starting transfers between devices  42.7 us (28%)
  Pallas kernels  31 us (20%)
  local copies, waits for them, and re-layouts  7.49 us (5%)
    ppermute x11, waiting for transfers between devices, near(): return lax.ppermute(v, 'dp', NEAR)  40.4 us
    ppermute x6, waiting for transfers between devices, along_x(): return lax.ppermute(v, 'dp', route(lambda x, y: (x + shift, y)))  18.6 us
    all_to_all x2, starting transfers between devices, sent_back(): lax.all_to_all(parts, 'dp', 0, 0, axis_index_groups=GROUPS, tiled=True)  13.1 us
    ppermute x11, starting transfers between devices, near(): return lax.ppermute(v, 'dp', NEAR)  9.05 us
    ppermute x6, starting transfers between devices, along_x(): return lax.ppermute(v, 'dp', route(lambda x, y: (x + shift, y)))  7.66 us
    unnamed x30, local copies, waits for them, and re-layouts  7.35 us
    pallas_call x1, Pallas kernels, update_statistics(): call(body, [f32(order, order), f32(8, 128)], [VMEM, VMEM, VMEM], [VMEM, V...  7.02 us
    ppermute x4, starting transfers between devices, far(): return lax.ppermute(v, 'dp', FAR)  7 us
  transfers between devices with their start and end apart: 26, of which 13 were waited for; matrix products, arithmetic and copies ran while one was open for 0% of the time, Pallas kernels for 14%

profile of v3, /device:TPU:6, one launch (start us, length us, event | category | flops | bytes accessed | tf_op | source)
XLA Modules:
  0.0 152.5 jit_solution(1424687537342559739)
XLA Ops:
  0.6 4.1 %shard_map.93 = (f32[192,1024]{1,0:T(8,128)}, f32[64,1024]{1,0:T(8,128)}, f32[128,1024]{1,0:T(8,128)}, f32[128,1024]{1,0:T(8,128)}, f32[128,1024]{1,0:T(8,128)}) custom-call(s32[1,8]{1,0:T(1,128)} %owner_ref.3, f32[64,8192]{1,0:T(8,128)} %g_ref.3, f32[1024,1024]{1,0:T(8,128)} %bitcast.3), custom_call_target="tpu_custom_call" | custom-call | bytes 4194304 | tf_op jit(solution)/shard_map/pallas_call | solution.py:181
  4.7 3.2 %collective-permute-start.1 = (f32[64,1024]{1,0:T(8,128)}, f32[64,1024]{1,0:T(8,128)S(1)}, u32[]{:S(2)}, u32[]{:S(2)}) collective-permute-start(f32[64,1024]{1,0:T(8,128)} %get-tuple-element.41), channel_id=1, source_target_pairs={{0,3},{1,2},{2,1},{3,0},{4,7},{5,6},{6,5},{7,4},{8,11},{9,10},{10,... | collective-permute-start | bytes 786440 | tf_op jit(solution)/shard_map/ppermute | solution.py:41
  8.8 2.4 %collective-permute-start = (f32[128,1024]{1,0:T(8,128)}, f32[128,1024]{1,0:T(8,128)S(1)}, u32[]{:S(2)}, u32[]{:S(2)}) collective-permute-start(f32[128,1024]{1,0:T(8,128)} %get-tuple-element.39), channel_id=1, source_target_pairs={{0,4},{1,5},{2,6},{3,7},{4,8},{5,9},{6,10},{7,11},{8,12},{9,13},{1... | collective-permute-start | bytes 1572872 | tf_op jit(solution)/shard_map/ppermute | solution.py:45
  14.4 4.3 %shard_map.94 = (f32[64,8192]{1,0:T(8,128)}, f32[64,8192]{1,0:T(8,128)}, f32[8,1024]{1,0:T(8,128)S(1)}) custom-call(f32[64,8192]{1,0:T(8,128)S(1)} %copy-done.2, f32[64,8192]{1,0:T(8,128)S(1)} %copy-done.8, f32[64,8192]{1,0:T(8,128)S(1)} %copy-done.9), custom_call_target="tpu_custom_call" | custom-call | bytes 12582912 | tf_op jit(solution)/shard_map/pallas_call | solution.py:214
  18.9 15.0 %collective-permute-done.3.refs_3_ = f32[128,1024]{1,0:T(8,128)S(1)} collective-permute-done((f32[128,1024]{1,0:T(8,128)}, f32[128,1024]{1,0:T(8,128)S(1)}, u32[]{:S(2)}, u32[]{:S(2)}) %collective-permute-start.3) | collective-permute-done | bytes 524320 | tf_op jit(solution)/shard_map/ppermute | solution.py:45
  34.5 3.4 %collective-permute-start.5 = (f32[8,1024]{1,0:T(8,128)S(1)}, f32[8,1024]{1,0:T(8,128)S(1)}, u32[]{:S(2)}, u32[]{:S(2)}) collective-permute-start(f32[8,1024]{1,0:T(8,128)S(1)} %get-tuple-element.46), channel_id=1, source_target_pairs={{0,4},{1,5},{2,6},{3,7},{4,8},{5,9},{6,10},{7,11},{8,12},{9,13},{1... | collective-permute-start | bytes 98312 | tf_op jit(solution)/shard_map/ppermute | solution.py:45
  39.7 3.6 %collective-permute-done.6 = f32[8,1024]{1,0:T(8,128)S(1)} collective-permute-done((f32[8,1024]{1,0:T(8,128)S(1)}, f32[8,1024]{1,0:T(8,128)S(1)}, u32[]{:S(2)}, u32[]{:S(2)}) %collective-permute-start.6) | collective-permute-done | bytes 32800 | tf_op jit(solution)/shard_map/ppermute | solution.py:45
  43.3 2.4 %collective-permute-start.8 = (f32[72,1024]{1,0:T(8,128)S(1)}, f32[72,1024]{1,0:T(8,128)S(1)}, u32[]{:S(2)}, u32[]{:S(2)}) collective-permute-start(f32[72,1024]{1,0:T(8,128)S(1)} %pad_maximum_fusion), channel_id=1, source_target_pairs={{0,3},{1,2},{2,1},{3,0},{4,7},{5,6},{6,5},{7,4},{8,11},{9,10},{10,... | collective-permute-start | bytes 884744 | tf_op jit(solution)/shard_map/ppermute | solution.py:41
  48.8 6.2 %collective-permute-done.4.refs_5_ = f32[64,1024]{1,0:T(8,128)S(1)} collective-permute-done((f32[64,1024]{1,0:T(8,128)S(1)}, f32[64,1024]{1,0:T(8,128)S(1)}, u32[]{:S(2)}, u32[]{:S(2)}) %collective-permute-start.4) | collective-permute-done | bytes 262176 | tf_op jit(solution)/shard_map/ppermute | solution.py:41
  56.0 4.2 %collective-permute-done.15.refs_11_ = f32[64,1024]{1,0:T(8,128)S(1)} collective-permute-done((f32[64,1024]{1,0:T(8,128)S(1)}, f32[64,1024]{1,0:T(8,128)S(1)}, u32[]{:S(2)}, u32[]{:S(2)}) %collective-permute-start.15) | collective-permute-done | bytes 262176 | tf_op jit(solution)/shard_map/ppermute | solution.py:37
  61.7 7.0 %collective-permute-done.16.refs_15_ = f32[64,1024]{1,0:T(8,128)S(1)} collective-permute-done((f32[64,1024]{1,0:T(8,128)S(1)}, f32[64,1024]{1,0:T(8,128)S(1)}, u32[]{:S(2)}, u32[]{:S(2)}) %collective-permute-start.16) | collective-permute-done | bytes 262176 | tf_op jit(solution)/shard_map/ppermute | solution.py:37
  72.3 9.2 %collective-permute-done.13.refs_10_ = f32[64,1024]{1,0:T(8,128)S(1)} collective-permute-done((f32[64,1024]{1,0:T(8,128)S(1)}, f32[64,1024]{1,0:T(8,128)S(1)}, u32[]{:S(2)}, u32[]{:S(2)}) %collective-permute-start.13) | collective-permute-done | bytes 262176 | tf_op jit(solution)/shard_map/ppermute | solution.py:37
  83.5 4.9 %shard_map.96 = (bf16[1024,1024]{1,0:T(8,128)(2,1)S(1)}, bf16[1024,1024]{1,0:T(8,128)(2,1)S(1)}, bf16[1024,1024]{1,0:T(8,128)(2,1)S(1)}, bf16[1024,1024]{1,0:T(8,128)(2,1)S(1)}) custom-call(f32[192,1024]{1,0:T(8,128)S(1)} %copy-done.12, f32[128,1024]{1,0:T(8,128)S(1)} %collective-permute-done.refs_1_, f32[128,1024]{1,0:T(8,128)S(1)} %collective-permute-done.2.refs_2_, ...), custom_call_target="tpu_custom_call" | custom-call | bytes 1048576 | tf_op jit(solution)/shard_map/pallas_call | solution.py:366
  88.4 7.0 %shard_map.98 = (f32[1024,1024]{1,0:T(8,128)}, f32[8,128]{1,0:T(8,128)S(1)}) custom-call(bf16[1024,1024]{1,0:T(8,128)(2,1)S(1)} %get-tuple-element.60.gh_ref, bf16[1024,1024]{1,0:T(8,128)(2,1)S(1)} %get-tuple-element.61.gl_ref, f32[1024,1024]{1,0:T(8,128)S(1)} %bitcast.7), custom_call_target="tpu_custom_call" | custom-call | bytes 1048576 | tf_op jit(solution)/shard_map/pallas_call | solution.py:514
  95.4 7.3 %collective-permute-done.18.refs_1_ = f32[264,1024]{1,0:T(8,128)S(1)} collective-permute-done((f32[264,1024]{1,0:T(8,128)S(1)}, f32[264,1024]{1,0:T(8,128)S(1)}, u32[]{:S(2)}, u32[]{:S(2)}) %collective-permute-start.18) | collective-permute-done | bytes 1081376 | tf_op jit(solution)/shard_map/ppermute | solution.py:37
  102.8 2.4 %shard_map.99 = (f32[8,256,128]{2,1,0:T(8,128)S(1)}, f32[8,128]{1,0:T(8,128)S(1)}) custom-call(bf16[1024,1024]{1,0:T(8,128)(2,1)S(1)} %get-tuple-element.57.high_ref, bf16[1024,1024]{1,0:T(8,128)(2,1)S(1)} %get-tuple-element.58.low_ref, f32[192,1024]{1,0:T(8,128)S(1)} %collective-permute-done.10.refs_8_.refs_0_, ...), custom_call_target="tpu_custom_call" | custom-call | tf_op jit(solution)/shard_map/pallas_call | solution.py:465
  106.2 6.6 %all-to-all-start = ((f32[8,256,128]{2,1,0:T(8,128)}), f32[8,256,128]{2,1,0:T(8,128)}, u32[]{:S(2)}, u32[]{:S(2)}) async-start(f32[8,256,128]{2,1,0:T(8,128)} %copy-done.11), calls=%async_computation | async-start | bytes 2097152 | tf_op jit(solution)/shard_map/all_to_all | solution.py:570
  112.7 2.2 %copy-done.1 = f32[1,1024,1024]{2,1,0:T(8,128)S(1)} copy-done((f32[1,1024,1024]{2,1,0:T(8,128)S(1)}, f32[1,1024,1024]{2,1,0:T(8,128)}, u32[]{:S(2)}) %copy-start.1) | copy-done | bytes 4194328
  115.8 9.5 %collective-permute-done.19.refs_2_ = f32[136,1024]{1,0:T(8,128)S(1)} collective-permute-done((f32[136,1024]{1,0:T(8,128)S(1)}, f32[136,1024]{1,0:T(8,128)S(1)}, u32[]{:S(2)}, u32[]{:S(2)}) %collective-permute-start.19) | collective-permute-done | bytes 557088 | tf_op jit(solution)/shard_map/ppermute | solution.py:37
  125.3 2.6 %shard_map.101 = (f32[8,264,128]{2,1,0:T(8,128)S(1)}, f32[8,128]{1,0:T(8,128)}) custom-call(bf16[1024,1024]{1,0:T(8,128)(2,1)S(1)} %get-tuple-element.57.high_ref, bf16[1024,1024]{1,0:T(8,128)(2,1)S(1)} %copy-done.4, f32[192,1024]{1,0:T(8,128)S(1)} %collective-permute-done.10.refs_8_.refs_0_, f32[264,1024]{1,0:T(8,128)S(1)} %copy-done.6, ...), custom_call_target="tpu_custom_call" | custom-call | bytes 146800640 | tf_op jit(solution)/shard_map/pallas_call | solution.py:465
  128.9 6.6 %all-to-all-start.1 = ((f32[8,264,128]{2,1,0:T(8,128)}), f32[8,264,128]{2,1,0:T(8,128)S(1)}, u32[]{:S(2)}, u32[]{:S(2)}) async-start(f32[8,264,128]{2,1,0:T(8,128)} %copy-done.10), calls=%async_computation.1 | async-start | bytes 2162688 | tf_op jit(solution)/shard_map/all_to_all | solution.py:570
  140.7 3.9 %collective-permute-start.23 = (f32[8,1024]{1,0:T(8,128)S(1)}, f32[8,1024]{1,0:T(8,128)S(1)}, u32[]{:S(2)}, u32[]{:S(2)}) collective-permute-start(f32[8,1024]{1,0:T(8,128)S(1)} %add.30), channel_id=1, source_target_pairs={{0,64},{16,80},{32,96},{48,112},{64,0},{80,16},{96,32},{112,48},{1... | collective-permute-start | bytes 98312 | tf_op jit(solution)/shard_map/ppermute | solution.py:54
  146.5 3.1 %collective-permute-done.20.ends_ref = f32[8,8,128]{2,1,0:T(8,128)S(1)} collective-permute-done((f32[8,8,128]{2,1,0:T(8,128)S(1)}, f32[8,8,128]{2,1,0:T(8,128)S(1)}, u32[]{:S(2)}, u32[]{:S(2)}) %collective-permute-start.20) | collective-permute-done | bytes 32800 | tf_op jit(solution)/shard_map/ppermute | solution.py:37
  149.6 2.8 %shard_map.102 = f32[64,8192]{1,0:T(8,128)} custom-call(s32[1,8]{1,0:T(1,128)S(1)} %copy-done.13, f32[8,256,128]{2,1,0:T(8,128)} %all-to-all-done.first_ref, f32[8,264,128]{2,1,0:T(8,128)S(1)} %all-to-all-done.1.second_ref, f32[8,8,128]{2,1,0:T(8,128)S(1)} %collective-permute-done.20.ends_ref, f32[8,1024]{1,0:T(8,128)S(1)} %slice_add_fusion.sums_ref, ...), custom_call_target="tpu_custom_call" | custom-call | bytes 4194304 | tf_op jit(solution)/shard_map/pallas_call | solution.py:558
  (81 shorter events, 27.7 us)
Async XLA Ops:
  4.7 14.0 %collective-permute-start.1 = (f32[64,1024]{1,0:T(8,128)}, f32[64,1024]{1,0:T(8,128)S(1)}, u32[]{:S(2)}, u32[]{:S(2)}) collective-permute-start(f32[64,1024]{1,0:T(8,128)} %get-tuple-element.41), channel_id=1, source_target_pairs={{0,3},{1,2},{2,1},{3,0},{4,7},{5,6},{6,5},{7,4},{8,11},{9,10},{10,... | collective-permute-start | bytes 786440 | tf_op jit(solution)/shard_map/ppermute | solution.py:41
  7.9 26.0 %collective-permute-start.3 = (f32[128,1024]{1,0:T(8,128)}, f32[128,1024]{1,0:T(8,128)S(1)}, u32[]{:S(2)}, u32[]{:S(2)}) collective-permute-start(f32[128,1024]{1,0:T(8,128)} %get-tuple-element.44), channel_id=1, source_target_pairs={{0,12},{1,13},{2,14},{3,15},{4,0},{5,1},{6,2},{7,3},{8,4},{9,5},{1... | collective-permute-start | bytes 1572872 | tf_op jit(solution)/shard_map/ppermute | solution.py:45
  8.7 30.0 %collective-permute-start.10 = (f32[192,1024]{1,0:T(8,128)}, f32[192,1024]{1,0:T(8,128)S(1)}, u32[]{:S(2)}, u32[]{:S(2)}) collective-permute-start(f32[192,1024]{1,0:T(8,128)} %get-tuple-element.38.refs_0_), channel_id=1, source_target_pairs={{0,1},{1,0},{2,3},{3,2},{4,5},{5,4},{6,7},{7,6},{8,9},{9,8},{10,11... | collective-permute-start | bytes 2359304 | tf_op jit(solution)/shard_map/ppermute | solution.py:37
  8.8 25.2 %collective-permute-start = (f32[128,1024]{1,0:T(8,128)}, f32[128,1024]{1,0:T(8,128)S(1)}, u32[]{:S(2)}, u32[]{:S(2)}) collective-permute-start(f32[128,1024]{1,0:T(8,128)} %get-tuple-element.39), channel_id=1, source_target_pairs={{0,4},{1,5},{2,6},{3,7},{4,8},{5,9},{6,10},{7,11},{8,12},{9,13},{1... | collective-permute-start | bytes 1572872 | tf_op jit(solution)/shard_map/ppermute | solution.py:45
  18.7 15.7 %collective-permute-start.2 = (f32[128,1024]{1,0:T(8,128)S(1)}, f32[128,1024]{1,0:T(8,128)S(1)}, u32[]{:S(2)}, u32[]{:S(2)}) collective-permute-start(f32[128,1024]{1,0:T(8,128)S(1)} %copy-done.14), channel_id=1, source_target_pairs={{0,8},{1,9},{2,10},{3,11},{4,12},{5,13},{6,14},{7,15},{8,0},{9,1},... | collective-permute-start | bytes 1572872 | tf_op jit(solution)/shard_map/ppermute | solution.py:45
  34.0 22.0 %collective-permute-start.9 = (f32[64,1024]{1,0:T(8,128)S(1)}, f32[64,1024]{1,0:T(8,128)S(1)}, u32[]{:S(2)}, u32[]{:S(2)}) collective-permute-start(f32[64,1024]{1,0:T(8,128)S(1)} %get-tuple-element.47), channel_id=1, source_target_pairs={{0,3},{1,2},{2,1},{3,0},{4,7},{5,6},{6,5},{7,4},{8,11},{9,10},{10,... | collective-permute-start | bytes 786440 | tf_op jit(solution)/shard_map/ppermute | solution.py:41
  34.5 5.3 %collective-permute-start.5 = (f32[8,1024]{1,0:T(8,128)S(1)}, f32[8,1024]{1,0:T(8,128)S(1)}, u32[]{:S(2)}, u32[]{:S(2)}) collective-permute-start(f32[8,1024]{1,0:T(8,128)S(1)} %get-tuple-element.46), channel_id=1, source_target_pairs={{0,4},{1,5},{2,6},{3,7},{4,8},{5,9},{6,10},{7,11},{8,12},{9,13},{1... | collective-permute-start | bytes 98312 | tf_op jit(solution)/shard_map/ppermute | solution.py:45
  37.8 5.5 %collective-permute-start.6 = (f32[8,1024]{1,0:T(8,128)S(1)}, f32[8,1024]{1,0:T(8,128)S(1)}, u32[]{:S(2)}, u32[]{:S(2)}) collective-permute-start(f32[8,1024]{1,0:T(8,128)S(1)} %get-tuple-element.46), channel_id=1, source_target_pairs={{0,8},{1,9},{2,10},{3,11},{4,12},{5,13},{6,14},{7,15},{8,0},{9,1},... | collective-permute-start | bytes 98312 | tf_op jit(solution)/shard_map/ppermute | solution.py:45
  37.8 5.5 %collective-permute-start.7 = (f32[8,1024]{1,0:T(8,128)S(1)}, f32[8,1024]{1,0:T(8,128)S(1)}, u32[]{:S(2)}, u32[]{:S(2)}) collective-permute-start(f32[8,1024]{1,0:T(8,128)S(1)} %get-tuple-element.46), channel_id=1, source_target_pairs={{0,12},{1,13},{2,14},{3,15},{4,0},{5,1},{6,2},{7,3},{8,4},{9,5},{1... | collective-permute-start | bytes 98312 | tf_op jit(solution)/shard_map/ppermute | solution.py:45
  38.7 8.1 %collective-permute-start.14 = (f32[64,1024]{1,0:T(8,128)S(1)}, f32[64,1024]{1,0:T(8,128)S(1)}, u32[]{:S(2)}, u32[]{:S(2)}) collective-permute-start(f32[64,1024]{1,0:T(8,128)S(1)} %collective-permute-done.1.refs_4_), channel_id=1, source_target_pairs={{0,1},{1,0},{2,3},{3,2},{4,5},{5,4},{6,7},{7,6},{8,9},{9,8},{10,11... | collective-permute-start | bytes 786440 | tf_op jit(solution)/shard_map/ppermute | solution.py:37
  43.3 18.3 %collective-permute-start.8 = (f32[72,1024]{1,0:T(8,128)S(1)}, f32[72,1024]{1,0:T(8,128)S(1)}, u32[]{:S(2)}, u32[]{:S(2)}) collective-permute-start(f32[72,1024]{1,0:T(8,128)S(1)} %pad_maximum_fusion), channel_id=1, source_target_pairs={{0,3},{1,2},{2,1},{3,0},{4,7},{5,6},{6,5},{7,4},{8,11},{9,10},{10,... | collective-permute-start | bytes 884744 | tf_op jit(solution)/shard_map/ppermute | solution.py:41
  45.8 9.2 %collective-permute-start.4 = (f32[64,1024]{1,0:T(8,128)S(1)}, f32[64,1024]{1,0:T(8,128)S(1)}, u32[]{:S(2)}, u32[]{:S(2)}) collective-permute-start(f32[64,1024]{1,0:T(8,128)S(1)} %get-tuple-element.45), channel_id=1, source_target_pairs={{0,3},{1,2},{2,1},{3,0},{4,7},{5,6},{6,5},{7,4},{8,11},{9,10},{10,... | collective-permute-start | bytes 786440 | tf_op jit(solution)/shard_map/ppermute | solution.py:41
  46.8 8.2 %collective-permute-start.11 = (f32[64,1024]{1,0:T(8,128)S(1)}, f32[64,1024]{1,0:T(8,128)S(1)}, u32[]{:S(2)}, u32[]{:S(2)}) collective-permute-start(f32[64,1024]{1,0:T(8,128)S(1)} %get-tuple-element.48), channel_id=1, source_target_pairs={{0,1},{1,0},{2,3},{3,2},{4,5},{5,4},{6,7},{7,6},{8,9},{9,8},{10,11... | collective-permute-start | bytes 786440 | tf_op jit(solution)/shard_map/ppermute | solution.py:37
  46.8 13.4 %collective-permute-start.15 = (f32[64,1024]{1,0:T(8,128)S(1)}, f32[64,1024]{1,0:T(8,128)S(1)}, u32[]{:S(2)}, u32[]{:S(2)}) collective-permute-start(f32[64,1024]{1,0:T(8,128)S(1)} %get-tuple-element.52), channel_id=1, source_target_pairs={{0,1},{1,0},{2,3},{3,2},{4,5},{5,4},{6,7},{7,6},{8,9},{9,8},{10,11... | collective-permute-start | bytes 786440 | tf_op jit(solution)/shard_map/ppermute | solution.py:37
  55.0 15.1 %collective-permute-start.12 = (f32[64,1024]{1,0:T(8,128)S(1)}, f32[64,1024]{1,0:T(8,128)S(1)}, u32[]{:S(2)}, u32[]{:S(2)}) collective-permute-start(f32[64,1024]{1,0:T(8,128)S(1)} %collective-permute-done.4.refs_5_), channel_id=1, source_target_pairs={{0,1},{1,0},{2,3},{3,2},{4,5},{5,4},{6,7},{7,6},{8,9},{9,8},{10,11... | collective-permute-start | bytes 786440 | tf_op jit(solution)/shard_map/ppermute | solution.py:37
  60.2 8.5 %collective-permute-start.16 = (f32[64,1024]{1,0:T(8,128)S(1)}, f32[64,1024]{1,0:T(8,128)S(1)}, u32[]{:S(2)}, u32[]{:S(2)}) collective-permute-start(f32[64,1024]{1,0:T(8,128)S(1)} %collective-permute-done.9.refs_7_), channel_id=1, source_target_pairs={{0,1},{1,0},{2,3},{3,2},{4,5},{5,4},{6,7},{7,6},{8,9},{9,8},{10,11... | collective-permute-start | bytes 786440 | tf_op jit(solution)/shard_map/ppermute | solution.py:37
  68.7 12.8 %collective-permute-start.17 = (f32[72,1024]{1,0:T(8,128)S(1)}, f32[72,1024]{1,0:T(8,128)S(1)}, u32[]{:S(2)}, u32[]{:S(2)}) collective-permute-start(f32[72,1024]{1,0:T(8,128)S(1)} %pad_maximum_fusion.1), channel_id=1, source_target_pairs={{0,1},{1,0},{2,3},{3,2},{4,5},{5,4},{6,7},{7,6},{8,9},{9,8},{10,11... | collective-permute-start | bytes 884744 | tf_op jit(solution)/shard_map/ppermute | solution.py:37
  70.1 11.4 %collective-permute-start.13 = (f32[64,1024]{1,0:T(8,128)S(1)}, f32[64,1024]{1,0:T(8,128)S(1)}, u32[]{:S(2)}, u32[]{:S(2)}) collective-permute-start(f32[64,1024]{1,0:T(8,128)S(1)} %get-tuple-element.50), channel_id=1, source_target_pairs={{0,1},{1,0},{2,3},{3,2},{4,5},{5,4},{6,7},{7,6},{8,9},{9,8},{10,11... | collective-permute-start | bytes 786440 | tf_op jit(solution)/shard_map/ppermute | solution.py:37
  81.5 21.3 %collective-permute-start.18 = (f32[264,1024]{1,0:T(8,128)S(1)}, f32[264,1024]{1,0:T(8,128)S(1)}, u32[]{:S(2)}, u32[]{:S(2)}) collective-permute-start(f32[264,1024]{1,0:T(8,128)S(1)} %shard_map.97), channel_id=1, source_target_pairs={{0,1},{1,0},{2,3},{3,2},{4,5},{5,4},{6,7},{7,6},{8,9},{9,8},{10,11... | collective-permute-start | bytes 3244040 | tf_op jit(solution)/shard_map/ppermute | solution.py:37
  106.2 22.7 %all-to-all-start = ((f32[8,256,128]{2,1,0:T(8,128)}), f32[8,256,128]{2,1,0:T(8,128)}, u32[]{:S(2)}, u32[]{:S(2)}) async-start(f32[8,256,128]{2,1,0:T(8,128)} %copy-done.11), calls=%async_computation | async-start | bytes 2097152 | tf_op jit(solution)/shard_map/all_to_all | solution.py:570
  115.7 9.6 %collective-permute-start.19 = (f32[136,1024]{1,0:T(8,128)S(1)}, f32[136,1024]{1,0:T(8,128)S(1)}, u32[]{:S(2)}, u32[]{:S(2)}) collective-permute-start(f32[136,1024]{1,0:T(8,128)S(1)} %shard_map.100), channel_id=1, source_target_pairs={{0,1},{1,0},{2,3},{3,2},{4,5},{5,4},{6,7},{7,6},{8,9},{9,8},{10,11... | collective-permute-start | bytes 1671176 | tf_op jit(solution)/shard_map/ppermute | solution.py:37
  128.9 16.8 %all-to-all-start.1 = ((f32[8,264,128]{2,1,0:T(8,128)}), f32[8,264,128]{2,1,0:T(8,128)S(1)}, u32[]{:S(2)}, u32[]{:S(2)}) async-start(f32[8,264,128]{2,1,0:T(8,128)} %copy-done.10), calls=%async_computation.1 | async-start | bytes 2162688 | tf_op jit(solution)/shard_map/all_to_all | solution.py:570
  140.7 5.8 %collective-permute-start.23 = (f32[8,1024]{1,0:T(8,128)S(1)}, f32[8,1024]{1,0:T(8,128)S(1)}, u32[]{:S(2)}, u32[]{:S(2)}) collective-permute-start(f32[8,1024]{1,0:T(8,128)S(1)} %add.30), channel_id=1, source_target_pairs={{0,64},{16,80},{32,96},{48,112},{64,0},{80,16},{96,32},{112,48},{1... | collective-permute-start | bytes 98312 | tf_op jit(solution)/shard_map/ppermute | solution.py:54
  145.7 3.9 %collective-permute-start.20 = (f32[8,8,128]{2,1,0:T(8,128)S(1)}, f32[8,8,128]{2,1,0:T(8,128)S(1)}, u32[]{:S(2)}, u32[]{:S(2)}) collective-permute-start(f32[8,8,128]{2,1,0:T(8,128)S(1)} %slice.48), channel_id=1, source_target_pairs={{0,1},{1,0},{2,3},{3,2},{4,5},{5,4},{6,7},{7,6},{8,9},{9,8},{10,11... | collective-permute-start | bytes 98312 | tf_op jit(solution)/shard_map/ppermute | solution.py:37
  (17 other events, 138.7 us)

commit v4 on v3

--- a/solution.py
+++ b/solution.py
@@ -154,6 +154,7 @@
     order = root.shape[0]
     count = width // order
     part = order // 8
+    sizes = [(part + rows, order), (rows, order)] + [(2 * rows, order)] * 3
 
     def body(owner_ref, g_ref, root_ref, lead_ref, oth_ref, x1_ref, x2_ref, x3_ref, sems):
         x, y, is_left, outer = spot()
@@ -180,7 +181,7 @@
 
     return call(
         body,
-        [f32(part + rows, order), f32(rows, order)] + [f32(2 * rows, order)] * 3,
+        [in_vmem(*size, dtype=jnp.float32) for size in sizes],
         [SMEM, HBM, HBM],
         [VMEM] * 5,
         [pltpu.SemaphoreType.DMA((4 * SIDE,))],
@@ -195,84 +196,86 @@
     count = width // order
 
     def body(g_ref, m_ref, s_ref, m_out, s_out, sums_ref):
-        for c in range(count):
-            cols = slice(c * order, (c + 1) * order)
-
-            def step(i, total):
-                at = pl.ds(pl.multiple_of(i * 8, 8), 8)
-                g = g_ref[at, cols]
-                new_m = BETA_ONE * m_ref[at, cols] + (1.0 - BETA_ONE) * g
-                new_s = BETA_TWO * s_ref[at, cols] + (1.0 - BETA_TWO) * g * g
-                m_out[at, cols] = new_m
-                s_out[at, cols] = new_s
-                a = new_m / BIAS_ONE / (jnp.sqrt(new_s / BIAS_TWO) + ADAM_EPS)
-                return total + a * a
-
-            total = lax.fori_loop(0, rows // 8, step, jnp.zeros((8, order), jnp.float32))
-            sums_ref[c : c + 1, :] = jnp.sum(total, axis=0, keepdims=True)
-
-    return call(
-        body,
-        [f32(rows, width)] * 2 + [f32(8, order)],
-        [VMEM] * 3,
-        [VMEM] * 3,
-        [],
-        0,
-        24 * rows * width,
+        def step(i, total):
+            at = pl.ds(pl.multiple_of(i * 8, 8), 8)
+            g = g_ref[at, :]
+            new_m = BETA_ONE * m_ref[at, :] + (1.0 - BETA_ONE) * g
+            new_s = BETA_TWO * s_ref[at, :] + (1.0 - BETA_TWO) * g * g
+            m_out[at, :] = new_m
+            s_out[at, :] = new_s
+            a = new_m / BIAS_ONE / (jnp.sqrt(new_s / BIAS_TWO) + ADAM_EPS)
+            return total + a * a
+
+        total = lax.fori_loop(0, rows // 8, step, jnp.zeros((8, 2 * order), jnp.float32))
+        total = jnp.sum(total, axis=0, keepdims=True)
+        for h in range(2):
+            sums_ref[pl.ds(2 * pl.program_id(0) + h, 1), :] = total[:, h * order : (h + 1) * order]
+
+    block = pl.BlockSpec((rows, 2 * order), lambda c: (0, c))
+    return pl.pallas_call(
+        body,
+        grid=(count // 2,),
+        out_shape=[f32(rows, width)] * 2 + [f32(8, order)],
+        in_specs=[block] * 3,
+        out_specs=[block] * 2 + [pl.BlockSpec((8, order), lambda c: (0, 0))],
+        compiler_params=pltpu.CompilerParams(vmem_limit_bytes=40 * 2**20),
+        cost_estimate=pl.CostEstimate(flops=0, bytes_accessed=24 * rows * width, transcendentals=0),
     )(gradient, moment, second)
 
 
-def pack(root, rows, units):
+def pack(root, rows):
     order = root.shape[0]
     half, quarter, part = order // 2, order // 4, order // 8
-    fold = units[-1]
-    last = (len(units) - 1) * part
-
-    def body(root_ref, out_ref, buf, sems):
+
+    def body(root_ref, b_ref, c_ref, buf, sems):
         x, y, is_left, outer = spot()
-        out_ref[last + part :, :] = jnp.zeros((8, order), jnp.float32)
+        places = [(b_ref, 0), (b_ref, part), (c_ref, 0)]
+        for to_ref in (b_ref, c_ref):
+            to_ref[to_ref.shape[0] - 8 :, :] = jnp.zeros((8, order), jnp.float32)
 
         @pl.when(is_left)
         def _():
             copies = []
-            for i, unit in enumerate(units):
-                to_ref = out_ref.at[pl.ds(i * part, part), :]
-                copies += unit_copies(root_ref, unit, rows, x, y, is_left, to_ref, sems, 2 * SIDE * i)
+            for i in range(3):
+                to_ref, first = places[i]
+                to_ref = to_ref.at[pl.ds(first, part), :]
+                copies += unit_copies(root_ref, i + 1, rows, x, y, is_left, to_ref, sems, 2 * SIDE * i)
             finish(run(copies))
 
         @pl.when(jnp.logical_not(is_left))
         def _():
-            at = pl.ds((fold - 2) * half, half)
-            copies = [pltpu.make_async_copy(root_ref.at[at, at], buf, sems.at[0])]
-            for i, unit in enumerate(units[:-1]):
-                to_ref = out_ref.at[pl.ds(i * part, part), :]
-                copies += cross_copies(root_ref, unit, to_ref, sems, 2 * i + 1)
+            copies = cross_copies(root_ref, 1, b_ref.at[pl.ds(0, part), :], sems, 0)
+            for i in range(2):
+                at = pl.ds(i * half, half)
+                copies.append(pltpu.make_async_copy(root_ref.at[at, at], buf.at[i], sems.at[2 + i]))
             finish(run(copies))
             row = lax.broadcasted_iota(jnp.int32, (quarter, quarter), 0)
             col = lax.broadcasted_iota(jnp.int32, (quarter, quarter), 1)
-            low = buf[quarter:, quarter:]
-            both = jnp.where(row <= col, buf[:quarter, :quarter], low)
-            at = slice(last, last + part)
-            for h in range(2):
-                out_ref[at, h * half : h * half + quarter] = buf[h * part : (h + 1) * part, quarter:]
-                out_ref[at, h * half + quarter : (h + 1) * half] = both[h * part : (h + 1) * part]
-            out_ref[last + part : last + part + 1, :quarter] = jnp.sum(
-                jnp.where(row == col, low, 0.0), axis=0, keepdims=True
-            )
+            for i in range(2):
+                low = buf[i, quarter:, quarter:]
+                both = jnp.where(row <= col, buf[i, :quarter, :quarter], low)
+                out_ref, first = places[i + 1]
+                at = slice(first, first + part)
+                for h in range(2):
+                    out_ref[at, h * half : h * half + quarter] = buf[i, h * part : (h + 1) * part, quarter:]
+                    out_ref[at, h * half + quarter : (h + 1) * half] = both[h * part : (h + 1) * part]
+                out_ref[first + part : first + part + 1, :quarter] = jnp.sum(
+                    jnp.where(row == col, low, 0.0), axis=0, keepdims=True
+                )
 
     return call(
         body,
-        f32(last + part + 8, order),
+        [f32(2 * part + 8, order), f32(part + 8, order)],
         [HBM],
-        VMEM,
-        [pltpu.VMEM((half, half), jnp.float32), pltpu.SemaphoreType.DMA((2 * SIDE * len(units),))],
-        0,
-        8 * len(units) * part * order,
+        [VMEM, VMEM],
+        [pltpu.VMEM((2, half, half), jnp.float32), pltpu.SemaphoreType.DMA((6 * SIDE,))],
+        0,
+        24 * part * order,
     )(root)
 
 
-def in_vmem(*shape):
-    return pltpu.VMEM(shape, jnp.bfloat16)
+def in_vmem(*shape, dtype=jnp.bfloat16):
+    return pltpu.VMEM(shape, dtype)
 
 
 def cut_two(src, high, low, tiles):
@@ -401,10 +404,20 @@
     few = part // 2
     count = len(chunks)
 
-    def body(high_ref, low_ref, *refs):
-        chunk_refs, sq_ref = refs[:count], refs[count]
-        whole, sq_out, b_high, b_low = refs[count + 1 :]
+    def body(*refs):
+        sources, sq_ref = refs[: 2 + count], refs[2 + count]
+        whole, sq_out, b_high, b_low, *buffers = refs[3 + count :]
+        sems = buffers.pop()
         x, y, is_left, outer = spot()
+        finish(
+            run(
+                [
+                    pltpu.make_async_copy(source, buffer, sems.at[i])
+                    for i, (source, buffer) in enumerate(zip(sources, buffers))
+                ]
+            )
+        )
+        high_ref, low_ref, *chunk_refs = buffers
         outs = []
         for k in range(dests):
             to_y = 3 - y if k % 2 else y
@@ -457,19 +470,17 @@
                         ]
             sq_out[...] = sq_ref[...] + total
 
-        if which == 1:
-            for k in range(dests):
-                whole[k, 8 * part :, :] = sq_out[...]
-
     short = pltpu.VMEM((order, half), jnp.bfloat16)
     return call(
         body,
-        [f32(dests, 8 * part + 8 * which, 128), f32(8, 128)],
-        [VMEM] * (3 + count),
+        [pltpu.HBM((dests, 8 * part + 8 * which, 128), jnp.float32), f32(8, 128)],
+        [HBM] * (2 + count) + [VMEM],
         [VMEM] * 2,
-        [short, short],
-        0,
-        140 * order * order * which,
+        [short, short]
+        + [pltpu.VMEM(v.shape, v.dtype) for v in (t_high, t_low, *chunks)]
+        + [pltpu.SemaphoreType.DMA((2 + count,))],
+        0,
+        0,
     )(t_high, t_low, *chunks, squares)
 
 
@@ -523,26 +534,24 @@
     )(g_high, g_low, stat)
 
 
-def place_columns(first, second, ends, sums, totals, owner_table, largest):
+def place_columns(first, second, sums, totals, owner_table, largest):
     count = first.shape[0]
     part = first.shape[1] // 8
     order = 8 * first.shape[2]
     end = 8 * part
 
-    def body(owner_ref, first_ref, second_ref, ends_ref, sums_ref, totals_ref, out_ref, scratch):
+    def body(owner_ref, first_ref, second_ref, sums_ref, totals_ref, out_ref, scratch):
         x, y, is_left, outer = spot()
         total = jnp.sum(jnp.sum(totals_ref[...], axis=0, keepdims=True), axis=1, keepdims=True)
         clip = jnp.minimum(1.0, largest / jnp.sqrt(total + 1e-06))
         scratch[...] = jnp.broadcast_to(jnp.sum(sums_ref[...], axis=1, keepdims=True), (count, 128))
-        for k in range(count):
-            from_y = 3 - y if k % 2 else y
-            p = 2 * lax.bitwise_and(x - k // 2, 3) + lax.shift_right_logical(from_y, 1)
-            from_left = lax.bitwise_and(from_y, 1) == 0
-            col = column_of(owner_ref, p, count)
-            squares = second_ref[p, end : end + 1, :] + ends_ref[p, :1, :]
-            scale = jnp.sqrt(scratch[pl.ds(col, 1), :] / (squares + 1e-06)) * clip
+        for c in range(count):
+            p = owner_ref[0, c]
+            from_left = (lax.bitwise_and(p, 1) == 0) == outer
+            squares = second_ref[p, end : end + 1, :]
+            scale = jnp.sqrt(scratch[c : c + 1, :] / (squares + 1e-06)) * clip
             for j in range(8):
-                cols = pl.ds(pl.multiple_of(col * order + j * 128, 128), 128)
+                cols = slice(c * order + j * 128, c * order + (j + 1) * 128)
                 at = slice(j * part, (j + 1) * part)
                 back = (j + 4) % 8
                 across = slice(back * part, (back + 1) * part)
@@ -558,12 +567,29 @@
     return call(
         body,
         f32(2 * part, count * order),
-        [SMEM] + [VMEM] * 5,
+        [SMEM] + [VMEM] * 4,
         VMEM,
         [pltpu.VMEM((count, 128), jnp.float32)],
         0,
         16 * count * part * order,
-    )(owner_table, first, second, ends, sums, totals)
+    )(owner_table, first, second, sums, totals)
+
+
+def with_squares(parts, squares):
+    rows = parts.shape[1]
+
+    def body(parts_ref, squares_ref, out_ref):
+        for k in range(parts.shape[0]):
+            out_ref[k] = squares_ref[...]
+
+    return pl.pallas_call(
+        body,
+        grid=(1,),
+        out_shape=f32(*parts.shape),
+        in_specs=[pl.BlockSpec(memory_space=pl.ANY), pl.BlockSpec((8, 128), lambda i: (0, 0))],
+        out_specs=pl.BlockSpec((parts.shape[0], 8, 128), lambda i: (0, rows // 8 - 1, 0)),
+        input_output_aliases={0: 0},
+    )(parts, squares)
 
 
 def sent_back(parts):
@@ -573,6 +599,7 @@
 def local(gradient, moment, second, statistics, inv_roots, owner_table):
     rows_dev, width = gradient.shape
     order = statistics.shape[1]
+    col_blocks = width // order
     root = inv_roots[0]
 
     lead, oth, x1, x2, x3 = cut(gradient, root, owner_table)
@@ -580,33 +607,24 @@
     far_y = {0: far(oth)}
     new_moment, new_second, own_sums = adam(gradient, moment, second, order)
     got_x = {1: along_x(x1, 1), 3: along_x(x3, 3)}
-    got_x[2] = along_x(tie(x2, far_y[0], own_sums), 2)
+    got_x[2] = along_x(tie(x2, far_y[0], got_x[1], got_x[3], own_sums), 2)
     own_y = {d: got_x[d][:rows_dev] for d in (1, 2, 3)}
     oth_y = {d: got_x[d][rows_dev:] for d in (1, 2, 3)}
-    own_sums = tie(own_sums, got_x[2])
-    sums = own_sums
     for d in (1, 2, 3):
-        sums = sums + along_x(own_sums, d)
-    far_y[1] = far(tie(oth_y[1], got_x[3]))
-    far_y[3] = far(tie(oth_y[3], got_x[1]))
-    far_y[2] = far(jnp.concatenate([oth_y[2], sums], axis=0))
-    sums = sums + far_y[2][rows_dev:]
-
-    near_own, near_far = {}, {}
-    near_far[0] = near(tie(far_y[0], lead_got))
-    near_own[3] = near(tie(own_y[3], near_far[0]))
-    near_far[3] = near(tie(far_y[3], near_own[3], got_x[2]))
-    near_own[1] = near(tie(own_y[1], lead_got))
-    near_far[1] = near(tie(far_y[1], near_own[1]))
-    near_own[2] = near(tie(own_y[2], near_far[1], far_y[2]))
-    near_far[2] = near(tie(jnp.concatenate([far_y[2][:rows_dev], sums], axis=0), near_far[3]))
-    sums = sums + near_far[2][rows_dev:]
-
-    chunk_b = pack(root, rows_dev, (1, 2))
-    chunk_c = pack(root, rows_dev, (3,))
+        far_y[d] = far(oth_y[d])
+
+    chunk_b, chunk_c = pack(root, rows_dev)
     r_high, r_low = split_root(root, rows_dev)
+    near_own = {1: near(tie(own_y[1], lead_got))}
+    near_far = {0: near(tie(far_y[0], lead_got))}
+    near_own[3] = near(tie(own_y[3], near_own[1], far_y[1], far_y[3]))
+    near_far[1] = near(tie(far_y[1], near_far[0], got_x[2]))
+    near_far[3] = near(tie(far_y[3], near_own[3]))
+    near_own[2] = near(tie(own_y[2], near_far[1], far_y[2], chunk_b, chunk_c, r_high))
+    near_far[2] = near(tie(far_y[2], near_far[3]))
+
     chunk_b = near(tie(chunk_b, near_own[2], near_far[2]))
-    chunk_c = near(tie(chunk_c, near_far[2]))
+    chunk_c = near(tie(chunk_c, near_own[2], near_far[2]))
 
     lead_rows = lead.shape[0] - rows_dev
     pieces = [(lead, lead_rows)] + [(got_x[d], 0) for d in (1, 2, 3)]
@@ -615,21 +633,30 @@
     pieces += [(near_far[d], 0) for d in range(SIDE)]
     g_high, g_low, t_high, t_low = first_product(pieces, rows_dev, r_high, r_low)
     new_stat, squares = update_statistics(g_high, g_low, statistics[0])
+    sums = tie(own_sums, squares)
+    for bit in (4, 8):
+        sums = sums + swap(sums, "dp", bit)
+    squares = tie(squares, sums)
     half_a, squares = second_product(0, t_high, t_low, [lead_got, chunk_b], squares)
-    back_a = sent_back(half_a)
-    half_b, _ = second_product(1, t_high, t_low, [lead_got, chunk_b, chunk_c], squares)
-    back_b = sent_back(tie(half_b, back_a))
-    ends = near(back_b[:, half_a.shape[1] :])
-
-    totals = tie(sums, back_a)
-    bit = 1
+    sums = tie(sums, squares)
+    sums = sums + swap(sums, "dp", 3)
+    back_a = sent_back(tie(half_a, chunk_c, sums))
+    half_b, squares = second_product(1, t_high, t_low, [lead_got, chunk_b, chunk_c], squares)
+    squares = squares + near(squares)
+    totals = sums + swap(sums, "fsdp", 1)
+    back_b = sent_back(tie(with_squares(half_b, tie(squares, totals)), back_a))
+    totals = tie(totals, back_a)
+    bit = 2
     while bit < lax.axis_size("fsdp"):
         totals = totals + swap(totals, "fsdp", bit)
         bit *= 2
+    both = jnp.concatenate([sums, totals], axis=0)
+    both = both + near(both)
+    sums, totals = both[:col_blocks], both[col_blocks:]
 
     count_all = order * lax.axis_size("fsdp") * width
     update = place_columns(
-        back_a, back_b, ends, sums, totals, owner_table, CLIP_RMS * math.sqrt(count_all)
+        back_a, back_b, sums, totals, owner_table, CLIP_RMS * math.sqrt(count_all)
     )
     return (update, new_moment, new_second, new_stat[None])
 

time: 154 us -> 146 us (0.948)
  waiting for transfers between devices: 70.3 us -> 49.1 us
  starting transfers between devices: 42.7 us -> 52.9 us
  Pallas kernels: 31 us -> 32.8 us
    ppermute x6 -> x3, waiting for transfers between devices: 18.6 us -> 0.01 us  [along_x(): return lax.ppermute(v, 'dp', route(lambda x, y: (x + shift, y)))]
    ppermute x11 -> x12, waiting for transfers between devices: 40.4 us -> 31.4 us  [near(): return lax.ppermute(v, 'dp', NEAR)]
    ppermute x3 -> x6, starting transfers between devices: 5.84 us -> 13.8 us  [swap(): return lax.ppermute(v, axis, [(i, i ^ bit) for i in range(count)])]
    ppermute x3 -> x6, waiting for transfers between devices: 3.98 us -> 11.2 us  [swap(): return lax.ppermute(v, axis, [(i, i ^ bit) for i in range(count)])]
    ppermute x6 -> x3, starting transfers between devices: 7.66 us -> 3.42 us  [along_x(): return lax.ppermute(v, 'dp', route(lambda x, y: (x + shift, y)))]
    ppermute x11 -> x12, starting transfers between devices: 9.05 us -> 12.2 us  [near(): return lax.ppermute(v, 'dp', NEAR)]
    all_to_all x2, starting transfers between devices: 13.1 us -> 15.3 us  [sent_back(): lax.all_to_all(parts, 'dp', 0, 0, axis_index_groups=GROUPS, tiled=True)]
    pallas_call x7, Pallas kernels: 18.6 us -> 20.3 us  [the longest x2 7.44 us: second_product(): call(body, [pltpu.HBM((dests, 8 * part + 8 * which, 128), jnp.float32), f...]
  transfers between devices with their start and end apart: 26 -> 27, of which waited for: 13 -> 17; matrix products, arithmetic and copies ran while one was open for 0% -> 1% of each run, Pallas kernels for 14% -> 19%
where the time goes in v4:
time: 146 us; the launch traced here: 144 us
  starting transfers between devices  52.9 us (36%)
  waiting for transfers between devices  49.1 us (34%)
  Pallas kernels  32.8 us (22%)
  local copies, waits for them, and re-layouts  7.75 us (5%)
    ppermute x12, waiting for transfers between devices, near(): return lax.ppermute(v, 'dp', NEAR)  31.4 us
    all_to_all x2, starting transfers between devices, sent_back(): lax.all_to_all(parts, 'dp', 0, 0, axis_index_groups=GROUPS, tiled=True)  15.3 us
    ppermute x6, starting transfers between devices, swap(): return lax.ppermute(v, axis, [(i, i ^ bit) for i in range(count)])  13.8 us
    ppermute x12, starting transfers between devices, near(): return lax.ppermute(v, 'dp', NEAR)  12.2 us
    ppermute x6, waiting for transfers between devices, swap(): return lax.ppermute(v, axis, [(i, i ^ bit) for i in range(count)])  11.2 us
    ppermute x4, starting transfers between devices, far(): return lax.ppermute(v, 'dp', FAR)  8.18 us
    unnamed x24, local copies, waits for them, and re-layouts  7.63 us
    pallas_call x2, Pallas kernels, second_product(): call(body, [pltpu.HBM((dests, 8 * part + 8 * which, 128), jnp.float32), f...  7.44 us
  transfers between devices with their start and end apart: 27, of which 17 were waited for; matrix products, arithmetic and copies ran while one was open for 1% of the time, Pallas kernels for 19%

profile of v4, /device:TPU:6, one launch (start us, length us, event | category | flops | bytes accessed | tf_op | source)
XLA Modules:
  0.0 144.0 jit_solution(8845419070392465034)
XLA Ops:
  0.6 2.5 %shard_map.93 = (f32[192,1024]{1,0:T(8,128)S(1)}, f32[64,1024]{1,0:T(8,128)S(1)}, f32[128,1024]{1,0:T(8,128)S(1)}, f32[128,1024]{1,0:T(8,128)S(1)}, f32[128,1024]{1,0:T(8,128)S(1)}) custom-call(s32[1,8]{1,0:T(1,128)} %owner_ref.3, f32[64,8192]{1,0:T(8,128)} %g_ref.3, f32[1024,1024]{1,0:T(8,128)} %bitcast.3), custom_call_target="tpu_custom_call" | custom-call | bytes 4194304 | tf_op jit(solution)/shard_map/pallas_call | solution.py:182
  13.7 3.9 %shard_map.94 = (f32[64,8192]{1,0:T(8,128)}, f32[64,8192]{1,0:T(8,128)}, f32[8,1024]{1,0:T(8,128)S(1)}) custom-call(f32[64,8192]{1,0:T(8,128)S(1)} %copy-done.1, f32[64,8192]{1,0:T(8,128)S(1)} %copy-done.7, f32[64,8192]{1,0:T(8,128)S(1)} %copy-done.8), custom_call_target="tpu_custom_call" | custom-call | bytes 12582912 | tf_op jit(solution)/shard_map/pallas_call | solution.py:215
  17.7 2.3 %collective-permute-start.4 = (f32[64,1024]{1,0:T(8,128)S(1)}, f32[64,1024]{1,0:T(8,128)S(1)}, u32[]{:S(2)}, u32[]{:S(2)}) collective-permute-start(f32[64,1024]{1,0:T(8,128)S(1)} %get-tuple-element.87), channel_id=1, source_target_pairs={{0,3},{1,2},{2,1},{3,0},{4,7},{5,6},{6,5},{7,4},{8,11},{9,10},{10,... | collective-permute-start | bytes 786440 | tf_op jit(solution)/shard_map/ppermute | solution.py:41
  25.1 3.0 %collective-permute-done.4.refs_5_ = f32[64,1024]{1,0:T(8,128)S(1)} collective-permute-done((f32[64,1024]{1,0:T(8,128)S(1)}, f32[64,1024]{1,0:T(8,128)S(1)}, u32[]{:S(2)}, u32[]{:S(2)}) %collective-permute-start.4) | collective-permute-done | bytes 262176 | tf_op jit(solution)/shard_map/ppermute | solution.py:41
  28.1 3.5 %collective-permute-done.6.refs_7_ = f32[64,1024]{1,0:T(8,128)S(1)} collective-permute-done((f32[64,1024]{1,0:T(8,128)S(1)}, f32[64,1024]{1,0:T(8,128)S(1)}, u32[]{:S(2)}, u32[]{:S(2)}) %collective-permute-start.6) | collective-permute-done | bytes 262176 | tf_op jit(solution)/shard_map/ppermute | solution.py:41
  33.5 4.4 %collective-permute-done.9.refs_12_ = f32[64,1024]{1,0:T(8,128)S(1)} collective-permute-done((f32[64,1024]{1,0:T(8,128)S(1)}, f32[64,1024]{1,0:T(8,128)S(1)}, u32[]{:S(2)}, u32[]{:S(2)}) %collective-permute-start.9) | collective-permute-done | bytes 262176 | tf_op jit(solution)/shard_map/ppermute | solution.py:37
  50.4 4.4 %collective-permute-done.13.refs_15_ = f32[64,1024]{1,0:T(8,128)S(1)} collective-permute-done((f32[64,1024]{1,0:T(8,128)S(1)}, f32[64,1024]{1,0:T(8,128)S(1)}, u32[]{:S(2)}, u32[]{:S(2)}) %collective-permute-start.13) | collective-permute-done | bytes 262176 | tf_op jit(solution)/shard_map/ppermute | solution.py:37
  56.0 4.3 %collective-permute-done.11.refs_10_ = f32[64,1024]{1,0:T(8,128)S(1)} collective-permute-done((f32[64,1024]{1,0:T(8,128)S(1)}, f32[64,1024]{1,0:T(8,128)S(1)}, u32[]{:S(2)}, u32[]{:S(2)}) %collective-permute-start.11) | collective-permute-done | bytes 262176 | tf_op jit(solution)/shard_map/ppermute | solution.py:37
  60.3 2.8 %collective-permute-done.14.refs_14_ = f32[64,1024]{1,0:T(8,128)S(1)} collective-permute-done((f32[64,1024]{1,0:T(8,128)S(1)}, f32[64,1024]{1,0:T(8,128)S(1)}, u32[]{:S(2)}, u32[]{:S(2)}) %collective-permute-start.14) | collective-permute-done | bytes 262176 | tf_op jit(solution)/shard_map/ppermute | solution.py:37
  65.2 4.9 %shard_map.97 = (bf16[1024,1024]{1,0:T(8,128)(2,1)S(1)}, bf16[1024,1024]{1,0:T(8,128)(2,1)S(1)}, bf16[1024,1024]{1,0:T(8,128)(2,1)S(1)}, bf16[1024,1024]{1,0:T(8,128)(2,1)S(1)}) custom-call(f32[192,1024]{1,0:T(8,128)S(1)} %copy-done.10, f32[128,1024]{1,0:T(8,128)S(1)} %collective-permute-done.refs_1_, f32[128,1024]{1,0:T(8,128)S(1)} %collective-permute-done.3.refs_2_, ...), custom_call_target="tpu_custom_call" | custom-call | bytes 1048576 | tf_op jit(solution)/shard_map/pallas_call | solution.py:369
  70.0 7.0 %shard_map.98 = (f32[1024,1024]{1,0:T(8,128)}, f32[8,128]{1,0:T(8,128)S(1)}) custom-call(bf16[1024,1024]{1,0:T(8,128)(2,1)S(1)} %get-tuple-element.64.gh_ref, bf16[1024,1024]{1,0:T(8,128)(2,1)S(1)} %get-tuple-element.65.gl_ref, f32[1024,1024]{1,0:T(8,128)S(1)} %bitcast.6), custom_call_target="tpu_custom_call" | custom-call | bytes 1048576 | tf_op jit(solution)/shard_map/pallas_call | solution.py:525
  78.7 2.4 %collective-permute-done.16 = f32[8,1024]{1,0:T(8,128)S(1)} collective-permute-done((f32[8,1024]{1,0:T(8,128)S(1)}, f32[8,1024]{1,0:T(8,128)S(1)}, u32[]{:S(2)}, u32[]{:S(2)}) %collective-permute-start.16) | collective-permute-done | bytes 32800 | tf_op jit(solution)/shard_map/ppermute | solution.py:54
  81.1 2.4 %collective-permute-start.17 = (f32[8,1024]{1,0:T(8,128)S(1)}, f32[8,1024]{1,0:T(8,128)S(1)}, u32[]{:S(2)}, u32[]{:S(2)}) collective-permute-start(f32[8,1024]{1,0:T(8,128)S(1)} %add.24), channel_id=1, source_target_pairs={{0,8},{1,9},{2,10},{3,11},{4,12},{5,13},{6,14},{7,15},{8,0},{9,1},... | collective-permute-start | bytes 98312 | tf_op jit(solution)/shard_map/ppermute | solution.py:54
  83.5 3.0 %collective-permute-done.17 = f32[8,1024]{1,0:T(8,128)S(1)} collective-permute-done((f32[8,1024]{1,0:T(8,128)S(1)}, f32[8,1024]{1,0:T(8,128)S(1)}, u32[]{:S(2)}, u32[]{:S(2)}) %collective-permute-start.17) | collective-permute-done | bytes 32800 | tf_op jit(solution)/shard_map/ppermute | solution.py:54
  86.5 3.4 %collective-permute-done.15.refs_3_ = f32[264,1024]{1,0:T(8,128)S(1)} collective-permute-done((f32[264,1024]{1,0:T(8,128)S(1)}, f32[264,1024]{1,0:T(8,128)S(1)}, u32[]{:S(2)}, u32[]{:S(2)}) %collective-permute-start.15) | collective-permute-done | bytes 1081376 | tf_op jit(solution)/shard_map/ppermute | solution.py:37
  89.9 3.8 %shard_map.99 = (f32[8,256,128]{2,1,0:T(8,128)}, f32[8,128]{1,0:T(8,128)S(1)}) custom-call(bf16[1024,1024]{1,0:T(8,128)(2,1)S(1)} %get-tuple-element.61.refs_0_, bf16[1024,1024]{1,0:T(8,128)(2,1)S(1)} %get-tuple-element.62.refs_1_, f32[192,1024]{1,0:T(8,128)S(1)} %collective-permute-done.7.refs_8_.refs_2_, f32[264,1024]{1,0:T(8,128)S(1)} %collective-permute-done.15.refs_3_, ...), custom_call_target="tpu_custom_call" | custom-call | tf_op jit(solution)/shard_map/pallas_call | solution.py:474
  93.8 4.0 %collective-permute-start.19 = (f32[8,1024]{1,0:T(8,128)S(1)}, f32[8,1024]{1,0:T(8,128)S(1)}, u32[]{:S(2)}, u32[]{:S(2)}) collective-permute-start(f32[8,1024]{1,0:T(8,128)S(1)} %add.25), channel_id=1, source_target_pairs={{0,3},{1,2},{2,1},{3,0},{4,7},{5,6},{6,5},{7,4},{8,11},{9,10},{10,... | collective-permute-start | bytes 98312 | tf_op jit(solution)/shard_map/ppermute | solution.py:54
  99.7 8.4 %all-to-all-start = ((f32[8,256,128]{2,1,0:T(8,128)}), f32[8,256,128]{2,1,0:T(8,128)}, u32[]{:S(2)}, u32[]{:S(2)}) async-start(f32[8,256,128]{2,1,0:T(8,128)} %get-tuple-element.73), calls=%async_computation | async-start | bytes 2097152 | tf_op jit(solution)/shard_map/all_to_all | solution.py:596
  110.9 3.6 %shard_map.100 = (f32[8,264,128]{2,1,0:T(8,128)}, f32[8,128]{1,0:T(8,128)S(1)}) custom-call(bf16[1024,1024]{1,0:T(8,128)(2,1)S(1)} %get-tuple-element.61.refs_0_, bf16[1024,1024]{1,0:T(8,128)(2,1)S(1)} %copy-done.3, f32[192,1024]{1,0:T(8,128)S(1)} %collective-permute-done.7.refs_8_.refs_2_, f32[264,1024]{1,0:T(8,128)S(1)} %copy-done.5, ...), custom_call_target="tpu_custom_call" | custom-call | tf_op jit(solution)/shard_map/pallas_call | solution.py:474
  114.6 3.6 %collective-permute-done.20 = f32[8,128]{1,0:T(8,128)S(1)} collective-permute-done((f32[8,128]{1,0:T(8,128)S(1)}, f32[8,128]{1,0:T(8,128)S(1)}, u32[]{:S(2)}, u32[]{:S(2)}) %collective-permute-start.20) | collective-permute-done | bytes 4128 | tf_op jit(solution)/shard_map/ppermute | solution.py:37
  120.1 6.9 %all-to-all-start.1 = ((f32[8,264,128]{2,1,0:T(8,128)}), f32[8,264,128]{2,1,0:T(8,128)S(1)}, u32[]{:S(2)}, u32[]{:S(2)}) async-start(f32[8,264,128]{2,1,0:T(8,128)} %shard_map.101), calls=%async_computation.1 | async-start | bytes 2162688 | tf_op jit(solution)/shard_map/all_to_all | solution.py:596
  130.9 3.9 %collective-permute-start.23 = (f32[8,1024]{1,0:T(8,128)S(1)}, f32[8,1024]{1,0:T(8,128)S(1)}, u32[]{:S(2)}, u32[]{:S(2)}) collective-permute-start(f32[8,1024]{1,0:T(8,128)S(1)} %add.29), channel_id=1, source_target_pairs={{0,64},{16,80},{32,96},{48,112},{64,0},{80,16},{96,32},{112,48},{1... | collective-permute-start | bytes 98312 | tf_op jit(solution)/shard_map/ppermute | solution.py:54
  136.9 4.3 %collective-permute-done.24 = f32[16,1024]{1,0:T(8,128)S(1)} collective-permute-done((f32[16,1024]{1,0:T(8,128)S(1)}, f32[16,1024]{1,0:T(8,128)S(1)}, u32[]{:S(2)}, u32[]{:S(2)}) %collective-permute-start.24) | collective-permute-done | bytes 65568 | tf_op jit(solution)/shard_map/ppermute | solution.py:37
  141.2 2.8 %shard_map.102 = f32[64,8192]{1,0:T(8,128)} custom-call(s32[1,8]{1,0:T(1,128)S(1)} %copy-done.11, f32[8,256,128]{2,1,0:T(8,128)} %all-to-all-done.first_ref, f32[8,264,128]{2,1,0:T(8,128)S(1)} %all-to-all-done.1.second_ref, f32[8,1024]{1,0:T(8,128)S(1)} %get-tuple-element.89.sums_ref, f32[8,1024]{1,0:T(8,128)S(1)} %get-tuple-element.88.totals_ref), custom_call_target="tpu_custom_call" | custom-call | bytes 4194304 | tf_op jit(solution)/shard_map/pallas_call | solution.py:567
  (77 shorter events, 47.7 us)
Async XLA Ops:
  3.1 14.6 %collective-permute-start = (f32[128,1024]{1,0:T(8,128)S(1)}, f32[128,1024]{1,0:T(8,128)S(1)}, u32[]{:S(2)}, u32[]{:S(2)}) collective-permute-start(f32[128,1024]{1,0:T(8,128)S(1)} %get-tuple-element.44), channel_id=1, source_target_pairs={{0,4},{1,5},{2,6},{3,7},{4,8},{5,9},{6,10},{7,11},{8,12},{9,13},{1... | collective-permute-start | bytes 1572872 | tf_op jit(solution)/shard_map/ppermute | solution.py:45
  3.6 19.5 %collective-permute-start.7 = (f32[192,1024]{1,0:T(8,128)S(1)}, f32[192,1024]{1,0:T(8,128)S(1)}, u32[]{:S(2)}, u32[]{:S(2)}) collective-permute-start(f32[192,1024]{1,0:T(8,128)S(1)} %get-tuple-element.43.refs_0_), channel_id=1, source_target_pairs={{0,1},{1,0},{2,3},{3,2},{4,5},{5,4},{6,7},{7,6},{8,9},{9,8},{10,11... | collective-permute-start | bytes 2359304 | tf_op jit(solution)/shard_map/ppermute | solution.py:37
  5.3 14.7 %collective-permute-start.2 = (f32[128,1024]{1,0:T(8,128)S(1)}, f32[128,1024]{1,0:T(8,128)S(1)}, u32[]{:S(2)}, u32[]{:S(2)}) collective-permute-start(f32[128,1024]{1,0:T(8,128)S(1)} %get-tuple-element.47), channel_id=1, source_target_pairs={{0,12},{1,13},{2,14},{3,15},{4,0},{5,1},{6,2},{7,3},{8,4},{9,5},{1... | collective-permute-start | bytes 1572872 | tf_op jit(solution)/shard_map/ppermute | solution.py:45
  6.8 13.2 %collective-permute-start.1 = (f32[64,1024]{1,0:T(8,128)S(1)}, f32[64,1024]{1,0:T(8,128)S(1)}, u32[]{:S(2)}, u32[]{:S(2)}) collective-permute-start(f32[64,1024]{1,0:T(8,128)S(1)} %get-tuple-element.46), channel_id=1, source_target_pairs={{0,3},{1,2},{2,1},{3,0},{4,7},{5,6},{6,5},{7,4},{8,11},{9,10},{10,... | collective-permute-start | bytes 786440 | tf_op jit(solution)/shard_map/ppermute | solution.py:41
  17.7 10.4 %collective-permute-start.4 = (f32[64,1024]{1,0:T(8,128)S(1)}, f32[64,1024]{1,0:T(8,128)S(1)}, u32[]{:S(2)}, u32[]{:S(2)}) collective-permute-start(f32[64,1024]{1,0:T(8,128)S(1)} %get-tuple-element.87), channel_id=1, source_target_pairs={{0,3},{1,2},{2,1},{3,0},{4,7},{5,6},{6,5},{7,4},{8,11},{9,10},{10,... | collective-permute-start | bytes 786440 | tf_op jit(solution)/shard_map/ppermute | solution.py:41
  20.0 17.9 %collective-permute-start.3 = (f32[128,1024]{1,0:T(8,128)S(1)}, f32[128,1024]{1,0:T(8,128)S(1)}, u32[]{:S(2)}, u32[]{:S(2)}) collective-permute-start(f32[128,1024]{1,0:T(8,128)S(1)} %get-tuple-element.49), channel_id=1, source_target_pairs={{0,8},{1,9},{2,10},{3,11},{4,12},{5,13},{6,14},{7,15},{8,0},{9,1},... | collective-permute-start | bytes 1572872 | tf_op jit(solution)/shard_map/ppermute | solution.py:45
  21.5 10.1 %collective-permute-start.6 = (f32[64,1024]{1,0:T(8,128)S(1)}, f32[64,1024]{1,0:T(8,128)S(1)}, u32[]{:S(2)}, u32[]{:S(2)}) collective-permute-start(f32[64,1024]{1,0:T(8,128)S(1)} %get-tuple-element.83), channel_id=1, source_target_pairs={{0,3},{1,2},{2,1},{3,0},{4,7},{5,6},{6,5},{7,4},{8,11},{9,10},{10,... | collective-permute-start | bytes 786440 | tf_op jit(solution)/shard_map/ppermute | solution.py:41
  23.1 9.2 %collective-permute-start.8 = (f32[64,1024]{1,0:T(8,128)S(1)}, f32[64,1024]{1,0:T(8,128)S(1)}, u32[]{:S(2)}, u32[]{:S(2)}) collective-permute-start(f32[64,1024]{1,0:T(8,128)S(1)} %get-tuple-element.50), channel_id=1, source_target_pairs={{0,1},{1,0},{2,3},{3,2},{4,5},{5,4},{6,7},{7,6},{8,9},{9,8},{10,11... | collective-permute-start | bytes 786440 | tf_op jit(solution)/shard_map/ppermute | solution.py:37
  24.3 13.6 %collective-permute-start.9 = (f32[64,1024]{1,0:T(8,128)S(1)}, f32[64,1024]{1,0:T(8,128)S(1)}, u32[]{:S(2)}, u32[]{:S(2)}) collective-permute-start(f32[64,1024]{1,0:T(8,128)S(1)} %collective-permute-done.1.refs_4_), channel_id=1, source_target_pairs={{0,1},{1,0},{2,3},{3,2},{4,5},{5,4},{6,7},{7,6},{8,9},{9,8},{10,11... | collective-permute-start | bytes 786440 | tf_op jit(solution)/shard_map/ppermute | solution.py:37
  32.3 11.2 %collective-permute-start.12 = (f32[64,1024]{1,0:T(8,128)S(1)}, f32[64,1024]{1,0:T(8,128)S(1)}, u32[]{:S(2)}, u32[]{:S(2)}) collective-permute-start(f32[64,1024]{1,0:T(8,128)S(1)} %get-tuple-element.57), channel_id=1, source_target_pairs={{0,1},{1,0},{2,3},{3,2},{4,5},{5,4},{6,7},{7,6},{8,9},{9,8},{10,11... | collective-permute-start | bytes 786440 | tf_op jit(solution)/shard_map/ppermute | solution.py:37
  37.9 11.2 %collective-permute-start.10 = (f32[64,1024]{1,0:T(8,128)S(1)}, f32[64,1024]{1,0:T(8,128)S(1)}, u32[]{:S(2)}, u32[]{:S(2)}) collective-permute-start(f32[64,1024]{1,0:T(8,128)S(1)} %collective-permute-done.4.refs_5_), channel_id=1, source_target_pairs={{0,1},{1,0},{2,3},{3,2},{4,5},{5,4},{6,7},{7,6},{8,9},{9,8},{10,11... | collective-permute-start | bytes 786440 | tf_op jit(solution)/shard_map/ppermute | solution.py:37
  39.2 9.9 %collective-permute-start.5 = (f32[64,1024]{1,0:T(8,128)S(1)}, f32[64,1024]{1,0:T(8,128)S(1)}, u32[]{:S(2)}, u32[]{:S(2)}) collective-permute-start(f32[64,1024]{1,0:T(8,128)S(1)} %get-tuple-element.85), channel_id=1, source_target_pairs={{0,3},{1,2},{2,1},{3,0},{4,7},{5,6},{6,5},{7,4},{8,11},{9,10},{10,... | collective-permute-start | bytes 786440 | tf_op jit(solution)/shard_map/ppermute | solution.py:41
  43.5 11.2 %collective-permute-start.13 = (f32[64,1024]{1,0:T(8,128)S(1)}, f32[64,1024]{1,0:T(8,128)S(1)}, u32[]{:S(2)}, u32[]{:S(2)}) collective-permute-start(f32[64,1024]{1,0:T(8,128)S(1)} %collective-permute-done.6.refs_7_), channel_id=1, source_target_pairs={{0,1},{1,0},{2,3},{3,2},{4,5},{5,4},{6,7},{7,6},{8,9},{9,8},{10,11... | collective-permute-start | bytes 786440 | tf_op jit(solution)/shard_map/ppermute | solution.py:37
  49.2 11.2 %collective-permute-start.11 = (f32[64,1024]{1,0:T(8,128)S(1)}, f32[64,1024]{1,0:T(8,128)S(1)}, u32[]{:S(2)}, u32[]{:S(2)}) collective-permute-start(f32[64,1024]{1,0:T(8,128)S(1)} %get-tuple-element.56), channel_id=1, source_target_pairs={{0,1},{1,0},{2,3},{3,2},{4,5},{5,4},{6,7},{7,6},{8,9},{9,8},{10,11... | collective-permute-start | bytes 786440 | tf_op jit(solution)/shard_map/ppermute | solution.py:37
  54.8 8.3 %collective-permute-start.14 = (f32[64,1024]{1,0:T(8,128)S(1)}, f32[64,1024]{1,0:T(8,128)S(1)}, u32[]{:S(2)}, u32[]{:S(2)}) collective-permute-start(f32[64,1024]{1,0:T(8,128)S(1)} %collective-permute-done.5.refs_6_), channel_id=1, source_target_pairs={{0,1},{1,0},{2,3},{3,2},{4,5},{5,4},{6,7},{7,6},{8,9},{9,8},{10,11... | collective-permute-start | bytes 786440 | tf_op jit(solution)/shard_map/ppermute | solution.py:37
  63.1 26.8 %collective-permute-start.15 = (f32[264,1024]{1,0:T(8,128)S(1)}, f32[264,1024]{1,0:T(8,128)S(1)}, u32[]{:S(2)}, u32[]{:S(2)}) collective-permute-start(f32[264,1024]{1,0:T(8,128)S(1)} %get-tuple-element.63), channel_id=1, source_target_pairs={{0,1},{1,0},{2,3},{3,2},{4,5},{5,4},{6,7},{7,6},{8,9},{9,8},{10,11... | collective-permute-start | bytes 3244040 | tf_op jit(solution)/shard_map/ppermute | solution.py:37
  64.9 34.8 %collective-permute-start.18 = (f32[136,1024]{1,0:T(8,128)S(1)}, f32[136,1024]{1,0:T(8,128)S(1)}, u32[]{:S(2)}, u32[]{:S(2)}) collective-permute-start(f32[136,1024]{1,0:T(8,128)S(1)} %get-tuple-element.70), channel_id=1, source_target_pairs={{0,1},{1,0},{2,3},{3,2},{4,5},{5,4},{6,7},{7,6},{8,9},{9,8},{10,11... | collective-permute-start | bytes 1671176 | tf_op jit(solution)/shard_map/ppermute | solution.py:37
  81.1 5.4 %collective-permute-start.17 = (f32[8,1024]{1,0:T(8,128)S(1)}, f32[8,1024]{1,0:T(8,128)S(1)}, u32[]{:S(2)}, u32[]{:S(2)}) collective-permute-start(f32[8,1024]{1,0:T(8,128)S(1)} %add.24), channel_id=1, source_target_pairs={{0,8},{1,9},{2,10},{3,11},{4,12},{5,13},{6,14},{7,15},{8,0},{9,1},... | collective-permute-start | bytes 98312 | tf_op jit(solution)/shard_map/ppermute | solution.py:54
  93.8 5.9 %collective-permute-start.19 = (f32[8,1024]{1,0:T(8,128)S(1)}, f32[8,1024]{1,0:T(8,128)S(1)}, u32[]{:S(2)}, u32[]{:S(2)}) collective-permute-start(f32[8,1024]{1,0:T(8,128)S(1)} %add.25), channel_id=1, source_target_pairs={{0,3},{1,2},{2,1},{3,0},{4,7},{5,6},{6,5},{7,4},{8,11},{9,10},{10,... | collective-permute-start | bytes 98312 | tf_op jit(solution)/shard_map/ppermute | solution.py:54
  99.7 20.4 %all-to-all-start = ((f32[8,256,128]{2,1,0:T(8,128)}), f32[8,256,128]{2,1,0:T(8,128)}, u32[]{:S(2)}, u32[]{:S(2)}) async-start(f32[8,256,128]{2,1,0:T(8,128)} %get-tuple-element.73), calls=%async_computation | async-start | bytes 2097152 | tf_op jit(solution)/shard_map/all_to_all | solution.py:596
  108.1 10.7 %collective-permute-start.21 = (f32[8,1024]{1,0:T(8,128)S(1)}, f32[8,1024]{1,0:T(8,128)S(1)}, u32[]{:S(2)}, u32[]{:S(2)}) collective-permute-start(f32[8,1024]{1,0:T(8,128)S(1)} %add.26), channel_id=1, source_target_pairs={{0,16},{16,0},{32,48},{48,32},{64,80},{80,64},{96,112},{112,96},{1... | collective-permute-start | bytes 98312 | tf_op jit(solution)/shard_map/ppermute | solution.py:54
  120.1 21.0 %all-to-all-start.1 = ((f32[8,264,128]{2,1,0:T(8,128)}), f32[8,264,128]{2,1,0:T(8,128)S(1)}, u32[]{:S(2)}, u32[]{:S(2)}) async-start(f32[8,264,128]{2,1,0:T(8,128)} %shard_map.101), calls=%async_computation.1 | async-start | bytes 2162688 | tf_op jit(solution)/shard_map/all_to_all | solution.py:596
  130.9 5.8 %collective-permute-start.23 = (f32[8,1024]{1,0:T(8,128)S(1)}, f32[8,1024]{1,0:T(8,128)S(1)}, u32[]{:S(2)}, u32[]{:S(2)}) collective-permute-start(f32[8,1024]{1,0:T(8,128)S(1)} %add.29), channel_id=1, source_target_pairs={{0,64},{16,80},{32,96},{48,112},{64,0},{80,16},{96,32},{112,48},{1... | collective-permute-start | bytes 98312 | tf_op jit(solution)/shard_map/ppermute | solution.py:54
  136.8 4.3 %collective-permute-start.24 = (f32[16,1024]{1,0:T(8,128)S(1)}, f32[16,1024]{1,0:T(8,128)S(1)}, u32[]{:S(2)}, u32[]{:S(2)}) collective-permute-start(f32[16,1024]{1,0:T(8,128)S(1)} %pad_maximum_fusion), channel_id=1, source_target_pairs={{0,1},{1,0},{2,3},{3,2},{4,5},{5,4},{6,7},{7,6},{8,9},{9,8},{10,11... | collective-permute-start | bytes 196616 | tf_op jit(solution)/shard_map/ppermute | solution.py:37
  (15 other events, 133.9 us)

commit v5 on v4

--- a/solution.py
+++ b/solution.py
@@ -230,8 +230,7 @@
     def body(root_ref, b_ref, c_ref, buf, sems):
         x, y, is_left, outer = spot()
         places = [(b_ref, 0), (b_ref, part), (c_ref, 0)]
-        for to_ref in (b_ref, c_ref):
-            to_ref[to_ref.shape[0] - 8 :, :] = jnp.zeros((8, order), jnp.float32)
+        b_ref[2 * part :, :] = jnp.zeros((8, order), jnp.float32)
 
         @pl.when(is_left)
         def _():
@@ -259,13 +258,13 @@
                 for h in range(2):
                     out_ref[at, h * half : h * half + quarter] = buf[i, h * part : (h + 1) * part, quarter:]
                     out_ref[at, h * half + quarter : (h + 1) * half] = both[h * part : (h + 1) * part]
-                out_ref[first + part : first + part + 1, :quarter] = jnp.sum(
+                b_ref[2 * part + i : 2 * part + i + 1, :quarter] = jnp.sum(
                     jnp.where(row == col, low, 0.0), axis=0, keepdims=True
                 )
 
     return call(
         body,
-        [f32(2 * part + 8, order), f32(part + 8, order)],
+        [f32(2 * part + 8, order), f32(part, order)],
         [HBM],
         [VMEM, VMEM],
         [pltpu.VMEM((2, half, half), jnp.float32), pltpu.SemaphoreType.DMA((6 * SIDE,))],
@@ -377,7 +376,7 @@
     )(*(piece for piece, _ in pieces), r_high, r_low)
 
 
-def unfold(c_ref, first, b_high, b_low, base):
+def unfold(c_ref, first, diag, b_high, b_low, base):
     half = c_ref.shape[1] // 2
     quarter = half // 2
     mid = quarter // 2
@@ -386,7 +385,6 @@
     at = slice(first, first + mid)
     cross = jnp.concatenate([c_ref[at, :quarter], c_ref[at, half : half + quarter]], axis=0)
     both = jnp.concatenate([c_ref[at, quarter:half], c_ref[at, half + quarter :]], axis=0)
-    diag = c_ref[first + mid : first + mid + 1, :quarter]
     turned = both.T
     top = jnp.where(row <= col, both, turned)
     low = jnp.where(row > col, both, jnp.where(row == col, diag, turned))
@@ -404,20 +402,10 @@
     few = part // 2
     count = len(chunks)
 
-    def body(*refs):
-        sources, sq_ref = refs[: 2 + count], refs[2 + count]
-        whole, sq_out, b_high, b_low, *buffers = refs[3 + count :]
-        sems = buffers.pop()
+    def body(high_ref, low_ref, *refs):
+        chunk_refs, sq_ref = refs[:count], refs[count]
+        whole, sq_out, b_high, b_low = refs[count + 1 :]
         x, y, is_left, outer = spot()
-        finish(
-            run(
-                [
-                    pltpu.make_async_copy(source, buffer, sems.at[i])
-                    for i, (source, buffer) in enumerate(zip(sources, buffers))
-                ]
-            )
-        )
-        high_ref, low_ref, *chunk_refs = buffers
         outs = []
         for k in range(dests):
             to_y = 3 - y if k % 2 else y
@@ -434,7 +422,9 @@
                     b_high[half:, at], b_low[half:, at] = split(mat.T)
                 else:
                     b_high[at, :], b_low[at, :] = split(mat)
-            unfold(*units[2 + which], b_high, b_low, half * which)
+            row = 2 * eighth + which
+            diag = chunk_refs[1][row : row + 1, :quarter]
+            unfold(*units[2 + which], diag, b_high, b_low, half * which)
             total = jnp.float32(0.0)
             for m in range(2):
                 at = slice(m * quarter, (m + 1) * quarter)
@@ -474,13 +464,12 @@
     return call(
         body,
         [pltpu.HBM((dests, 8 * part + 8 * which, 128), jnp.float32), f32(8, 128)],
-        [HBM] * (2 + count) + [VMEM],
+        [VMEM] * (3 + count),
         [VMEM] * 2,
-        [short, short]
-        + [pltpu.VMEM(v.shape, v.dtype) for v in (t_high, t_low, *chunks)]
-        + [pltpu.SemaphoreType.DMA((2 + count,))],
-        0,
-        0,
+        [short, short],
+        0,
+        0,
+        8,
     )(t_high, t_low, *chunks, squares)
 
 
@@ -530,7 +519,7 @@
         [short, short],
         0,
         order * order,
-        24,
+        14,
     )(g_high, g_low, stat)
 
 

time: 146 us -> 144 us (0.986)
  transfers between devices with their start and end apart: 27 -> 27, of which waited for: 17 -> 18; matrix products, arithmetic and copies ran while one was open for 1% -> 1% of each run, Pallas kernels for 19% -> 18%
where the time goes in v5:
time: 144 us; the launch traced here: 143 us
  starting transfers between devices  52.9 us (37%)
  waiting for transfers between devices  49 us (34%)
  Pallas kernels  31.6 us (22%)
  local copies, waits for them, and re-layouts  7.75 us (5%)
    ppermute x12, waiting for transfers between devices, near(): return lax.ppermute(v, 'dp', NEAR)  31.2 us
    all_to_all x2, starting transfers between devices, sent_back(): lax.all_to_all(parts, 'dp', 0, 0, axis_index_groups=GROUPS, tiled=True)  15.3 us
    ppermute x6, starting transfers between devices, swap(): return lax.ppermute(v, axis, [(i, i ^ bit) for i in range(count)])  13.6 us
    ppermute x12, starting transfers between devices, near(): return lax.ppermute(v, 'dp', NEAR)  12.4 us
    ppermute x6, waiting for transfers between devices, swap(): return lax.ppermute(v, axis, [(i, i ^ bit) for i in range(count)])  11.2 us
    ppermute x4, starting transfers between devices, far(): return lax.ppermute(v, 'dp', FAR)  8.17 us
    unnamed x24, local copies, waits for them, and re-layouts  7.63 us
    pallas_call x1, Pallas kernels, update_statistics(): call(body, [f32(order, order), f32(8, 128)], [VMEM, VMEM, VMEM], [VMEM, V...  6.97 us
  transfers between devices with their start and end apart: 27, of which 18 were waited for; matrix products, arithmetic and copies ran while one was open for 1% of the time, Pallas kernels for 18%

profile of v5, /device:TPU:6, one launch (start us, length us, event | category | flops | bytes accessed | tf_op | source)
XLA Modules:
  0.0 142.6 jit_solution(8935561740724455358)
XLA Ops:
  0.6 2.5 %shard_map.93 = (f32[192,1024]{1,0:T(8,128)S(1)}, f32[64,1024]{1,0:T(8,128)S(1)}, f32[128,1024]{1,0:T(8,128)S(1)}, f32[128,1024]{1,0:T(8,128)S(1)}, f32[128,1024]{1,0:T(8,128)S(1)}) custom-call(s32[1,8]{1,0:T(1,128)} %owner_ref.3, f32[64,8192]{1,0:T(8,128)} %g_ref.3, f32[1024,1024]{1,0:T(8,128)} %bitcast.3), custom_call_target="tpu_custom_call" | custom-call | bytes 4194304 | tf_op jit(solution)/shard_map/pallas_call | solution.py:182
  13.7 3.9 %shard_map.94 = (f32[64,8192]{1,0:T(8,128)}, f32[64,8192]{1,0:T(8,128)}, f32[8,1024]{1,0:T(8,128)S(1)}) custom-call(f32[64,8192]{1,0:T(8,128)S(1)} %copy-done.1, f32[64,8192]{1,0:T(8,128)S(1)} %copy-done.7, f32[64,8192]{1,0:T(8,128)S(1)} %copy-done.8), custom_call_target="tpu_custom_call" | custom-call | bytes 12582912 | tf_op jit(solution)/shard_map/pallas_call | solution.py:215
  17.7 2.3 %collective-permute-start.4 = (f32[64,1024]{1,0:T(8,128)S(1)}, f32[64,1024]{1,0:T(8,128)S(1)}, u32[]{:S(2)}, u32[]{:S(2)}) collective-permute-start(f32[64,1024]{1,0:T(8,128)S(1)} %get-tuple-element.87), channel_id=1, source_target_pairs={{0,3},{1,2},{2,1},{3,0},{4,7},{5,6},{6,5},{7,4},{8,11},{9,10},{10,... | collective-permute-start | bytes 786440 | tf_op jit(solution)/shard_map/ppermute | solution.py:41
  25.1 3.0 %collective-permute-done.4.refs_5_ = f32[64,1024]{1,0:T(8,128)S(1)} collective-permute-done((f32[64,1024]{1,0:T(8,128)S(1)}, f32[64,1024]{1,0:T(8,128)S(1)}, u32[]{:S(2)}, u32[]{:S(2)}) %collective-permute-start.4) | collective-permute-done | bytes 262176 | tf_op jit(solution)/shard_map/ppermute | solution.py:41
  28.1 3.5 %collective-permute-done.6.refs_7_ = f32[64,1024]{1,0:T(8,128)S(1)} collective-permute-done((f32[64,1024]{1,0:T(8,128)S(1)}, f32[64,1024]{1,0:T(8,128)S(1)}, u32[]{:S(2)}, u32[]{:S(2)}) %collective-permute-start.6) | collective-permute-done | bytes 262176 | tf_op jit(solution)/shard_map/ppermute | solution.py:41
  33.5 4.3 %collective-permute-done.9.refs_12_ = f32[64,1024]{1,0:T(8,128)S(1)} collective-permute-done((f32[64,1024]{1,0:T(8,128)S(1)}, f32[64,1024]{1,0:T(8,128)S(1)}, u32[]{:S(2)}, u32[]{:S(2)}) %collective-permute-start.9) | collective-permute-done | bytes 262176 | tf_op jit(solution)/shard_map/ppermute | solution.py:37
  50.4 4.3 %collective-permute-done.13.refs_15_ = f32[64,1024]{1,0:T(8,128)S(1)} collective-permute-done((f32[64,1024]{1,0:T(8,128)S(1)}, f32[64,1024]{1,0:T(8,128)S(1)}, u32[]{:S(2)}, u32[]{:S(2)}) %collective-permute-start.13) | collective-permute-done | bytes 262176 | tf_op jit(solution)/shard_map/ppermute | solution.py:37
  56.0 4.3 %collective-permute-done.11.refs_10_ = f32[64,1024]{1,0:T(8,128)S(1)} collective-permute-done((f32[64,1024]{1,0:T(8,128)S(1)}, f32[64,1024]{1,0:T(8,128)S(1)}, u32[]{:S(2)}, u32[]{:S(2)}) %collective-permute-start.11) | collective-permute-done | bytes 262176 | tf_op jit(solution)/shard_map/ppermute | solution.py:37
  60.3 2.8 %collective-permute-done.14.refs_14_ = f32[64,1024]{1,0:T(8,128)S(1)} collective-permute-done((f32[64,1024]{1,0:T(8,128)S(1)}, f32[64,1024]{1,0:T(8,128)S(1)}, u32[]{:S(2)}, u32[]{:S(2)}) %collective-permute-start.14) | collective-permute-done | bytes 262176 | tf_op jit(solution)/shard_map/ppermute | solution.py:37
  65.2 4.8 %shard_map.97 = (bf16[1024,1024]{1,0:T(8,128)(2,1)S(1)}, bf16[1024,1024]{1,0:T(8,128)(2,1)S(1)}, bf16[1024,1024]{1,0:T(8,128)(2,1)S(1)}, bf16[1024,1024]{1,0:T(8,128)(2,1)S(1)}) custom-call(f32[192,1024]{1,0:T(8,128)S(1)} %copy-done.10, f32[128,1024]{1,0:T(8,128)S(1)} %collective-permute-done.refs_1_, f32[128,1024]{1,0:T(8,128)S(1)} %collective-permute-done.3.refs_2_, ...), custom_call_target="tpu_custom_call" | custom-call | bytes 1048576 | tf_op jit(solution)/shard_map/pallas_call | solution.py:368
  70.0 7.0 %shard_map.98 = (f32[1024,1024]{1,0:T(8,128)}, f32[8,128]{1,0:T(8,128)S(1)}) custom-call(bf16[1024,1024]{1,0:T(8,128)(2,1)S(1)} %get-tuple-element.64.gh_ref, bf16[1024,1024]{1,0:T(8,128)(2,1)S(1)} %get-tuple-element.65.gl_ref, f32[1024,1024]{1,0:T(8,128)S(1)} %bitcast.6), custom_call_target="tpu_custom_call" | custom-call | bytes 1048576 | tf_op jit(solution)/shard_map/pallas_call | solution.py:514
  78.6 2.4 %collective-permute-done.16 = f32[8,1024]{1,0:T(8,128)S(1)} collective-permute-done((f32[8,1024]{1,0:T(8,128)S(1)}, f32[8,1024]{1,0:T(8,128)S(1)}, u32[]{:S(2)}, u32[]{:S(2)}) %collective-permute-start.16) | collective-permute-done | bytes 32800 | tf_op jit(solution)/shard_map/ppermute | solution.py:54
  81.0 2.4 %collective-permute-start.17 = (f32[8,1024]{1,0:T(8,128)S(1)}, f32[8,1024]{1,0:T(8,128)S(1)}, u32[]{:S(2)}, u32[]{:S(2)}) collective-permute-start(f32[8,1024]{1,0:T(8,128)S(1)} %add.24), channel_id=1, source_target_pairs={{0,8},{1,9},{2,10},{3,11},{4,12},{5,13},{6,14},{7,15},{8,0},{9,1},... | collective-permute-start | bytes 98312 | tf_op jit(solution)/shard_map/ppermute | solution.py:54
  83.4 3.0 %collective-permute-done.17 = f32[8,1024]{1,0:T(8,128)S(1)} collective-permute-done((f32[8,1024]{1,0:T(8,128)S(1)}, f32[8,1024]{1,0:T(8,128)S(1)}, u32[]{:S(2)}, u32[]{:S(2)}) %collective-permute-start.17) | collective-permute-done | bytes 32800 | tf_op jit(solution)/shard_map/ppermute | solution.py:54
  86.4 3.5 %collective-permute-done.15.refs_1_ = f32[264,1024]{1,0:T(8,128)S(1)} collective-permute-done((f32[264,1024]{1,0:T(8,128)S(1)}, f32[264,1024]{1,0:T(8,128)S(1)}, u32[]{:S(2)}, u32[]{:S(2)}) %collective-permute-start.15) | collective-permute-done | bytes 1081376 | tf_op jit(solution)/shard_map/ppermute | solution.py:37
  89.9 3.3 %shard_map.99 = (f32[8,256,128]{2,1,0:T(8,128)}, f32[8,128]{1,0:T(8,128)S(1)}) custom-call(bf16[1024,1024]{1,0:T(8,128)(2,1)S(1)} %get-tuple-element.61.high_ref, bf16[1024,1024]{1,0:T(8,128)(2,1)S(1)} %get-tuple-element.62.low_ref, f32[192,1024]{1,0:T(8,128)S(1)} %collective-permute-done.7.refs_8_.refs_0_, f32[264,1024]{1,0:T(8,128)S(1)} %collective-permute-done.15.refs_1_, ...), custom_call_target="tpu_custom_call" | custom-call | tf_op jit(solution)/shard_map/pallas_call | solution.py:464
  93.3 3.7 %collective-permute-start.19 = (f32[8,1024]{1,0:T(8,128)S(1)}, f32[8,1024]{1,0:T(8,128)S(1)}, u32[]{:S(2)}, u32[]{:S(2)}) collective-permute-start(f32[8,1024]{1,0:T(8,128)S(1)} %add.25), channel_id=1, source_target_pairs={{0,3},{1,2},{2,1},{3,0},{4,7},{5,6},{6,5},{7,4},{8,11},{9,10},{10,... | collective-permute-start | bytes 98312 | tf_op jit(solution)/shard_map/ppermute | solution.py:54
  98.9 8.4 %all-to-all-start = ((f32[8,256,128]{2,1,0:T(8,128)}), f32[8,256,128]{2,1,0:T(8,128)}, u32[]{:S(2)}, u32[]{:S(2)}) async-start(f32[8,256,128]{2,1,0:T(8,128)} %get-tuple-element.73), calls=%async_computation | async-start | bytes 2097152 | tf_op jit(solution)/shard_map/all_to_all | solution.py:585
  110.1 3.0 %shard_map.100 = (f32[8,264,128]{2,1,0:T(8,128)}, f32[8,128]{1,0:T(8,128)S(1)}) custom-call(bf16[1024,1024]{1,0:T(8,128)(2,1)S(1)} %get-tuple-element.61.high_ref, bf16[1024,1024]{1,0:T(8,128)(2,1)S(1)} %copy-done.3, f32[192,1024]{1,0:T(8,128)S(1)} %collective-permute-done.7.refs_8_.refs_0_, f32[264,1024]{1,0:T(8,128)S(1)} %copy-done.5, ...), custom_call_target="tpu_custom_call" | custom-call | tf_op jit(solution)/shard_map/pallas_call | solution.py:464
  113.2 3.6 %collective-permute-done.20 = f32[8,128]{1,0:T(8,128)S(1)} collective-permute-done((f32[8,128]{1,0:T(8,128)S(1)}, f32[8,128]{1,0:T(8,128)S(1)}, u32[]{:S(2)}, u32[]{:S(2)}) %collective-permute-start.20) | collective-permute-done | bytes 4128 | tf_op jit(solution)/shard_map/ppermute | solution.py:37
  118.7 6.9 %all-to-all-start.1 = ((f32[8,264,128]{2,1,0:T(8,128)}), f32[8,264,128]{2,1,0:T(8,128)S(1)}, u32[]{:S(2)}, u32[]{:S(2)}) async-start(f32[8,264,128]{2,1,0:T(8,128)} %shard_map.101), calls=%async_computation.1 | async-start | bytes 2162688 | tf_op jit(solution)/shard_map/all_to_all | solution.py:585
  129.5 3.9 %collective-permute-start.23 = (f32[8,1024]{1,0:T(8,128)S(1)}, f32[8,1024]{1,0:T(8,128)S(1)}, u32[]{:S(2)}, u32[]{:S(2)}) collective-permute-start(f32[8,1024]{1,0:T(8,128)S(1)} %add.29), channel_id=1, source_target_pairs={{0,64},{16,80},{32,96},{48,112},{64,0},{80,16},{96,32},{112,48},{1... | collective-permute-start | bytes 98312 | tf_op jit(solution)/shard_map/ppermute | solution.py:54
  135.4 4.3 %collective-permute-done.24 = f32[16,1024]{1,0:T(8,128)S(1)} collective-permute-done((f32[16,1024]{1,0:T(8,128)S(1)}, f32[16,1024]{1,0:T(8,128)S(1)}, u32[]{:S(2)}, u32[]{:S(2)}) %collective-permute-start.24) | collective-permute-done | bytes 65568 | tf_op jit(solution)/shard_map/ppermute | solution.py:37
  139.8 2.8 %shard_map.102 = f32[64,8192]{1,0:T(8,128)} custom-call(s32[1,8]{1,0:T(1,128)S(1)} %copy-done.11, f32[8,256,128]{2,1,0:T(8,128)} %all-to-all-done.first_ref, f32[8,264,128]{2,1,0:T(8,128)S(1)} %all-to-all-done.1.second_ref, f32[8,1024]{1,0:T(8,128)S(1)} %get-tuple-element.89.sums_ref, f32[8,1024]{1,0:T(8,128)S(1)} %get-tuple-element.88.totals_ref), custom_call_target="tpu_custom_call" | custom-call | bytes 4194304 | tf_op jit(solution)/shard_map/pallas_call | solution.py:556
  (77 shorter events, 47.9 us)
Async XLA Ops:
  3.1 14.6 %collective-permute-start = (f32[128,1024]{1,0:T(8,128)S(1)}, f32[128,1024]{1,0:T(8,128)S(1)}, u32[]{:S(2)}, u32[]{:S(2)}) collective-permute-start(f32[128,1024]{1,0:T(8,128)S(1)} %get-tuple-element.44), channel_id=1, source_target_pairs={{0,4},{1,5},{2,6},{3,7},{4,8},{5,9},{6,10},{7,11},{8,12},{9,13},{1... | collective-permute-start | bytes 1572872 | tf_op jit(solution)/shard_map/ppermute | solution.py:45
  3.6 19.5 %collective-permute-start.7 = (f32[192,1024]{1,0:T(8,128)S(1)}, f32[192,1024]{1,0:T(8,128)S(1)}, u32[]{:S(2)}, u32[]{:S(2)}) collective-permute-start(f32[192,1024]{1,0:T(8,128)S(1)} %get-tuple-element.43.refs_0_), channel_id=1, source_target_pairs={{0,1},{1,0},{2,3},{3,2},{4,5},{5,4},{6,7},{7,6},{8,9},{9,8},{10,11... | collective-permute-start | bytes 2359304 | tf_op jit(solution)/shard_map/ppermute | solution.py:37
  5.3 14.8 %collective-permute-start.2 = (f32[128,1024]{1,0:T(8,128)S(1)}, f32[128,1024]{1,0:T(8,128)S(1)}, u32[]{:S(2)}, u32[]{:S(2)}) collective-permute-start(f32[128,1024]{1,0:T(8,128)S(1)} %get-tuple-element.47), channel_id=1, source_target_pairs={{0,12},{1,13},{2,14},{3,15},{4,0},{5,1},{6,2},{7,3},{8,4},{9,5},{1... | collective-permute-start | bytes 1572872 | tf_op jit(solution)/shard_map/ppermute | solution.py:45
  6.8 13.2 %collective-permute-start.1 = (f32[64,1024]{1,0:T(8,128)S(1)}, f32[64,1024]{1,0:T(8,128)S(1)}, u32[]{:S(2)}, u32[]{:S(2)}) collective-permute-start(f32[64,1024]{1,0:T(8,128)S(1)} %get-tuple-element.46), channel_id=1, source_target_pairs={{0,3},{1,2},{2,1},{3,0},{4,7},{5,6},{6,5},{7,4},{8,11},{9,10},{10,... | collective-permute-start | bytes 786440 | tf_op jit(solution)/shard_map/ppermute | solution.py:41
  17.7 10.3 %collective-permute-start.4 = (f32[64,1024]{1,0:T(8,128)S(1)}, f32[64,1024]{1,0:T(8,128)S(1)}, u32[]{:S(2)}, u32[]{:S(2)}) collective-permute-start(f32[64,1024]{1,0:T(8,128)S(1)} %get-tuple-element.87), channel_id=1, source_target_pairs={{0,3},{1,2},{2,1},{3,0},{4,7},{5,6},{6,5},{7,4},{8,11},{9,10},{10,... | collective-permute-start | bytes 786440 | tf_op jit(solution)/shard_map/ppermute | solution.py:41
  20.1 17.8 %collective-permute-start.3 = (f32[128,1024]{1,0:T(8,128)S(1)}, f32[128,1024]{1,0:T(8,128)S(1)}, u32[]{:S(2)}, u32[]{:S(2)}) collective-permute-start(f32[128,1024]{1,0:T(8,128)S(1)} %get-tuple-element.49), channel_id=1, source_target_pairs={{0,8},{1,9},{2,10},{3,11},{4,12},{5,13},{6,14},{7,15},{8,0},{9,1},... | collective-permute-start | bytes 1572872 | tf_op jit(solution)/shard_map/ppermute | solution.py:45
  21.5 10.1 %collective-permute-start.6 = (f32[64,1024]{1,0:T(8,128)S(1)}, f32[64,1024]{1,0:T(8,128)S(1)}, u32[]{:S(2)}, u32[]{:S(2)}) collective-permute-start(f32[64,1024]{1,0:T(8,128)S(1)} %get-tuple-element.83), channel_id=1, source_target_pairs={{0,3},{1,2},{2,1},{3,0},{4,7},{5,6},{6,5},{7,4},{8,11},{9,10},{10,... | collective-permute-start | bytes 786440 | tf_op jit(solution)/shard_map/ppermute | solution.py:41
  23.1 9.2 %collective-permute-start.8 = (f32[64,1024]{1,0:T(8,128)S(1)}, f32[64,1024]{1,0:T(8,128)S(1)}, u32[]{:S(2)}, u32[]{:S(2)}) collective-permute-start(f32[64,1024]{1,0:T(8,128)S(1)} %get-tuple-element.50), channel_id=1, source_target_pairs={{0,1},{1,0},{2,3},{3,2},{4,5},{5,4},{6,7},{7,6},{8,9},{9,8},{10,11... | collective-permute-start | bytes 786440 | tf_op jit(solution)/shard_map/ppermute | solution.py:37
  24.3 13.6 %collective-permute-start.9 = (f32[64,1024]{1,0:T(8,128)S(1)}, f32[64,1024]{1,0:T(8,128)S(1)}, u32[]{:S(2)}, u32[]{:S(2)}) collective-permute-start(f32[64,1024]{1,0:T(8,128)S(1)} %collective-permute-done.1.refs_4_), channel_id=1, source_target_pairs={{0,1},{1,0},{2,3},{3,2},{4,5},{5,4},{6,7},{7,6},{8,9},{9,8},{10,11... | collective-permute-start | bytes 786440 | tf_op jit(solution)/shard_map/ppermute | solution.py:37
  32.2 11.2 %collective-permute-start.12 = (f32[64,1024]{1,0:T(8,128)S(1)}, f32[64,1024]{1,0:T(8,128)S(1)}, u32[]{:S(2)}, u32[]{:S(2)}) collective-permute-start(f32[64,1024]{1,0:T(8,128)S(1)} %get-tuple-element.57), channel_id=1, source_target_pairs={{0,1},{1,0},{2,3},{3,2},{4,5},{5,4},{6,7},{7,6},{8,9},{9,8},{10,11... | collective-permute-start | bytes 786440 | tf_op jit(solution)/shard_map/ppermute | solution.py:37
  37.9 11.2 %collective-permute-start.10 = (f32[64,1024]{1,0:T(8,128)S(1)}, f32[64,1024]{1,0:T(8,128)S(1)}, u32[]{:S(2)}, u32[]{:S(2)}) collective-permute-start(f32[64,1024]{1,0:T(8,128)S(1)} %collective-permute-done.4.refs_5_), channel_id=1, source_target_pairs={{0,1},{1,0},{2,3},{3,2},{4,5},{5,4},{6,7},{7,6},{8,9},{9,8},{10,11... | collective-permute-start | bytes 786440 | tf_op jit(solution)/shard_map/ppermute | solution.py:37
  39.2 9.9 %collective-permute-start.5 = (f32[64,1024]{1,0:T(8,128)S(1)}, f32[64,1024]{1,0:T(8,128)S(1)}, u32[]{:S(2)}, u32[]{:S(2)}) collective-permute-start(f32[64,1024]{1,0:T(8,128)S(1)} %get-tuple-element.85), channel_id=1, source_target_pairs={{0,3},{1,2},{2,1},{3,0},{4,7},{5,6},{6,5},{7,4},{8,11},{9,10},{10,... | collective-permute-start | bytes 786440 | tf_op jit(solution)/shard_map/ppermute | solution.py:41
  43.5 11.2 %collective-permute-start.13 = (f32[64,1024]{1,0:T(8,128)S(1)}, f32[64,1024]{1,0:T(8,128)S(1)}, u32[]{:S(2)}, u32[]{:S(2)}) collective-permute-start(f32[64,1024]{1,0:T(8,128)S(1)} %collective-permute-done.6.refs_7_), channel_id=1, source_target_pairs={{0,1},{1,0},{2,3},{3,2},{4,5},{5,4},{6,7},{7,6},{8,9},{9,8},{10,11... | collective-permute-start | bytes 786440 | tf_op jit(solution)/shard_map/ppermute | solution.py:37
  49.1 11.2 %collective-permute-start.11 = (f32[64,1024]{1,0:T(8,128)S(1)}, f32[64,1024]{1,0:T(8,128)S(1)}, u32[]{:S(2)}, u32[]{:S(2)}) collective-permute-start(f32[64,1024]{1,0:T(8,128)S(1)} %get-tuple-element.56), channel_id=1, source_target_pairs={{0,1},{1,0},{2,3},{3,2},{4,5},{5,4},{6,7},{7,6},{8,9},{9,8},{10,11... | collective-permute-start | bytes 786440 | tf_op jit(solution)/shard_map/ppermute | solution.py:37
  54.7 8.4 %collective-permute-start.14 = (f32[64,1024]{1,0:T(8,128)S(1)}, f32[64,1024]{1,0:T(8,128)S(1)}, u32[]{:S(2)}, u32[]{:S(2)}) collective-permute-start(f32[64,1024]{1,0:T(8,128)S(1)} %collective-permute-done.5.refs_6_), channel_id=1, source_target_pairs={{0,1},{1,0},{2,3},{3,2},{4,5},{5,4},{6,7},{7,6},{8,9},{9,8},{10,11... | collective-permute-start | bytes 786440 | tf_op jit(solution)/shard_map/ppermute | solution.py:37
  63.1 26.8 %collective-permute-start.15 = (f32[264,1024]{1,0:T(8,128)S(1)}, f32[264,1024]{1,0:T(8,128)S(1)}, u32[]{:S(2)}, u32[]{:S(2)}) collective-permute-start(f32[264,1024]{1,0:T(8,128)S(1)} %get-tuple-element.63), channel_id=1, source_target_pairs={{0,1},{1,0},{2,3},{3,2},{4,5},{5,4},{6,7},{7,6},{8,9},{9,8},{10,11... | collective-permute-start | bytes 3244040 | tf_op jit(solution)/shard_map/ppermute | solution.py:37
  64.9 34.1 %collective-permute-start.18 = (f32[128,1024]{1,0:T(8,128)S(1)}, f32[128,1024]{1,0:T(8,128)S(1)}, u32[]{:S(2)}, u32[]{:S(2)}) collective-permute-start(f32[128,1024]{1,0:T(8,128)S(1)} %get-tuple-element.70), channel_id=1, source_target_pairs={{0,1},{1,0},{2,3},{3,2},{4,5},{5,4},{6,7},{7,6},{8,9},{9,8},{10,11... | collective-permute-start | bytes 1572872 | tf_op jit(solution)/shard_map/ppermute | solution.py:37
  81.0 5.4 %collective-permute-start.17 = (f32[8,1024]{1,0:T(8,128)S(1)}, f32[8,1024]{1,0:T(8,128)S(1)}, u32[]{:S(2)}, u32[]{:S(2)}) collective-permute-start(f32[8,1024]{1,0:T(8,128)S(1)} %add.24), channel_id=1, source_target_pairs={{0,8},{1,9},{2,10},{3,11},{4,12},{5,13},{6,14},{7,15},{8,0},{9,1},... | collective-permute-start | bytes 98312 | tf_op jit(solution)/shard_map/ppermute | solution.py:54
  93.3 5.6 %collective-permute-start.19 = (f32[8,1024]{1,0:T(8,128)S(1)}, f32[8,1024]{1,0:T(8,128)S(1)}, u32[]{:S(2)}, u32[]{:S(2)}) collective-permute-start(f32[8,1024]{1,0:T(8,128)S(1)} %add.25), channel_id=1, source_target_pairs={{0,3},{1,2},{2,1},{3,0},{4,7},{5,6},{6,5},{7,4},{8,11},{9,10},{10,... | collective-permute-start | bytes 98312 | tf_op jit(solution)/shard_map/ppermute | solution.py:54
  98.9 19.8 %all-to-all-start = ((f32[8,256,128]{2,1,0:T(8,128)}), f32[8,256,128]{2,1,0:T(8,128)}, u32[]{:S(2)}, u32[]{:S(2)}) async-start(f32[8,256,128]{2,1,0:T(8,128)} %get-tuple-element.73), calls=%async_computation | async-start | bytes 2097152 | tf_op jit(solution)/shard_map/all_to_all | solution.py:585
  107.3 10.1 %collective-permute-start.21 = (f32[8,1024]{1,0:T(8,128)S(1)}, f32[8,1024]{1,0:T(8,128)S(1)}, u32[]{:S(2)}, u32[]{:S(2)}) collective-permute-start(f32[8,1024]{1,0:T(8,128)S(1)} %add.26), channel_id=1, source_target_pairs={{0,16},{16,0},{32,48},{48,32},{64,80},{80,64},{96,112},{112,96},{1... | collective-permute-start | bytes 98312 | tf_op jit(solution)/shard_map/ppermute | solution.py:54
  118.7 21.1 %all-to-all-start.1 = ((f32[8,264,128]{2,1,0:T(8,128)}), f32[8,264,128]{2,1,0:T(8,128)S(1)}, u32[]{:S(2)}, u32[]{:S(2)}) async-start(f32[8,264,128]{2,1,0:T(8,128)} %shard_map.101), calls=%async_computation.1 | async-start | bytes 2162688 | tf_op jit(solution)/shard_map/all_to_all | solution.py:585
  129.5 5.8 %collective-permute-start.23 = (f32[8,1024]{1,0:T(8,128)S(1)}, f32[8,1024]{1,0:T(8,128)S(1)}, u32[]{:S(2)}, u32[]{:S(2)}) collective-permute-start(f32[8,1024]{1,0:T(8,128)S(1)} %add.29), channel_id=1, source_target_pairs={{0,64},{16,80},{32,96},{48,112},{64,0},{80,16},{96,32},{112,48},{1... | collective-permute-start | bytes 98312 | tf_op jit(solution)/shard_map/ppermute | solution.py:54
  135.3 4.3 %collective-permute-start.24 = (f32[16,1024]{1,0:T(8,128)S(1)}, f32[16,1024]{1,0:T(8,128)S(1)}, u32[]{:S(2)}, u32[]{:S(2)}) collective-permute-start(f32[16,1024]{1,0:T(8,128)S(1)} %pad_maximum_fusion), channel_id=1, source_target_pairs={{0,1},{1,0},{2,3},{3,2},{4,5},{5,4},{6,7},{7,6},{8,9},{9,8},{10,11... | collective-permute-start | bytes 196616 | tf_op jit(solution)/shard_map/ppermute | solution.py:37
  (15 other events, 133.4 us)

commit v6 on v5

--- a/solution.py
+++ b/solution.py
@@ -564,21 +564,21 @@
     )(owner_table, first, second, sums, totals)
 
 
-def with_squares(parts, squares):
+def with_squares(parts, squares, near_squares):
     rows = parts.shape[1]
 
-    def body(parts_ref, squares_ref, out_ref):
+    def body(parts_ref, squares_ref, near_ref, out_ref):
         for k in range(parts.shape[0]):
-            out_ref[k] = squares_ref[...]
+            out_ref[k] = squares_ref[...] + near_ref[...]
 
     return pl.pallas_call(
         body,
         grid=(1,),
         out_shape=f32(*parts.shape),
-        in_specs=[pl.BlockSpec(memory_space=pl.ANY), pl.BlockSpec((8, 128), lambda i: (0, 0))],
+        in_specs=[pl.BlockSpec(memory_space=pl.ANY)] + [pl.BlockSpec((8, 128), lambda i: (0, 0))] * 2,
         out_specs=pl.BlockSpec((parts.shape[0], 8, 128), lambda i: (0, rows // 8 - 1, 0)),
         input_output_aliases={0: 0},
-    )(parts, squares)
+    )(parts, squares, near_squares)
 
 
 def sent_back(parts):
@@ -605,7 +605,7 @@
     chunk_b, chunk_c = pack(root, rows_dev)
     r_high, r_low = split_root(root, rows_dev)
     near_own = {1: near(tie(own_y[1], lead_got))}
-    near_far = {0: near(tie(far_y[0], lead_got))}
+    near_far = {0: near(tie(far_y[0], own_sums))}
     near_own[3] = near(tie(own_y[3], near_own[1], far_y[1], far_y[3]))
     near_far[1] = near(tie(far_y[1], near_far[0], got_x[2]))
     near_far[3] = near(tie(far_y[3], near_own[3]))
@@ -631,9 +631,9 @@
     sums = sums + swap(sums, "dp", 3)
     back_a = sent_back(tie(half_a, chunk_c, sums))
     half_b, squares = second_product(1, t_high, t_low, [lead_got, chunk_b, chunk_c], squares)
-    squares = squares + near(squares)
+    near_squares = near(squares)
     totals = sums + swap(sums, "fsdp", 1)
-    back_b = sent_back(tie(with_squares(half_b, tie(squares, totals)), back_a))
+    back_b = sent_back(tie(with_squares(half_b, tie(squares, totals), near_squares), back_a))
     totals = tie(totals, back_a)
     bit = 2
     while bit < lax.axis_size("fsdp"):

time: 144 us -> 144 us (level)
    unnamed x24 -> x28, local copies, waits for them, and re-layouts: 7.63 us -> 8.22 us
  transfers between devices with their start and end apart: 27 -> 27, of which waited for: 18 -> 18; matrix products, arithmetic and copies ran while one was open for 1% -> 0% of each run, Pallas kernels for 18% -> 18%
where the time goes in v6:
time: 144 us; the launch traced here: 143 us
  starting transfers between devices  52.9 us (37%)
  waiting for transfers between devices  49 us (34%)
  Pallas kernels  31.6 us (22%)
  local copies, waits for them, and re-layouts  8.33 us (6%)
    ppermute x12, waiting for transfers between devices, near(): return lax.ppermute(v, 'dp', NEAR)  31.1 us
    all_to_all x2, starting transfers between devices, sent_back(): lax.all_to_all(parts, 'dp', 0, 0, axis_index_groups=GROUPS, tiled=True)  15.3 us
    ppermute x6, starting transfers between devices, swap(): return lax.ppermute(v, axis, [(i, i ^ bit) for i in range(count)])  13.6 us
    ppermute x12, starting transfers between devices, near(): return lax.ppermute(v, 'dp', NEAR)  12.4 us
    ppermute x6, waiting for transfers between devices, swap(): return lax.ppermute(v, axis, [(i, i ^ bit) for i in range(count)])  11.2 us
    unnamed x28, local copies, waits for them, and re-layouts  8.22 us
    ppermute x4, starting transfers between devices, far(): return lax.ppermute(v, 'dp', FAR)  8.17 us
    pallas_call x1, Pallas kernels, update_statistics(): call(body, [f32(order, order), f32(8, 128)], [VMEM, VMEM, VMEM], [VMEM, V...  6.97 us
  transfers between devices with their start and end apart: 27, of which 18 were waited for; matrix products, arithmetic and copies ran while one was open for 0% of the time, Pallas kernels for 18%

profile of v6, /device:TPU:6, one launch (start us, length us, event | category | flops | bytes accessed | tf_op | source)
XLA Modules:
  0.0 142.6 jit_solution(16118109079402211903)
XLA Ops:
  0.6 2.5 %shard_map.93 = (f32[192,1024]{1,0:T(8,128)S(1)}, f32[64,1024]{1,0:T(8,128)S(1)}, f32[128,1024]{1,0:T(8,128)S(1)}, f32[128,1024]{1,0:T(8,128)S(1)}, f32[128,1024]{1,0:T(8,128)S(1)}) custom-call(s32[1,8]{1,0:T(1,128)} %owner_ref.3, f32[64,8192]{1,0:T(8,128)} %g_ref.3, f32[1024,1024]{1,0:T(8,128)} %bitcast.3), custom_call_target="tpu_custom_call" | custom-call | bytes 4194304 | tf_op jit(solution)/shard_map/pallas_call | solution.py:182
  13.7 3.9 %shard_map.94 = (f32[64,8192]{1,0:T(8,128)}, f32[64,8192]{1,0:T(8,128)}, f32[8,1024]{1,0:T(8,128)S(1)}) custom-call(f32[64,8192]{1,0:T(8,128)S(1)} %copy-done.1, f32[64,8192]{1,0:T(8,128)S(1)} %copy-done.7, f32[64,8192]{1,0:T(8,128)S(1)} %copy-done.8), custom_call_target="tpu_custom_call" | custom-call | bytes 12582912 | tf_op jit(solution)/shard_map/pallas_call | solution.py:215
  17.7 2.3 %collective-permute-start.4 = (f32[64,1024]{1,0:T(8,128)S(1)}, f32[64,1024]{1,0:T(8,128)S(1)}, u32[]{:S(2)}, u32[]{:S(2)}) collective-permute-start(f32[64,1024]{1,0:T(8,128)S(1)} %get-tuple-element.87), channel_id=1, source_target_pairs={{0,3},{1,2},{2,1},{3,0},{4,7},{5,6},{6,5},{7,4},{8,11},{9,10},{10,... | collective-permute-start | bytes 786440 | tf_op jit(solution)/shard_map/ppermute | solution.py:41
  25.1 3.0 %collective-permute-done.4.refs_5_ = f32[64,1024]{1,0:T(8,128)S(1)} collective-permute-done((f32[64,1024]{1,0:T(8,128)S(1)}, f32[64,1024]{1,0:T(8,128)S(1)}, u32[]{:S(2)}, u32[]{:S(2)}) %collective-permute-start.4) | collective-permute-done | bytes 262176 | tf_op jit(solution)/shard_map/ppermute | solution.py:41
  28.1 3.5 %collective-permute-done.6.refs_7_ = f32[64,1024]{1,0:T(8,128)S(1)} collective-permute-done((f32[64,1024]{1,0:T(8,128)S(1)}, f32[64,1024]{1,0:T(8,128)S(1)}, u32[]{:S(2)}, u32[]{:S(2)}) %collective-permute-start.6) | collective-permute-done | bytes 262176 | tf_op jit(solution)/shard_map/ppermute | solution.py:41
  33.5 4.3 %collective-permute-done.9.refs_12_ = f32[64,1024]{1,0:T(8,128)S(1)} collective-permute-done((f32[64,1024]{1,0:T(8,128)S(1)}, f32[64,1024]{1,0:T(8,128)S(1)}, u32[]{:S(2)}, u32[]{:S(2)}) %collective-permute-start.9) | collective-permute-done | bytes 262176 | tf_op jit(solution)/shard_map/ppermute | solution.py:37
  50.4 4.3 %collective-permute-done.13.refs_15_ = f32[64,1024]{1,0:T(8,128)S(1)} collective-permute-done((f32[64,1024]{1,0:T(8,128)S(1)}, f32[64,1024]{1,0:T(8,128)S(1)}, u32[]{:S(2)}, u32[]{:S(2)}) %collective-permute-start.13) | collective-permute-done | bytes 262176 | tf_op jit(solution)/shard_map/ppermute | solution.py:37
  56.0 4.3 %collective-permute-done.11.refs_10_ = f32[64,1024]{1,0:T(8,128)S(1)} collective-permute-done((f32[64,1024]{1,0:T(8,128)S(1)}, f32[64,1024]{1,0:T(8,128)S(1)}, u32[]{:S(2)}, u32[]{:S(2)}) %collective-permute-start.11) | collective-permute-done | bytes 262176 | tf_op jit(solution)/shard_map/ppermute | solution.py:37
  60.3 2.8 %collective-permute-done.14.refs_14_ = f32[64,1024]{1,0:T(8,128)S(1)} collective-permute-done((f32[64,1024]{1,0:T(8,128)S(1)}, f32[64,1024]{1,0:T(8,128)S(1)}, u32[]{:S(2)}, u32[]{:S(2)}) %collective-permute-start.14) | collective-permute-done | bytes 262176 | tf_op jit(solution)/shard_map/ppermute | solution.py:37
  65.2 4.8 %shard_map.97 = (bf16[1024,1024]{1,0:T(8,128)(2,1)S(1)}, bf16[1024,1024]{1,0:T(8,128)(2,1)S(1)}, bf16[1024,1024]{1,0:T(8,128)(2,1)S(1)}, bf16[1024,1024]{1,0:T(8,128)(2,1)S(1)}) custom-call(f32[192,1024]{1,0:T(8,128)S(1)} %copy-done.10, f32[128,1024]{1,0:T(8,128)S(1)} %collective-permute-done.refs_1_, f32[128,1024]{1,0:T(8,128)S(1)} %collective-permute-done.3.refs_2_, ...), custom_call_target="tpu_custom_call" | custom-call | bytes 1048576 | tf_op jit(solution)/shard_map/pallas_call | solution.py:368
  70.0 7.0 %shard_map.98 = (f32[1024,1024]{1,0:T(8,128)}, f32[8,128]{1,0:T(8,128)S(1)}) custom-call(bf16[1024,1024]{1,0:T(8,128)(2,1)S(1)} %get-tuple-element.64.gh_ref, bf16[1024,1024]{1,0:T(8,128)(2,1)S(1)} %get-tuple-element.65.gl_ref, f32[1024,1024]{1,0:T(8,128)S(1)} %bitcast.6), custom_call_target="tpu_custom_call" | custom-call | bytes 1048576 | tf_op jit(solution)/shard_map/pallas_call | solution.py:514
  78.6 2.4 %collective-permute-done.16 = f32[8,1024]{1,0:T(8,128)S(1)} collective-permute-done((f32[8,1024]{1,0:T(8,128)S(1)}, f32[8,1024]{1,0:T(8,128)S(1)}, u32[]{:S(2)}, u32[]{:S(2)}) %collective-permute-start.16) | collective-permute-done | bytes 32800 | tf_op jit(solution)/shard_map/ppermute | solution.py:54
  81.0 2.4 %collective-permute-start.17 = (f32[8,1024]{1,0:T(8,128)S(1)}, f32[8,1024]{1,0:T(8,128)S(1)}, u32[]{:S(2)}, u32[]{:S(2)}) collective-permute-start(f32[8,1024]{1,0:T(8,128)S(1)} %add.21), channel_id=1, source_target_pairs={{0,8},{1,9},{2,10},{3,11},{4,12},{5,13},{6,14},{7,15},{8,0},{9,1},... | collective-permute-start | bytes 98312 | tf_op jit(solution)/shard_map/ppermute | solution.py:54
  83.4 3.0 %collective-permute-done.17 = f32[8,1024]{1,0:T(8,128)S(1)} collective-permute-done((f32[8,1024]{1,0:T(8,128)S(1)}, f32[8,1024]{1,0:T(8,128)S(1)}, u32[]{:S(2)}, u32[]{:S(2)}) %collective-permute-start.17) | collective-permute-done | bytes 32800 | tf_op jit(solution)/shard_map/ppermute | solution.py:54
  86.4 3.5 %collective-permute-done.15.refs_1_ = f32[264,1024]{1,0:T(8,128)S(1)} collective-permute-done((f32[264,1024]{1,0:T(8,128)S(1)}, f32[264,1024]{1,0:T(8,128)S(1)}, u32[]{:S(2)}, u32[]{:S(2)}) %collective-permute-start.15) | collective-permute-done | bytes 1081376 | tf_op jit(solution)/shard_map/ppermute | solution.py:37
  89.9 3.4 %shard_map.99 = (f32[8,256,128]{2,1,0:T(8,128)}, f32[8,128]{1,0:T(8,128)S(1)}) custom-call(bf16[1024,1024]{1,0:T(8,128)(2,1)S(1)} %get-tuple-element.61.high_ref, bf16[1024,1024]{1,0:T(8,128)(2,1)S(1)} %get-tuple-element.62.low_ref, f32[192,1024]{1,0:T(8,128)S(1)} %collective-permute-done.7.refs_8_.refs_0_, f32[264,1024]{1,0:T(8,128)S(1)} %collective-permute-done.15.refs_1_, ...), custom_call_target="tpu_custom_call" | custom-call | tf_op jit(solution)/shard_map/pallas_call | solution.py:464
  93.3 3.7 %collective-permute-start.19 = (f32[8,1024]{1,0:T(8,128)S(1)}, f32[8,1024]{1,0:T(8,128)S(1)}, u32[]{:S(2)}, u32[]{:S(2)}) collective-permute-start(f32[8,1024]{1,0:T(8,128)S(1)} %add.22), channel_id=1, source_target_pairs={{0,3},{1,2},{2,1},{3,0},{4,7},{5,6},{6,5},{7,4},{8,11},{9,10},{10,... | collective-permute-start | bytes 98312 | tf_op jit(solution)/shard_map/ppermute | solution.py:54
  98.9 8.4 %all-to-all-start = ((f32[8,256,128]{2,1,0:T(8,128)}), f32[8,256,128]{2,1,0:T(8,128)}, u32[]{:S(2)}, u32[]{:S(2)}) async-start(f32[8,256,128]{2,1,0:T(8,128)} %get-tuple-element.73), calls=%async_computation | async-start | bytes 2097152 | tf_op jit(solution)/shard_map/all_to_all | solution.py:585
  110.2 3.0 %shard_map.100 = (f32[8,264,128]{2,1,0:T(8,128)}, f32[8,128]{1,0:T(8,128)S(1)}) custom-call(bf16[1024,1024]{1,0:T(8,128)(2,1)S(1)} %get-tuple-element.61.high_ref, bf16[1024,1024]{1,0:T(8,128)(2,1)S(1)} %copy-done.3, f32[192,1024]{1,0:T(8,128)S(1)} %collective-permute-done.7.refs_8_.refs_0_, f32[264,1024]{1,0:T(8,128)S(1)} %copy-done.5, ...), custom_call_target="tpu_custom_call" | custom-call | tf_op jit(solution)/shard_map/pallas_call | solution.py:464
  113.2 3.6 %collective-permute-done.21.near_ref = f32[8,128]{1,0:T(8,128)S(1)} collective-permute-done((f32[8,128]{1,0:T(8,128)S(1)}, f32[8,128]{1,0:T(8,128)S(1)}, u32[]{:S(2)}, u32[]{:S(2)}) %collective-permute-start.21) | collective-permute-done | bytes 4128 | tf_op jit(solution)/shard_map/ppermute | solution.py:37
  118.7 6.9 %all-to-all-start.1 = ((f32[8,264,128]{2,1,0:T(8,128)}), f32[8,264,128]{2,1,0:T(8,128)S(1)}, u32[]{:S(2)}, u32[]{:S(2)}) async-start(f32[8,264,128]{2,1,0:T(8,128)} %shard_map.101), calls=%async_computation.1 | async-start | bytes 2162688 | tf_op jit(solution)/shard_map/all_to_all | solution.py:585
  129.5 3.9 %collective-permute-start.23 = (f32[8,1024]{1,0:T(8,128)S(1)}, f32[8,1024]{1,0:T(8,128)S(1)}, u32[]{:S(2)}, u32[]{:S(2)}) collective-permute-start(f32[8,1024]{1,0:T(8,128)S(1)} %add.25), channel_id=1, source_target_pairs={{0,64},{16,80},{32,96},{48,112},{64,0},{80,16},{96,32},{112,48},{1... | collective-permute-start | bytes 98312 | tf_op jit(solution)/shard_map/ppermute | solution.py:54
  135.4 4.3 %collective-permute-done.24 = f32[16,1024]{1,0:T(8,128)S(1)} collective-permute-done((f32[16,1024]{1,0:T(8,128)S(1)}, f32[16,1024]{1,0:T(8,128)S(1)}, u32[]{:S(2)}, u32[]{:S(2)}) %collective-permute-start.24) | collective-permute-done | bytes 65568 | tf_op jit(solution)/shard_map/ppermute | solution.py:37
  139.8 2.8 %shard_map.102 = f32[64,8192]{1,0:T(8,128)} custom-call(s32[1,8]{1,0:T(1,128)S(1)} %copy-done.12, f32[8,256,128]{2,1,0:T(8,128)} %all-to-all-done.first_ref, f32[8,264,128]{2,1,0:T(8,128)S(1)} %all-to-all-done.1.second_ref, f32[8,1024]{1,0:T(8,128)S(1)} %get-tuple-element.89.sums_ref, f32[8,1024]{1,0:T(8,128)S(1)} %get-tuple-element.88.totals_ref), custom_call_target="tpu_custom_call" | custom-call | bytes 4194304 | tf_op jit(solution)/shard_map/pallas_call | solution.py:556
  (80 shorter events, 47.9 us)
Async XLA Ops:
  3.1 14.6 %collective-permute-start = (f32[128,1024]{1,0:T(8,128)S(1)}, f32[128,1024]{1,0:T(8,128)S(1)}, u32[]{:S(2)}, u32[]{:S(2)}) collective-permute-start(f32[128,1024]{1,0:T(8,128)S(1)} %get-tuple-element.44), channel_id=1, source_target_pairs={{0,4},{1,5},{2,6},{3,7},{4,8},{5,9},{6,10},{7,11},{8,12},{9,13},{1... | collective-permute-start | bytes 1572872 | tf_op jit(solution)/shard_map/ppermute | solution.py:45
  3.6 19.5 %collective-permute-start.7 = (f32[192,1024]{1,0:T(8,128)S(1)}, f32[192,1024]{1,0:T(8,128)S(1)}, u32[]{:S(2)}, u32[]{:S(2)}) collective-permute-start(f32[192,1024]{1,0:T(8,128)S(1)} %get-tuple-element.43.refs_0_), channel_id=1, source_target_pairs={{0,1},{1,0},{2,3},{3,2},{4,5},{5,4},{6,7},{7,6},{8,9},{9,8},{10,11... | collective-permute-start | bytes 2359304 | tf_op jit(solution)/shard_map/ppermute | solution.py:37
  5.3 14.8 %collective-permute-start.2 = (f32[128,1024]{1,0:T(8,128)S(1)}, f32[128,1024]{1,0:T(8,128)S(1)}, u32[]{:S(2)}, u32[]{:S(2)}) collective-permute-start(f32[128,1024]{1,0:T(8,128)S(1)} %get-tuple-element.47), channel_id=1, source_target_pairs={{0,12},{1,13},{2,14},{3,15},{4,0},{5,1},{6,2},{7,3},{8,4},{9,5},{1... | collective-permute-start | bytes 1572872 | tf_op jit(solution)/shard_map/ppermute | solution.py:45
  6.8 13.2 %collective-permute-start.1 = (f32[64,1024]{1,0:T(8,128)S(1)}, f32[64,1024]{1,0:T(8,128)S(1)}, u32[]{:S(2)}, u32[]{:S(2)}) collective-permute-start(f32[64,1024]{1,0:T(8,128)S(1)} %get-tuple-element.46), channel_id=1, source_target_pairs={{0,3},{1,2},{2,1},{3,0},{4,7},{5,6},{6,5},{7,4},{8,11},{9,10},{10,... | collective-permute-start | bytes 786440 | tf_op jit(solution)/shard_map/ppermute | solution.py:41
  17.7 10.3 %collective-permute-start.4 = (f32[64,1024]{1,0:T(8,128)S(1)}, f32[64,1024]{1,0:T(8,128)S(1)}, u32[]{:S(2)}, u32[]{:S(2)}) collective-permute-start(f32[64,1024]{1,0:T(8,128)S(1)} %get-tuple-element.87), channel_id=1, source_target_pairs={{0,3},{1,2},{2,1},{3,0},{4,7},{5,6},{6,5},{7,4},{8,11},{9,10},{10,... | collective-permute-start | bytes 786440 | tf_op jit(solution)/shard_map/ppermute | solution.py:41
  20.1 17.8 %collective-permute-start.3 = (f32[128,1024]{1,0:T(8,128)S(1)}, f32[128,1024]{1,0:T(8,128)S(1)}, u32[]{:S(2)}, u32[]{:S(2)}) collective-permute-start(f32[128,1024]{1,0:T(8,128)S(1)} %get-tuple-element.49), channel_id=1, source_target_pairs={{0,8},{1,9},{2,10},{3,11},{4,12},{5,13},{6,14},{7,15},{8,0},{9,1},... | collective-permute-start | bytes 1572872 | tf_op jit(solution)/shard_map/ppermute | solution.py:45
  21.5 10.1 %collective-permute-start.6 = (f32[64,1024]{1,0:T(8,128)S(1)}, f32[64,1024]{1,0:T(8,128)S(1)}, u32[]{:S(2)}, u32[]{:S(2)}) collective-permute-start(f32[64,1024]{1,0:T(8,128)S(1)} %get-tuple-element.83), channel_id=1, source_target_pairs={{0,3},{1,2},{2,1},{3,0},{4,7},{5,6},{6,5},{7,4},{8,11},{9,10},{10,... | collective-permute-start | bytes 786440 | tf_op jit(solution)/shard_map/ppermute | solution.py:41
  23.1 9.2 %collective-permute-start.8 = (f32[64,1024]{1,0:T(8,128)S(1)}, f32[64,1024]{1,0:T(8,128)S(1)}, u32[]{:S(2)}, u32[]{:S(2)}) collective-permute-start(f32[64,1024]{1,0:T(8,128)S(1)} %get-tuple-element.50), channel_id=1, source_target_pairs={{0,1},{1,0},{2,3},{3,2},{4,5},{5,4},{6,7},{7,6},{8,9},{9,8},{10,11... | collective-permute-start | bytes 786440 | tf_op jit(solution)/shard_map/ppermute | solution.py:37
  24.3 13.6 %collective-permute-start.9 = (f32[64,1024]{1,0:T(8,128)S(1)}, f32[64,1024]{1,0:T(8,128)S(1)}, u32[]{:S(2)}, u32[]{:S(2)}) collective-permute-start(f32[64,1024]{1,0:T(8,128)S(1)} %collective-permute-done.1.refs_4_), channel_id=1, source_target_pairs={{0,1},{1,0},{2,3},{3,2},{4,5},{5,4},{6,7},{7,6},{8,9},{9,8},{10,11... | collective-permute-start | bytes 786440 | tf_op jit(solution)/shard_map/ppermute | solution.py:37
  32.2 11.2 %collective-permute-start.12 = (f32[64,1024]{1,0:T(8,128)S(1)}, f32[64,1024]{1,0:T(8,128)S(1)}, u32[]{:S(2)}, u32[]{:S(2)}) collective-permute-start(f32[64,1024]{1,0:T(8,128)S(1)} %get-tuple-element.57), channel_id=1, source_target_pairs={{0,1},{1,0},{2,3},{3,2},{4,5},{5,4},{6,7},{7,6},{8,9},{9,8},{10,11... | collective-permute-start | bytes 786440 | tf_op jit(solution)/shard_map/ppermute | solution.py:37
  37.9 11.2 %collective-permute-start.10 = (f32[64,1024]{1,0:T(8,128)S(1)}, f32[64,1024]{1,0:T(8,128)S(1)}, u32[]{:S(2)}, u32[]{:S(2)}) collective-permute-start(f32[64,1024]{1,0:T(8,128)S(1)} %collective-permute-done.4.refs_5_), channel_id=1, source_target_pairs={{0,1},{1,0},{2,3},{3,2},{4,5},{5,4},{6,7},{7,6},{8,9},{9,8},{10,11... | collective-permute-start | bytes 786440 | tf_op jit(solution)/shard_map/ppermute | solution.py:37
  39.2 9.9 %collective-permute-start.5 = (f32[64,1024]{1,0:T(8,128)S(1)}, f32[64,1024]{1,0:T(8,128)S(1)}, u32[]{:S(2)}, u32[]{:S(2)}) collective-permute-start(f32[64,1024]{1,0:T(8,128)S(1)} %get-tuple-element.85), channel_id=1, source_target_pairs={{0,3},{1,2},{2,1},{3,0},{4,7},{5,6},{6,5},{7,4},{8,11},{9,10},{10,... | collective-permute-start | bytes 786440 | tf_op jit(solution)/shard_map/ppermute | solution.py:41
  43.5 11.2 %collective-permute-start.13 = (f32[64,1024]{1,0:T(8,128)S(1)}, f32[64,1024]{1,0:T(8,128)S(1)}, u32[]{:S(2)}, u32[]{:S(2)}) collective-permute-start(f32[64,1024]{1,0:T(8,128)S(1)} %collective-permute-done.6.refs_7_), channel_id=1, source_target_pairs={{0,1},{1,0},{2,3},{3,2},{4,5},{5,4},{6,7},{7,6},{8,9},{9,8},{10,11... | collective-permute-start | bytes 786440 | tf_op jit(solution)/shard_map/ppermute | solution.py:37
  49.1 11.2 %collective-permute-start.11 = (f32[64,1024]{1,0:T(8,128)S(1)}, f32[64,1024]{1,0:T(8,128)S(1)}, u32[]{:S(2)}, u32[]{:S(2)}) collective-permute-start(f32[64,1024]{1,0:T(8,128)S(1)} %get-tuple-element.56), channel_id=1, source_target_pairs={{0,1},{1,0},{2,3},{3,2},{4,5},{5,4},{6,7},{7,6},{8,9},{9,8},{10,11... | collective-permute-start | bytes 786440 | tf_op jit(solution)/shard_map/ppermute | solution.py:37
  54.7 8.4 %collective-permute-start.14 = (f32[64,1024]{1,0:T(8,128)S(1)}, f32[64,1024]{1,0:T(8,128)S(1)}, u32[]{:S(2)}, u32[]{:S(2)}) collective-permute-start(f32[64,1024]{1,0:T(8,128)S(1)} %collective-permute-done.5.refs_6_), channel_id=1, source_target_pairs={{0,1},{1,0},{2,3},{3,2},{4,5},{5,4},{6,7},{7,6},{8,9},{9,8},{10,11... | collective-permute-start | bytes 786440 | tf_op jit(solution)/shard_map/ppermute | solution.py:37
  63.1 26.8 %collective-permute-start.15 = (f32[264,1024]{1,0:T(8,128)S(1)}, f32[264,1024]{1,0:T(8,128)S(1)}, u32[]{:S(2)}, u32[]{:S(2)}) collective-permute-start(f32[264,1024]{1,0:T(8,128)S(1)} %get-tuple-element.63), channel_id=1, source_target_pairs={{0,1},{1,0},{2,3},{3,2},{4,5},{5,4},{6,7},{7,6},{8,9},{9,8},{10,11... | collective-permute-start | bytes 3244040 | tf_op jit(solution)/shard_map/ppermute | solution.py:37
  64.9 34.1 %collective-permute-start.18 = (f32[128,1024]{1,0:T(8,128)S(1)}, f32[128,1024]{1,0:T(8,128)S(1)}, u32[]{:S(2)}, u32[]{:S(2)}) collective-permute-start(f32[128,1024]{1,0:T(8,128)S(1)} %get-tuple-element.70), channel_id=1, source_target_pairs={{0,1},{1,0},{2,3},{3,2},{4,5},{5,4},{6,7},{7,6},{8,9},{9,8},{10,11... | collective-permute-start | bytes 1572872 | tf_op jit(solution)/shard_map/ppermute | solution.py:37
  81.0 5.4 %collective-permute-start.17 = (f32[8,1024]{1,0:T(8,128)S(1)}, f32[8,1024]{1,0:T(8,128)S(1)}, u32[]{:S(2)}, u32[]{:S(2)}) collective-permute-start(f32[8,1024]{1,0:T(8,128)S(1)} %add.21), channel_id=1, source_target_pairs={{0,8},{1,9},{2,10},{3,11},{4,12},{5,13},{6,14},{7,15},{8,0},{9,1},... | collective-permute-start | bytes 98312 | tf_op jit(solution)/shard_map/ppermute | solution.py:54
  93.3 5.6 %collective-permute-start.19 = (f32[8,1024]{1,0:T(8,128)S(1)}, f32[8,1024]{1,0:T(8,128)S(1)}, u32[]{:S(2)}, u32[]{:S(2)}) collective-permute-start(f32[8,1024]{1,0:T(8,128)S(1)} %add.22), channel_id=1, source_target_pairs={{0,3},{1,2},{2,1},{3,0},{4,7},{5,6},{6,5},{7,4},{8,11},{9,10},{10,... | collective-permute-start | bytes 98312 | tf_op jit(solution)/shard_map/ppermute | solution.py:54
  98.9 19.7 %all-to-all-start = ((f32[8,256,128]{2,1,0:T(8,128)}), f32[8,256,128]{2,1,0:T(8,128)}, u32[]{:S(2)}, u32[]{:S(2)}) async-start(f32[8,256,128]{2,1,0:T(8,128)} %get-tuple-element.73), calls=%async_computation | async-start | bytes 2097152 | tf_op jit(solution)/shard_map/all_to_all | solution.py:585
  107.3 5.8 %collective-permute-start.20 = (f32[8,1024]{1,0:T(8,128)S(1)}, f32[8,1024]{1,0:T(8,128)S(1)}, u32[]{:S(2)}, u32[]{:S(2)}) collective-permute-start(f32[8,1024]{1,0:T(8,128)S(1)} %add.23), channel_id=1, source_target_pairs={{0,16},{16,0},{32,48},{48,32},{64,80},{80,64},{96,112},{112,96},{1... | collective-permute-start | bytes 98312 | tf_op jit(solution)/shard_map/ppermute | solution.py:54
  118.7 21.1 %all-to-all-start.1 = ((f32[8,264,128]{2,1,0:T(8,128)}), f32[8,264,128]{2,1,0:T(8,128)S(1)}, u32[]{:S(2)}, u32[]{:S(2)}) async-start(f32[8,264,128]{2,1,0:T(8,128)} %shard_map.101), calls=%async_computation.1 | async-start | bytes 2162688 | tf_op jit(solution)/shard_map/all_to_all | solution.py:585
  129.5 5.8 %collective-permute-start.23 = (f32[8,1024]{1,0:T(8,128)S(1)}, f32[8,1024]{1,0:T(8,128)S(1)}, u32[]{:S(2)}, u32[]{:S(2)}) collective-permute-start(f32[8,1024]{1,0:T(8,128)S(1)} %add.25), channel_id=1, source_target_pairs={{0,64},{16,80},{32,96},{48,112},{64,0},{80,16},{96,32},{112,48},{1... | collective-permute-start | bytes 98312 | tf_op jit(solution)/shard_map/ppermute | solution.py:54
  135.3 4.3 %collective-permute-start.24 = (f32[16,1024]{1,0:T(8,128)S(1)}, f32[16,1024]{1,0:T(8,128)S(1)}, u32[]{:S(2)}, u32[]{:S(2)}) collective-permute-start(f32[16,1024]{1,0:T(8,128)S(1)} %pad_maximum_fusion), channel_id=1, source_target_pairs={{0,1},{1,0},{2,3},{3,2},{4,5},{5,4},{6,7},{7,6},{8,9},{9,8},{10,11... | collective-permute-start | bytes 196616 | tf_op jit(solution)/shard_map/ppermute | solution.py:37
  (17 other events, 137.7 us)
